TPU v7x, 32 devices: a whole 2x2x4 slice. The times are simulated.
32 devices in a mesh: dp: 2 (over x), seq: 4 (over y, core), tensor: 4 (over z).
Axes of the slice: x: 2, y: 2, z: 4, core: 2. Of those that a mesh axis runs over, the one named last changes fastest.
Arguments:
- features: bfloat16 [2, 2, 1536, 768], P(None, 'dp', 'seq'), may hold values from -6 to 6
- upstream: bfloat16 [2, 2, 1536, 768], P(None, 'dp', 'seq'), may hold values from -6 to 6
- key_mask: int32 [2, 2, 1536], P(None, 'dp'), may hold values from 0 to 1, as said below
- vectors: bfloat16 [2, 6, 768], P(None, None, ('dp', 'seq')), may hold values from 0.099609375 to 1.8984375
- proj_qkv: bfloat16 [2, 768, 3, 768], P(None, ('dp', 'seq'), None, 'tensor')
- qv_bias: bfloat16 [2, 2, 768], P(None, None, ('tensor', 'dp', 'seq')), may hold values from -3 to 3
- proj_out: bfloat16 [2, 768, 768], P(None, 'tensor', ('dp', 'seq')), may hold values from -0.21875 to 0.21875
- expand_weight: bfloat16 [2, 768, 3072], P(None, ('dp', 'seq'), 'tensor'), may hold values from -0.21875 to 0.21875
- expand_bias: bfloat16 [2, 3072], P(None, ('tensor', 'dp', 'seq')), may hold values from -3 to 3
- shrink_weight: bfloat16 [2, 3072, 768], P(None, 'tensor', ('dp', 'seq')), may hold values from -0.109375 to 0.109375
Outputs:
- encoded: bfloat16 [2, 2, 1536, 768], P(None, 'dp', 'seq')
- grad_features: float32 [2, 2, 1536, 768], P(None, 'dp', 'seq')
- grad_vectors: float32 [2, 6, 768], P(None, None, ('dp', 'seq'))
- grad_proj_qkv: float32 [2, 768, 3, 768], P(None, ('dp', 'seq'), None, 'tensor')
- grad_qv_bias: float32 [2, 2, 768], P(None, None, ('tensor', 'dp', 'seq'))
- grad_proj_out: float32 [2, 768, 768], P(None, 'tensor', ('dp', 'seq'))
- grad_expand_weight: float32 [2, 768, 3072], P(None, ('dp', 'seq'), 'tensor')
- grad_expand_bias: float32 [2, 3072], P(None, ('tensor', 'dp', 'seq'))
- grad_shrink_weight: float32 [2, 3072, 768], P(None, 'tensor', ('dp', 'seq'))
Inputs may be any that keep to these rules, and one draw needn't show every extreme that they name: `key_mask`: each clip's last frames, between 0 and 36 of them, are 0 and all others 1; some clip has exactly 36 padded frames.
All inputs are finite; a program needn't handle non-finite values.
Results may differ from a plain program's by a relative error of at most 0.009.
Values may be sent and summed in bfloat16 or wider, within the bound.
No kernel may reach another device: no remote copies, remote signals or barrier semaphores. Data moves between devices by JAX's collectives and lax.ppermute only.
A program may use at most 192 MiB of HBM per device.

v0:
```python
from functools import partial

import jax
import jax.numpy as jnp
from jax import lax
from jax.sharding import PartitionSpec as P

HD = 64
LAYERS = 2


def layer_norm(values, gain, shift):
    center = values - jnp.mean(values, axis=-1, keepdims=True)
    spread = jnp.mean(center * center, axis=-1, keepdims=True)
    return center * lax.rsqrt(spread + 1e-05) * gain + shift


def fetch(params, depth):
    return (
        lax.all_gather(params[0][depth], ("dp", "seq"), axis=1, tiled=True),
        lax.all_gather(params[1][depth], ("dp", "seq"), axis=0, tiled=True),
        lax.all_gather(params[2][depth], ("dp", "seq"), axis=1, tiled=True),
        lax.all_gather(params[3][depth], ("dp", "seq"), axis=1, tiled=True),
        lax.all_gather(params[4][depth], ("dp", "seq"), axis=0, tiled=True),
        lax.all_gather(params[5][depth], ("dp", "seq"), axis=0, tiled=True),
        lax.all_gather(params[6][depth], ("dp", "seq"), axis=1, tiled=True),
    )


def fetch_again(params, depth):
    return (
        lax.all_gather(params[0][depth], ("dp", "seq"), axis=1, tiled=True),
        lax.all_gather(params[1][depth], ("dp", "seq"), axis=0, tiled=True),
        lax.all_gather(params[2][depth], ("dp", "seq"), axis=1, tiled=True),
        lax.all_gather(params[3][depth], ("dp", "seq"), axis=1, tiled=True),
        lax.all_gather(params[4][depth], ("dp", "seq"), axis=0, tiled=True),
        lax.all_gather(params[5][depth], ("dp", "seq"), axis=0, tiled=True),
        lax.all_gather(params[6][depth], ("dp", "seq"), axis=1, tiled=True),
    )


def branch_total(partial_term):
    return lax.psum(partial_term, "tensor")


def normed_total(partial_term):
    return lax.psum(partial_term, "tensor")


def split_heads(values):
    return values.reshape(values.shape[0], values.shape[1], values.shape[2] // HD, HD)


def score_block(query_heads, key_heads, valid):
    scores = jnp.einsum(
        "cqhe,ckhe->chqk", query_heads, key_heads, preferred_element_type=jnp.float32
    ) * HD ** (-0.5)
    return jnp.where(valid, scores, -1000000000.0)


def attend(queries, key_all, value_all, valid):
    scores = score_block(split_heads(queries), split_heads(key_all), valid)
    highest = jnp.max(scores, axis=-1, keepdims=True)
    expo = jnp.exp(scores - highest)
    total = jnp.sum(expo, axis=-1, keepdims=True)
    probs = (expo / total).astype(jnp.bfloat16)
    log_total = highest + jnp.log(total)
    mixed = jnp.einsum(
        "chqk,ckhe->cqhe", probs, split_heads(value_all), preferred_element_type=jnp.float32
    )
    return (mixed.reshape(queries.shape).astype(jnp.bfloat16), log_total)


def attend_back(queries, key_all, value_all, log_total, grad_mixed, valid):
    query_heads = split_heads(queries)
    key_heads = split_heads(key_all)
    scores = score_block(query_heads, key_heads, valid)
    probs = jnp.exp(scores - log_total)
    probs_low = probs.astype(jnp.bfloat16)
    grad_heads = split_heads(grad_mixed)
    grad_value = jnp.einsum(
        "chqk,cqhe->ckhe", probs_low, grad_heads, preferred_element_type=jnp.float32
    )
    grad_probs = jnp.einsum(
        "cqhe,ckhe->chqk", grad_heads, split_heads(value_all), preferred_element_type=jnp.float32
    )
    inner = jnp.sum(grad_probs * probs, axis=-1, keepdims=True)
    grad_scores = (probs * (grad_probs - inner)).astype(jnp.bfloat16)
    grad_query = jnp.einsum(
        "chqk,ckhe->cqhe", grad_scores, key_heads, preferred_element_type=jnp.float32
    ) * HD ** (-0.5)
    grad_key = jnp.einsum(
        "chqk,cqhe->ckhe", grad_scores, query_heads, preferred_element_type=jnp.float32
    ) * HD ** (-0.5)
    return (
        grad_query.reshape(queries.shape),
        grad_key.reshape(key_all.shape),
        grad_value.reshape(value_all.shape),
    )


def forward_layer(frames, valid, weights):
    vecs, proj_qkv, qv_bias, proj_out, expand_weight, expand_bias, shrink_weight = weights
    vec_float = vecs.astype(jnp.float32)
    bias_float = qv_bias.astype(jnp.float32)
    normed = layer_norm(frames, vec_float[0], vec_float[1]).astype(jnp.bfloat16)
    packed = jnp.einsum("ctd,dje->ctje", normed, proj_qkv, preferred_element_type=jnp.float32)
    queries = (packed[:, :, 0] + bias_float[0]).astype(jnp.bfloat16)
    key_rows = packed[:, :, 1].astype(jnp.bfloat16)
    value_rows = (packed[:, :, 2] + bias_float[1]).astype(jnp.bfloat16)
    key_all, value_all = (
        lax.all_gather(key_rows, "seq", axis=1, tiled=True),
        lax.all_gather(value_rows, "seq", axis=1, tiled=True),
    )
    mixed, log_total = attend(queries, key_all, value_all, valid)
    branch = jnp.einsum("ctf,fd->ctd", mixed, proj_out, preferred_element_type=jnp.float32)
    after = frames + (branch_total(branch) + vec_float[2])
    normed_two = layer_norm(after, vec_float[3], vec_float[4]).astype(jnp.bfloat16)
    hidden = jnp.einsum(
        "ctd,df->ctf", normed_two, expand_weight, preferred_element_type=jnp.float32
    ) + expand_bias.astype(jnp.float32)
    active = jax.nn.gelu(hidden, approximate=False).astype(jnp.bfloat16)
    shrunk = jnp.einsum("ctf,fd->ctd", active, shrink_weight, preferred_element_type=jnp.float32)
    result = after + (branch_total(shrunk) + vec_float[5])
    saved = (
        frames,
        normed,
        queries,
        key_all,
        value_all,
        log_total,
        mixed,
        after,
        normed_two,
        hidden,
        active,
    )
    return (result, saved)


def backward_layer(grad_out, saved, weights, valid):
    (
        frames,
        normed,
        queries,
        key_all,
        value_all,
        log_total,
        mixed,
        after,
        normed_two,
        hidden,
        active,
    ) = saved
    vecs, proj_qkv, qv_bias, proj_out, expand_weight, expand_bias, shrink_weight = weights
    vec_float = vecs.astype(jnp.float32)
    grad_branch_own = grad_out.astype(jnp.bfloat16)
    grad_shrink_bias = jnp.sum(grad_branch_own.astype(jnp.float32), axis=(0, 1))
    grad_shrink = jnp.einsum(
        "ctf,ctd->fd", active, grad_branch_own, preferred_element_type=jnp.float32
    )
    grad_active = jnp.einsum(
        "ctd,fd->ctf", grad_branch_own, shrink_weight, preferred_element_type=jnp.float32
    )
    _, gelu_back = jax.vjp(partial(jax.nn.gelu, approximate=False), hidden)
    grad_hidden = gelu_back(grad_active)[0].astype(jnp.bfloat16)
    grad_expand_bias = jnp.sum(grad_hidden.astype(jnp.float32), axis=(0, 1))
    grad_expand = jnp.einsum(
        "ctd,ctf->df", normed_two, grad_hidden, preferred_element_type=jnp.float32
    )
    expand_term = jnp.einsum(
        "ctf,df->ctd", grad_hidden, expand_weight, preferred_element_type=jnp.float32
    )
    grad_normed_two = normed_total(expand_term)
    _, norm_back_two = jax.vjp(layer_norm, after, vec_float[3], vec_float[4])
    grad_after, grad_gain_two, grad_shift_two = norm_back_two(grad_normed_two)
    grad_after = grad_after + grad_out
    grad_attn_own = grad_after.astype(jnp.bfloat16)
    grad_out_bias = jnp.sum(grad_attn_own.astype(jnp.float32), axis=(0, 1))
    grad_proj_out = jnp.einsum(
        "ctf,ctd->fd", mixed, grad_attn_own, preferred_element_type=jnp.float32
    )
    grad_mixed = jnp.einsum(
        "ctd,fd->ctf", grad_attn_own, proj_out, preferred_element_type=jnp.float32
    ).astype(jnp.bfloat16)
    grad_query, key_term, value_term = attend_back(
        queries, key_all, value_all, log_total, grad_mixed, valid
    )
    grad_key, grad_value = (
        lax.psum_scatter(key_term, "seq", scatter_dimension=1, tiled=True),
        lax.psum_scatter(value_term, "seq", scatter_dimension=1, tiled=True),
    )
    stacked = jnp.stack(
        [
            grad_query.astype(jnp.bfloat16),
            grad_key.astype(jnp.bfloat16),
            grad_value.astype(jnp.bfloat16),
        ],
        axis=2,
    )
    grad_qkv = jnp.einsum("ctd,ctje->dje", normed, stacked, preferred_element_type=jnp.float32)
    grad_qv_bias = jnp.sum(stacked[:, :, 0::2].astype(jnp.float32), axis=(0, 1))
    qkv_term = jnp.einsum("ctje,dje->ctd", stacked, proj_qkv, preferred_element_type=jnp.float32)
    grad_normed = normed_total(qkv_term)
    _, norm_back_one = jax.vjp(layer_norm, frames, vec_float[0], vec_float[1])
    grad_frames, grad_gain, grad_shift = norm_back_one(grad_normed)
    grad_frames = grad_frames + grad_after
    grad_vecs = jnp.stack(
        [grad_gain, grad_shift, grad_out_bias, grad_gain_two, grad_shift_two, grad_shrink_bias]
    )
    return (
        grad_frames,
        (
            grad_vecs,
            grad_qkv,
            grad_qv_bias,
            grad_proj_out,
            grad_expand,
            grad_expand_bias,
            grad_shrink,
        ),
    )


def body(
    features,
    upstream,
    key_mask,
    vectors,
    proj_qkv,
    qv_bias,
    proj_out,
    expand_weight,
    expand_bias,
    shrink_weight,
):
    params = (vectors, proj_qkv, qv_bias, proj_out, expand_weight, expand_bias, shrink_weight)
    micro_count = features.shape[0]
    totals = [None] * LAYERS
    encoded_list = []
    grad_list = []
    for micro_idx in range(micro_count):
        valid = (key_mask[micro_idx] > 0)[:, None, None, :]
        state = features[micro_idx].astype(jnp.float32)
        used = []
        kept = []
        for depth in range(LAYERS):
            weights = fetch(params, depth)
            state, saved = forward_layer(state, valid, weights)
            used.append(weights)
            kept.append(saved)
        encoded_list.append(state.astype(jnp.bfloat16))
        grad_state = upstream[micro_idx].astype(jnp.float32)
        for depth in reversed(range(LAYERS)):
            weights_back = fetch_again(params, depth)
            grad_state, layer_grads = backward_layer(grad_state, kept[depth], weights_back, valid)
            if totals[depth] is None:
                totals[depth] = layer_grads
            else:
                totals[depth] = jax.tree.map(
                    lambda left, right: left + right, totals[depth], layer_grads
                )
        grad_list.append(grad_state)
    stacked = [jnp.stack([totals[depth][member] for depth in range(LAYERS)]) for member in range(7)]
    reduced = (
        lax.psum_scatter(stacked[0], ("dp", "seq"), scatter_dimension=2, tiled=True),
        lax.psum_scatter(stacked[1], ("dp", "seq"), scatter_dimension=1, tiled=True),
        lax.psum_scatter(stacked[2], ("dp", "seq"), scatter_dimension=2, tiled=True),
        lax.psum_scatter(stacked[3], ("dp", "seq"), scatter_dimension=2, tiled=True),
        lax.psum_scatter(stacked[4], ("dp", "seq"), scatter_dimension=1, tiled=True),
        lax.psum_scatter(stacked[5], ("dp", "seq"), scatter_dimension=1, tiled=True),
        lax.psum_scatter(stacked[6], ("dp", "seq"), scatter_dimension=2, tiled=True),
    )
    encoded = jnp.stack(encoded_list)
    grad_features = jnp.stack(grad_list)
    grad_vectors = reduced[0]
    return (
        encoded,
        grad_features,
        grad_vectors,
        reduced[1],
        reduced[2],
        reduced[3],
        reduced[4],
        reduced[5],
        reduced[6],
    )


def solution(mesh):
    placed = (
        P(None, "dp", "seq", None),
        P(None, "dp", "seq", None),
        P(None, "dp", None),
        P(None, None, ("dp", "seq")),
        P(None, ("dp", "seq"), None, "tensor"),
        P(None, None, ("tensor", "dp", "seq")),
        P(None, "tensor", ("dp", "seq")),
        P(None, ("dp", "seq"), "tensor"),
        P(None, ("tensor", "dp", "seq")),
        P(None, "tensor", ("dp", "seq")),
    )
    return jax.shard_map(
        body,
        mesh=mesh,
        in_specs=placed,
        out_specs=(
            P(None, "dp", "seq", None),
            P(None, "dp", "seq", None),
            P(None, None, ("dp", "seq")),
            P(None, ("dp", "seq"), None, "tensor"),
            P(None, None, ("tensor", "dp", "seq")),
            P(None, "tensor", ("dp", "seq")),
            P(None, ("dp", "seq"), "tensor"),
            P(None, ("tensor", "dp", "seq")),
            P(None, "tensor", ("dp", "seq")),
        ),
        check_vma=False,
    )
```

profile of v0, /device:TPU:0, one launch (start us, length us, event | category | flops | bytes accessed | tf_op | source)
XLA Modules:
  0.0 1411.5 jit_solution(15447099040067588949)
XLA Ops:
  12.0 11.0 all-gather
  23.5 13.4 slice_reduce_fusion.6
  37.7 13.4 all-gather.1
  65.5 8.7 all-gather.2
  79.9 8.1 all_gather.47
  88.8 10.4 all-gather.4
  99.6 7.9 all-gather.16
  134.7 14.2 %all-reduce.11 = (bf16[768]{0:T(1024)(128)(2,1)S(1)}, bf16[768]{0:T(1024)(128)(2,1)}) all-reduce(bf16[768]{0:T(1024)(128)(2,1)S(1)} %dynamic-update-slice, bf16[768]{0:T(1024)(128)(2,1)S(1)} %dynamic-update-slice.1), channel_id=8, replica_groups=mesh['dp'=2,'seq'=4,'tensor'=4] {'dp','seq'}, use_global_device_ids=true, to_apply=%add | all-reduce | flops 1536 | bytes 6144
  149.5 77.4 %all-reduce.35.cloned.1.call-done = (f32[1,384,768]{2,1,0:T(8,128)}, f32[1,384,768]{2,1,0:T(8,128)}) async-done(((f32[1,384,768]{2,1,0:T(8,128)}, f32[1,384,768]{2,1,0:T(8,128)}), (f32[1,384,768]{2,1,0:T(8,128)}, f32[1,384,768]{2,1,0:T(8,128)})) %all-reduce.35.cloned.1.call-update) | async-done | bytes 2359312 | tf_op jit(solution)/shard_map/psum | solution.py:43
  246.6 9.5 all-gather.8
  256.7 14.4 %all-gather.9 = bf16[1,768,3,192]{3,2,0,1:T(4,128)(2,1)} all-gather(bf16[1,96,3,192]{3,2,0,1:T(4,128)(2,1)S(1)} %copy.67), channel_id=11, replica_groups=mesh['dp'=2,'seq'=4,'tensor'=4] {'dp','seq'}, dimensions={1}, use_global_device_ids=true | all-gather | bytes 995328 | tf_op jit(solution)/shard_map/all_gather | solution.py:21
  274.7 9.0 all-gather.10
  286.9 10.9 all-gather.12
  300.0 13.4 slice_reduce_fusion
  313.4 27.6 %all-reduce.33.cloned.1.call-done = (f32[1,384,768]{2,1,0:T(8,128)}, f32[1,384,768]{2,1,0:T(8,128)}) async-done(((f32[1,384,768]{2,1,0:T(8,128)}, f32[1,384,768]{2,1,0:T(8,128)}), (f32[1,384,768]{2,1,0:T(8,128)}, f32[1,384,768]{2,1,0:T(8,128)})) %all-reduce.33.cloned.1.call-update) | async-done | bytes 2359312 | tf_op jit(solution)/shard_map/psum | solution.py:43
  370.5 7.9 all_gather.120
  394.2 92.5 %all-reduce.31.cloned.1.call-done = (f32[1,384,768]{2,1,0:T(8,128)}, f32[1,384,768]{2,1,0:T(8,128)}) async-done(((f32[1,384,768]{2,1,0:T(8,128)}, f32[1,384,768]{2,1,0:T(8,128)}), (f32[1,384,768]{2,1,0:T(8,128)}, f32[1,384,768]{2,1,0:T(8,128)})) %all-reduce.31.cloned.1.call-update) | async-done | bytes 2359312 | tf_op jit(solution)/shard_map/psum | solution.py:43
  512.6 93.6 %all-reduce.29.cloned.1.call-done = (f32[1,384,768]{2,1,0:T(8,128)}, f32[1,384,768]{2,1,0:T(8,128)}) async-done(((f32[1,384,768]{2,1,0:T(8,128)}, f32[1,384,768]{2,1,0:T(8,128)}), (f32[1,384,768]{2,1,0:T(8,128)}, f32[1,384,768]{2,1,0:T(8,128)})) %all-reduce.29.cloned.1.call-update) | async-done | bytes 2359312 | tf_op jit(solution)/shard_map/psum | solution.py:47
  648.4 25.5 %reduce-scatter.33.cloned.1.call-done = f32[1,384,192]{1,2,0:T(8,128)} async-done(((f32[1,1536,192]{1,2,0:T(8,128)}), f32[1,384,192]{1,2,0:T(8,128)}) %reduce-scatter.33.cloned.1.call-update) | async-done | bytes 294928 | tf_op jit(solution)/shard_map/reduce_scatter | solution.py:191
  674.9 27.1 %reduce-scatter.23.cloned.1.call-done = f32[1,384,192]{1,2,0:T(8,128)} async-done(((f32[1,1536,192]{1,2,0:T(8,128)}), f32[1,384,192]{1,2,0:T(8,128)}) %reduce-scatter.23.cloned.1.call-update) | async-done | bytes 294928 | tf_op jit(solution)/shard_map/reduce_scatter | solution.py:190
  704.7 25.5 %reduce-scatter.25.cloned.1.call-done = f32[1,384,192]{1,2,0:T(8,128)} async-done(((f32[1,1536,192]{1,2,0:T(8,128)}), f32[1,384,192]{1,2,0:T(8,128)}) %reduce-scatter.25.cloned.1.call-update) | async-done | bytes 294928 | tf_op jit(solution)/shard_map/reduce_scatter | solution.py:191
  733.1 96.1 %all-reduce.27.cloned.1.call-done = (f32[1,384,768]{2,1,0:T(8,128)}, f32[1,384,768]{2,1,0:T(8,128)}) async-done(((f32[1,384,768]{2,1,0:T(8,128)}, f32[1,384,768]{2,1,0:T(8,128)}), (f32[1,384,768]{2,1,0:T(8,128)}, f32[1,384,768]{2,1,0:T(8,128)})) %all-reduce.27.cloned.1.call-update) | async-done | bytes 2359312 | tf_op jit(solution)/shard_map/psum | solution.py:47
  844.9 94.7 %all-reduce.25.cloned.1.call-done = (f32[1,384,768]{2,1,0:T(8,128)}, f32[1,384,768]{2,1,0:T(8,128)}) async-done(((f32[1,384,768]{2,1,0:T(8,128)}, f32[1,384,768]{2,1,0:T(8,128)}), (f32[1,384,768]{2,1,0:T(8,128)}, f32[1,384,768]{2,1,0:T(8,128)})) %all-reduce.25.cloned.1.call-update) | async-done | bytes 2359312 | tf_op jit(solution)/shard_map/psum | solution.py:47
  990.8 17.3 %reduce-scatter.37.cloned.1.call-done = f32[1,384,192]{1,2,0:T(8,128)} async-done(((f32[1,1536,192]{1,2,0:T(8,128)}), f32[1,384,192]{1,2,0:T(8,128)}) %reduce-scatter.37.cloned.1.call-update) | async-done | bytes 294928 | tf_op jit(solution)/shard_map/reduce_scatter | solution.py:191
  1009.1 27.1 %reduce-scatter.27.cloned.1.call-done = f32[1,384,192]{1,2,0:T(8,128)} async-done(((f32[1,1536,192]{1,2,0:T(8,128)}), f32[1,384,192]{1,2,0:T(8,128)}) %reduce-scatter.27.cloned.1.call-update) | async-done | bytes 294928 | tf_op jit(solution)/shard_map/reduce_scatter | solution.py:190
  1039.0 26.2 %reduce-scatter.29.cloned.1.call-done = f32[1,384,192]{1,2,0:T(8,128)} async-done(((f32[1,1536,192]{1,2,0:T(8,128)}), f32[1,384,192]{1,2,0:T(8,128)}) %reduce-scatter.29.cloned.1.call-update) | async-done | bytes 294928 | tf_op jit(solution)/shard_map/reduce_scatter | solution.py:191
  1086.9 8.2 copy.48
  1111.1 130.0 %all-reduce.23.cloned.1.call-done = (f32[1,384,768]{2,1,0:T(8,128)}, f32[1,384,768]{2,1,0:T(8,128)}, f32[1,384,768]{2,1,0:T(8,128)}, f32[1,384,768]{2,1,0:T(8,128)}) async-done(((f32[1,384,768]{2,1,0:T(8,128)}, f32[1,384,768]{2,1,0:T(8,128)}, f32[1,384,768]{2,1,0:T(8,128)}, f32[1,384,768]{2,1,0:T(8,128)}), (f32[1,384,768]{2,1,0:T(8,128)}, f32[1,384,768]{2,1,0:T(8,128)}, f32[1,384,768]{2,1,0:T(8,128)}, ...) | async-done | bytes 4718608 | tf_op jit(solution)/shard_map/psum | solution.py:43
  1262.0 8.0 reshape.2888
  1284.8 55.4 %all-reduce.21.cloned.1.call-done = f32[2,768,768]{1,0,2:T(2,128)} async-done(((f32[2,768,768]{1,0,2:T(2,128)}), f32[2,768,768]{1,0,2:T(2,128)}) %all-reduce.21.cloned.1.call-update) | async-done | bytes 4718608
  1347.9 12.6 all-reduce.2
  1373.1 30.3 %reduce-scatter.39.cloned.1.call-done = f32[2,96,768]{2,1,0:T(8,128)} async-done(((f32[2,768,768]{2,1,0:T(8,128)}), f32[2,96,768]{2,1,0:T(8,128)}) %reduce-scatter.39.cloned.1.call-update) | async-done | bytes 589840 | tf_op jit(solution)/shard_map/reduce_scatter | solution.py:270
  (966 shorter events, 362.3 us)
Async XLA Ops:
  8.0 218.9 %all-reduce.35.cloned.1.call-start = ((), (), s32[]{:S(2)}) async-start(), calls=%async_computation.37 | async-start | bytes 4718592 | tf_op jit(solution)/shard_map/psum | solution.py:43
  130.5 100.0 %all-gather.23.cloned.1.call-start = ((), (), s32[]{:S(2)}) async-start(), calls=%async_computation.22 | async-start | bytes 1327104 | tf_op jit(solution)/shard_map/all_gather | solution.py:24
  132.1 108.8 %all-gather.25.cloned.1.call-start = ((), (), s32[]{:S(2)}) async-start(), calls=%async_computation.23 | async-start | bytes 1327104 | tf_op jit(solution)/shard_map/all_gather | solution.py:26
  133.0 208.1 %all-reduce.33.cloned.1.call-start = ((), (), s32[]{:S(2)}) async-start(), calls=%async_computation.36 | async-start | bytes 4718592 | tf_op jit(solution)/shard_map/psum | solution.py:43
  228.9 112.1 %copy-start.10 = (f32[1,384,768]{2,1,0:T(8,128)}, f32[1,384,768]{2,1,0:T(8,128)S(1)}, u32[]{:S(2)}) copy-start(f32[1,384,768]{2,1,0:T(8,128)S(1)} %get-tuple-element.145) | copy-start | bytes 3538948
  228.9 112.1 %copy-start.13 = (f32[1,384,768]{2,1,0:T(8,128)}, f32[1,384,768]{2,1,0:T(8,128)S(1)}, u32[]{:S(2)}) copy-start(f32[1,384,768]{2,1,0:T(8,128)S(1)} %get-tuple-element.153) | copy-start | bytes 3538948
  245.9 240.9 %all-reduce.31.cloned.1.call-start = ((), (), s32[]{:S(2)}) async-start(), calls=%async_computation.35 | async-start | bytes 4718592 | tf_op jit(solution)/shard_map/psum | solution.py:43
  391.8 99.4 %all-gather.27.cloned.1.call-start = ((), (), s32[]{:S(2)}) async-start(), calls=%async_computation.24 | async-start | bytes 1327104 | tf_op jit(solution)/shard_map/all_gather | solution.py:24
  392.4 104.4 %all-gather.29.cloned.1.call-start = ((), (), s32[]{:S(2)}) async-start(), calls=%async_computation.25 | async-start | bytes 1327104 | tf_op jit(solution)/shard_map/all_gather | solution.py:26
  393.1 213.2 %all-reduce.29.cloned.1.call-start = ((), (), s32[]{:S(2)}) async-start(), calls=%async_computation.34 | async-start | bytes 4718592 | tf_op jit(solution)/shard_map/psum | solution.py:47
  489.1 120.5 %copy-start.6 = (f32[1,384,768]{2,1,0:T(8,128)}, f32[1,384,768]{2,1,0:T(8,128)S(1)}, u32[]{:S(2)}) copy-start(f32[1,384,768]{2,1,0:T(8,128)S(1)} %get-tuple-element.133) | copy-start | bytes 3538948
  489.1 120.5 %copy-start.8 = (f32[1,384,768]{2,1,0:T(8,128)}, f32[1,384,768]{2,1,0:T(8,128)S(1)}, u32[]{:S(2)}) copy-start(f32[1,384,768]{2,1,0:T(8,128)S(1)} %get-tuple-element.184) | copy-start | bytes 3538948
  511.1 136.3 %reduce-scatter.31.cloned.1.call-start = ((), (), s32[]{:S(2)}) async-start(), calls=%async_computation.17 | async-start | bytes 1474560 | tf_op jit(solution)/shard_map/reduce_scatter | solution.py:190
  620.7 53.2 %reduce-scatter.33.cloned.1.call-start = ((), (), s32[]{:S(2)}) async-start(), calls=%async_computation.18 | async-start | bytes 1474560 | tf_op jit(solution)/shard_map/reduce_scatter | solution.py:191
  626.1 75.8 %reduce-scatter.23.cloned.1.call-start = ((), (), s32[]{:S(2)}) async-start(), calls=%async_computation.13 | async-start | bytes 1474560 | tf_op jit(solution)/shard_map/reduce_scatter | solution.py:190
  636.3 94.0 %reduce-scatter.25.cloned.1.call-start = ((), (), s32[]{:S(2)}) async-start(), calls=%async_computation.14 | async-start | bytes 1474560 | tf_op jit(solution)/shard_map/reduce_scatter | solution.py:191
  641.7 187.5 %all-reduce.27.cloned.1.call-start = ((), (), s32[]{:S(2)}) async-start(), calls=%async_computation.33 | async-start | bytes 4718592 | tf_op jit(solution)/shard_map/psum | solution.py:47
  733.1 206.6 %all-reduce.25.cloned.1.call-start = ((), (), s32[]{:S(2)}) async-start(), calls=%async_computation.32 | async-start | bytes 4718592 | tf_op jit(solution)/shard_map/psum | solution.py:47
  840.4 99.2 %copy-start.203 = (f32[384]{0:T(512)S(1)}, f32[384]{0:T(512)}, u32[]{:S(2)}) copy-start(f32[384]{0:T(512)} %copy-done.202) | copy-start | bytes 4612
  840.4 99.2 %copy-start.206 = (f32[384]{0:T(512)S(1)}, f32[384]{0:T(512)}, u32[]{:S(2)}) copy-start(f32[384]{0:T(512)} %copy-done.205) | copy-start | bytes 4612
  844.4 104.4 %slice-start.2 = ((s8[7077888]{0:T(1024)(128)(4,1)}), s8[2883584]{0:T(1024)(128)(4,1)S(1)}, s32[]{:S(2)}) async-start(s8[7077888]{0:T(1024)(128)(4,1)} %bitcast.604), calls=%async_computation.40 | async-start | bytes 5767168
  844.4 145.3 %reduce-scatter.35.cloned.1.call-start = ((), (), s32[]{:S(2)}) async-start(), calls=%async_computation.19 | async-start | bytes 1474560 | tf_op jit(solution)/shard_map/reduce_scatter | solution.py:190
  954.9 53.2 %reduce-scatter.37.cloned.1.call-start = ((), (), s32[]{:S(2)}) async-start(), calls=%async_computation.20 | async-start | bytes 1474560 | tf_op jit(solution)/shard_map/reduce_scatter | solution.py:191
  961.1 75.1 %reduce-scatter.27.cloned.1.call-start = ((), (), s32[]{:S(2)}) async-start(), calls=%async_computation.15 | async-start | bytes 1474560 | tf_op jit(solution)/shard_map/reduce_scatter | solution.py:190
  973.9 91.3 %reduce-scatter.29.cloned.1.call-start = ((), (), s32[]{:S(2)}) async-start(), calls=%async_computation.16 | async-start | bytes 1474560 | tf_op jit(solution)/shard_map/reduce_scatter | solution.py:191
  979.3 261.8 %all-reduce.23.cloned.1.call-start = ((), (), s32[]{:S(2)}) async-start(), calls=%async_computation.31 | async-start | bytes 9437184 | tf_op jit(solution)/shard_map/psum | solution.py:43
  1068.0 215.3 %reduce-scatter.47.cloned.1.call-start = ((), (), s32[]{:S(2)}) async-start(), calls=%async_computation.29 | async-start | bytes 442368
  1082.7 257.5 %all-reduce.21.cloned.1.call-start = ((), (), s32[]{:S(2)}) async-start(), calls=%async_computation.30 | async-start | bytes 9437184
  1095.1 247.0 %reduce-scatter.45.cloned.1.call-start = ((), (), s32[]{:S(2)}) async-start(), calls=%async_computation.28 | async-start | bytes 1327104
  1105.6 263.3 %reduce-scatter.41.cloned.1.call-start = ((), (), s32[]{:S(2)}) async-start(), calls=%async_computation.26 | async-start | bytes 442368
  1251.5 119.0 %reduce-scatter.43.cloned.1.call-start = ((), (), s32[]{:S(2)}) async-start(), calls=%async_computation.27 | async-start | bytes 3981312
  1270.1 133.3 %reduce-scatter.39.cloned.1.call-start = ((), (), s32[]{:S(2)}) async-start(), calls=%async_computation.21 | async-start | bytes 5308416 | tf_op jit(solution)/shard_map/reduce_scatter | solution.py:270
  (311 other events, 2913.6 us)
Sparse Core Ops, SparseCore 0:
  130.6 96.2 all-reduce.34
  246.0 95.0 all-reduce.32
  391.9 94.7 all-reduce.30
  511.2 95.0 all-reduce.28
  733.2 95.9 all-reduce.26
  844.6 95.0 all-reduce.24
  1068.1 172.9 all-reduce.22
  1244.4 95.7 all-reduce.20
Sparse Core Ops, SparseCore 1:
  133.4 24.2 all-gather.22
  160.0 23.9 all-gather.24
  394.7 22.6 all-gather.26
  419.3 23.9 all-gather.28
  620.8 24.6 reduce-scatter.30
  648.3 25.6 reduce-scatter.32
  676.3 25.6 reduce-scatter.22
  704.6 25.6 reduce-scatter.24
  955.0 24.6 reduce-scatter.34
  982.5 25.6 reduce-scatter.36
  1010.6 25.6 reduce-scatter.26
  1039.6 25.6 reduce-scatter.28
  1082.7 33.9 reduce-scatter.46
  1120.0 36.6 reduce-scatter.44
  1251.6 35.3 reduce-scatter.40
  1290.8 54.3 reduce-scatter.42
  1349.6 53.8 reduce-scatter.38
where the time goes:
time: 1420 us; the launch traced here: 1410 us
  waiting for transfers between devices  848 us (60%)
  blocking collectives  176 us (12%)
  matrix products  143 us (10%)
  local copies, waits for them, and re-layouts  131 us (9%)
  other arithmetic  88.8 us (6%)
  between operations  21.7 us (2%)
    psum x4, waiting for transfers between devices, branch_total(): return lax.psum(partial_term, 'tensor')  328 us
    psum x3, waiting for transfers between devices, normed_total(): return lax.psum(partial_term, 'tensor')  284 us
    reduce_scatter x4, waiting for transfers between devices, backward_layer(): lax.psum_scatter(value_term, 'seq', scatter_dimension=1, tiled=True)  94.6 us
    unnamed x687, local copies, waits for them, and re-layouts  76.8 us
    unnamed x30, waiting for transfers between devices  57 us
    reduce_scatter x4, waiting for transfers between devices, backward_layer(): lax.psum_scatter(key_term, 'seq', scatter_dimension=1, tiled=True)  54.2 us
    all_gather x4, blocking collectives, forward_layer(): lax.all_gather(value_rows, 'seq', axis=1, tiled=True)  31.5 us
    all_gather x4, blocking collectives, forward_layer(): lax.all_gather(key_rows, 'seq', axis=1, tiled=True)  30.7 us
  transfers between devices with their start and end apart: 25, of which 15 were waited for; matrix products, arithmetic and copies ran while one was open for 15% of the time, Pallas kernels for 0%

commit v1 on v0

v1 whole, which is shorter than its diff:
```python
from functools import partial

import jax
import jax.numpy as jnp
from jax import lax
from jax.experimental import pallas as pl
from jax.experimental.pallas import tpu as pltpu
from jax.sharding import PartitionSpec as P

HD = 64
LAYERS = 2
AXES = ("dp", "seq", "tensor")
BF = jnp.bfloat16
F32 = jnp.float32
VMEM_LIMIT = 48 * 1024 * 1024

BITS = {"x": 16, "y": 8, "c": 4, "z2": 2, "z1": 1}

ORDER_E = ("z2", "z1", "x", "y")
ORDER_S = ("z2", "z1", "y", "x")
ORDERS_A = (("z2", "z1", "x", "y"), ("z2", "x", "y", "z1"), ("z2", "y", "z1", "x"))

SPEC_V = pl.BlockSpec(memory_space=pltpu.VMEM)
SPEC_S = pl.BlockSpec(memory_space=pltpu.SMEM)
SPEC_A = pl.BlockSpec(memory_space=pl.ANY)


def swap(value, bit, mesh_shape):
    dp_size, seq_size, ten_size = mesh_shape
    pairs = []
    for d in range(dp_size):
        for s in range(seq_size):
            for t in range(ten_size):
                e, u, v = d, s, t
                if bit == "x":
                    e = d ^ 1
                elif bit == "y":
                    u = s ^ 2
                elif bit == "c":
                    u = s ^ 1
                elif bit == "z2":
                    v = t ^ 2
                else:
                    v = t ^ 1
                pairs.append(((d * seq_size + s) * ten_size + t, (e * seq_size + u) * ten_size + v))
    return lax.ppermute(value, AXES, pairs)


def swap_group(value, pair, mesh_shape):
    dp_size, seq_size, ten_size = mesh_shape
    ry, rp = pair >> 1, pair & 1
    pairs = []
    for d in range(dp_size):
        for s in range(seq_size):
            for t in range(ten_size):
                to = (d * seq_size + (s ^ (2 * ry))) * ten_size + (t ^ rp)
                pairs.append(((d * seq_size + s) * ten_size + t, to))
    return lax.ppermute(value, AXES, pairs)


def gather_block(block, order, mesh_shape):
    cur = block[None]
    for bit in order[:3]:
        cur = jnp.concatenate([cur, swap(cur, bit, mesh_shape)], axis=0)
    more = swap(cur, order[3], mesh_shape)
    return [cur, more, swap(cur, "c", mesh_shape), swap(more, "c", mesh_shape)]


def scatter_sum(parts, order, mesh_shape):
    parts = list(parts)
    for step in range(4):
        got = swap(parts[step].astype(BF), order[step], mesh_shape).astype(F32)
        for later in range(step + 1, 5):
            size = 8 >> later if later < 4 else 1
            start = size if later < 4 else 0
            parts[later] = parts[later].astype(F32) + got[start : start + size]
    return parts[4][0]


def part_of(rel, order):
    flags = [1 if rel & BITS[b] else 0 for b in order]
    for step in range(4):
        if flags[step]:
            place = 0
            for f in flags[step + 1 :]:
                place = place * 2 + f
            return step, place
    return 4, 0


def place():
    dp, seq, ten = lax.axis_index("dp"), lax.axis_index("seq"), lax.axis_index("tensor")
    return lax.rem(dp, 2), lax.div(seq, 2), lax.rem(seq, 2), ten


def xor_bit(value, flag):
    return 1 - value if flag else value


def xor_two(value, flags):
    if flags == 0:
        return value
    high, low = lax.div(value, 2), lax.rem(value, 2)
    return xor_bit(high, flags & 2) * 2 + xor_bit(low, flags & 1)


def row_block(x, y, c, rel):
    return (xor_bit(x, rel & 16) * 2 + xor_bit(y, rel & 8)) * 2 + xor_bit(c, rel & 4)


def group_of(y, ten, pair):
    return xor_bit(y, pair & 2) * 2 + xor_bit(lax.rem(ten, 2), pair & 1)


class Loader:
    def __init__(self, refs, orders, scratch, sems, col=0, width=None):
        x, y, c, ten = place()
        self.copies = {rz: [] for rz in range(4)}
        count = 0
        rows = 96 // len(orders)
        for n, order in enumerate(orders):
            for a in range(4):
                ref = refs[n * 4 + a]
                for j in range(8):
                    rel = sum(BITS[order[k]] for k in range(3) if j & (1 << k))
                    rel |= BITS[order[3]] if a & 1 else 0
                    rel |= BITS["c"] if a & 2 else 0
                    row = row_block(x, y, c, rel) * 96 + n * rows
                    dst = scratch.at[xor_two(ten, rel & 3), pl.ds(pl.multiple_of(row, 32), rows)]
                    src = ref.at[j] if width is None else ref.at[j, :, pl.ds(col, width)]
                    self.copies[rel & 3].append(pltpu.make_async_copy(src, dst, sems.at[count]))
                    count += 1
        self.ten = ten

    def start(self):
        for rz in range(4):
            for copy in self.copies[rz]:
                copy.start()

    def wait(self, rz):
        for copy in self.copies[rz]:
            copy.wait()

    def index(self, rz):
        return xor_two(self.ten, rz)


def dot_nn(left, right):
    return jnp.dot(left, right, preferred_element_type=F32)


def dot_nt(left, right):
    return lax.dot_general(left, right, (((1,), (1,)), ((), ())), preferred_element_type=F32)


def norm_parts(value):
    center = value - jnp.mean(value, axis=-1, keepdims=True)
    spread = jnp.mean(center * center, axis=-1, keepdims=True)
    rstd = lax.rsqrt(spread + 1e-05)
    return center * rstd, rstd


def norm_back(hat, rstd, gain, grad):
    scaled = grad * gain
    first = jnp.mean(scaled, axis=-1, keepdims=True)
    second = jnp.mean(scaled * hat, axis=-1, keepdims=True)
    return rstd * (scaled - first - hat * second)


def put_transposed(value, turned, own_ref, other_ref):
    x, y, c, _ = place()
    turned[...] = value.T
    for xy in range(4):
        for side, ref in ((0, own_ref), (4, other_ref)):
            row = row_block(x, y, c, (16 if xy & 2 else 0) | (8 if xy & 1 else 0) | side) * 96
            ref[pl.ds(xy * 96, 96), :] = turned[pl.ds(pl.multiple_of(row, 32), 96), :].astype(BF)


def call(kernel, outs, scratch, specs, args, flops=0, name=None):
    return pl.pallas_call(
        kernel,
        out_shape=[jax.ShapeDtypeStruct(s, d) for s, d in outs],
        in_specs=specs,
        out_specs=[SPEC_V] * len(outs),
        scratch_shapes=scratch,
        compiler_params=pltpu.CompilerParams(vmem_limit_bytes=VMEM_LIMIT),
        cost_estimate=pl.CostEstimate(flops=flops, bytes_accessed=4000000, transcendentals=0),
        name=name,
    )(*args)


def project_kernel(n_a, x_ref, vec_ref, bias_ref, *refs):
    a_refs, refs = refs[:n_a], refs[n_a:]
    outs, (own_ref, other_ref, w, turned, sems) = refs[:4], refs[4:]
    load = Loader(a_refs, ORDERS_A if n_a == 12 else (ORDER_A,), w, sems, 0, 640)
    load.start()
    _, y, _, ten = place()
    hat, _ = norm_parts(x_ref[...].astype(F32))
    normed = hat * vec_ref[0:1, :] + vec_ref[1:2, :]
    low = normed.astype(BF)
    put_transposed(normed, turned, own_ref, other_ref)
    for rz in range(4):
        load.wait(rz)
    for pair in range(4):
        g = group_of(y, ten, pair)
        packed = dot_nn(low, w[g])[:, :576] + bias_ref[g]
        outs[pair][...] = packed.astype(BF)


ORDER_A = ("z2", "x", "y", "z1")


def project(x, vec, bias, a, tokens):
    outs = [((tokens, 576), BF)] * 4 + [((384, tokens), BF)] * 2
    scratch = [pltpu.VMEM((4, 768, 640), BF), pltpu.VMEM((768, tokens), F32), pltpu.SemaphoreType.DMA((8 * len(a),))]
    return call(
        partial(project_kernel, len(a)), outs, scratch, [SPEC_V] * 3 + [SPEC_A] * len(a), (x, vec, bias, *a),
        flops=2 * tokens * 768 * 2304, name="project",
    )


def attend_kernel(count_ref, p0, p1, p2, p3, o0, o1, o2, o3, m0, m1, m2, m3, kv_ref, q_ref, mixed_ref, lse_ref):
    _, y, c, ten = place()
    tokens = p0.shape[0]
    half = lax.rem(ten, 2)
    for pair, (p, o) in enumerate(((p0, o0), (p1, o1), (p2, o2), (p3, o3))):
        for side, ref in ((0, p), (1, o)):
            block = (xor_bit(y, pair & 2) * 2 + xor_bit(c, side)) * 2 + xor_bit(half, pair & 1)
            kv_ref[pl.ds(pl.multiple_of(block * tokens, 64), tokens), :] = ref[:, :384]
        q_ref[pl.ds(pair * tokens, tokens), :] = p[:, 384:576] * jnp.asarray(HD ** (-0.5), BF)
    total = kv_ref.shape[0]
    count = count_ref[0]
    ones = jnp.ones((total, HD), BF)
    valid = lax.broadcasted_iota(jnp.int32, (tokens, 128), 1) + (total - 128) < count
    for h in range(3):
        keys = kv_ref[:, h * HD : (h + 1) * HD]
        values = jnp.concatenate([kv_ref[:, 192 + h * HD : 192 + (h + 1) * HD], ones], axis=1)
        for pair, m in enumerate((m0, m1, m2, m3)):
            rows = pl.ds(pair * tokens, tokens)
            scores = dot_nt(q_ref[rows, h * HD : (h + 1) * HD], keys)
            last = jnp.where(valid, scores[:, total - 128 :], -1000000000.0)
            scores = jnp.concatenate([scores[:, : total - 128], last], axis=1)
            highest = jnp.max(scores, axis=-1, keepdims=True)
            expo = jnp.exp(scores - highest).astype(BF)
            both = dot_nn(expo, values)
            weight = both[:, HD : HD + 1]
            mixed = both[:, :HD] / weight
            mixed_ref[rows, h * HD : (h + 1) * HD] = mixed
            m[:, h * HD : (h + 1) * HD] = mixed.astype(BF)
            lse_ref[rows, h : h + 1] = highest + jnp.log(weight)


def attend(count, pieces, others):
    tokens = pieces[0].shape[0]
    outs = [((tokens, 192), BF)] * 4 + [
        ((8 * tokens, 384), BF),
        ((4 * tokens, 192), BF),
        ((4 * tokens, 192), F32),
        ((4 * tokens, 128), F32),
    ]
    return call(
        attend_kernel, outs, [], [SPEC_S] + [SPEC_V] * 8, (count, *pieces, *others),
        flops=4 * 4 * tokens * 8 * tokens * 192 * 4, name="attend",
    )


def mlp_kernel(n_a, m0, m1, m2, m3, x_ref, vec_ref, eb_ref, *refs):
    a_refs, e_refs, s_refs, refs = refs[:n_a], refs[n_a : n_a + 4], refs[n_a + 4 : n_a + 8], refs[n_a + 8 :]
    (x_out, after_ref, mixed_ref, own_ref, other_ref, active_ref, slope_ref, wo, we, ws, turned, sa, se, ss) = refs
    load_a = Loader(a_refs, ORDERS_A if n_a == 12 else (ORDER_A,), wo, sa, 512, 256)
    load_e = Loader(e_refs, (ORDER_E,), we, se)
    load_s = Loader(s_refs, (ORDER_S,), ws, ss)
    load_a.start()
    load_e.start()
    load_s.start()
    _, y, _, ten = place()
    for rz in range(4):
        load_a.wait(rz)
    after = x_ref[...].astype(F32) + vec_ref[2:3, :]
    for pair, m in enumerate((m0, m1, m2, m3)):
        g = group_of(y, ten, pair)
        piece = m[...]
        mixed_ref[g] = piece
        after = after + dot_nt(piece, wo[g][:, 64:])
    after_ref[...] = after
    hat, _ = norm_parts(after)
    normed = hat * vec_ref[3:4, :] + vec_ref[4:5, :]
    low = normed.astype(BF)
    put_transposed(normed, turned, own_ref, other_ref)
    out = after + vec_ref[5:6, :]
    for rz in range(4):
        z = load_e.index(rz)
        load_e.wait(rz)
        hidden = dot_nn(low, we[z]) + eb_ref[z]
        lower = 0.5 * (1.0 + lax.erf(hidden * 0.7071067811865476))
        slope_ref[z] = lower + hidden * (jnp.exp(-0.5 * hidden * hidden) * 0.3989422804014327)
        active = (hidden * lower).astype(BF)
        active_ref[z] = active
        load_s.wait(rz)
        out = out + dot_nt(active, ws[z])
    x_out[...] = out


def mlp(pieces, x, vec, eb, a, e, s):
    tokens = x.shape[0]
    outs = [
        ((tokens, 768), F32),
        ((tokens, 768), F32),
        ((4, tokens, 192), BF),
        ((384, tokens), BF),
        ((384, tokens), BF),
        ((4, tokens, 768), BF),
        ((4, tokens, 768), F32),
    ]
    scratch = [
        pltpu.VMEM((4, 768, 256), BF),
        pltpu.VMEM((4, 768, 768), BF),
        pltpu.VMEM((4, 768, 768), BF),
        pltpu.VMEM((768, tokens), F32),
        pltpu.SemaphoreType.DMA((8 * len(a),)),
        pltpu.SemaphoreType.DMA((32,)),
        pltpu.SemaphoreType.DMA((32,)),
    ]
    return call(
        partial(mlp_kernel, len(a)), outs, scratch, [SPEC_V] * 7 + [SPEC_A] * (len(a) + 8), (*pieces, x, vec, eb, *a, *e, *s),
        flops=2 * tokens * 768 * 6912, name="mlp",
    )


def mlp_back_kernel(n_a, dy_ref, after_ref, vec_ref, slope_ref, *refs):
    a_refs, e_refs, s_refs, refs = refs[:n_a], refs[n_a : n_a + 4], refs[n_a + 4 : n_a + 8], refs[n_a + 8 :]
    d_out, refs = refs[:4], refs[4:]
    (da_ref, hid_ref, z_own, z_other, a_own, a_other, sums_ref, ebs_ref, wo, we, ws, turned, sa, se, ss) = refs
    load_a = Loader(a_refs, ORDERS_A if n_a == 12 else (ORDER_A,), wo, sa, 512, 256)
    load_e = Loader(e_refs, (ORDER_E,), we, se)
    load_s = Loader(s_refs, (ORDER_S,), ws, ss)
    load_s.start()
    load_e.start()
    load_a.start()
    _, y, _, ten = place()
    dy = dy_ref[...].astype(F32)
    dz = dy.astype(BF)
    dz_wide = dz.astype(F32)
    put_transposed(dz_wide, turned, z_own, z_other)
    grad = jnp.zeros(dy.shape, F32)
    for rz in range(4):
        z = load_s.index(rz)
        load_s.wait(rz)
        d_active = dot_nn(dz, ws[z])
        d_hidden = (d_active * slope_ref[z]).astype(BF)
        hid_ref[z] = d_hidden
        ebs_ref[z] = jnp.sum(d_hidden.astype(F32), axis=0, keepdims=True)
        load_e.wait(rz)
        grad = grad + dot_nt(d_hidden, we[z])
    hat, rstd = norm_parts(after_ref[...])
    d_after = dy + norm_back(hat, rstd, vec_ref[3:4, :], grad)
    da_ref[...] = d_after
    da = d_after.astype(BF)
    da_wide = da.astype(F32)
    put_transposed(da_wide, turned, a_own, a_other)
    sums_ref[0:1, :] = jnp.sum(da_wide, axis=0, keepdims=True)
    sums_ref[1:2, :] = jnp.sum(grad * hat, axis=0, keepdims=True)
    sums_ref[2:3, :] = jnp.sum(grad, axis=0, keepdims=True)
    sums_ref[3:4, :] = jnp.sum(dz_wide, axis=0, keepdims=True)
    sums_ref[4:8, :] = jnp.zeros((4, dy.shape[1]), F32)
    for rz in range(4):
        load_a.wait(rz)
    for pair in range(4):
        g = group_of(y, ten, pair)
        d_out[pair][...] = dot_nn(da, wo[g])[:, 64:].astype(BF)


def mlp_back(dy, after, vec, slope, a, e, s):
    tokens = dy.shape[0]
    outs = [((tokens, 192), BF)] * 4 + [
        ((tokens, 768), F32),
        ((4, tokens, 768), BF),
        ((384, tokens), BF),
        ((384, tokens), BF),
        ((384, tokens), BF),
        ((384, tokens), BF),
        ((8, 768), F32),
        ((4, 1, 768), F32),
    ]
    scratch = [
        pltpu.VMEM((4, 768, 256), BF),
        pltpu.VMEM((4, 768, 768), BF),
        pltpu.VMEM((4, 768, 768), BF),
        pltpu.VMEM((768, tokens), F32),
        pltpu.SemaphoreType.DMA((8 * len(a),)),
        pltpu.SemaphoreType.DMA((32,)),
        pltpu.SemaphoreType.DMA((32,)),
    ]
    return call(
        partial(mlp_back_kernel, len(a)), outs, scratch, [SPEC_V] * 4 + [SPEC_A] * (len(a) + 8),
        (dy, after, vec, slope, *a, *e, *s), flops=2 * tokens * 768 * 6912, name="mlp_back",
    )


def attend_back_kernel(count_ref, d0, d1, d2, d3, kv_ref, q_ref, mixed_ref, lse_ref, dq_ref, own_ref, other_ref, do, inner, stat, dkv):
    _, y, c, ten = place()
    tokens = d0.shape[0]
    half = lax.rem(ten, 2)
    inner[...] = jnp.zeros(inner.shape, F32)
    for pair, d in enumerate((d0, d1, d2, d3)):
        rows = pl.ds(pair * tokens, tokens)
        grad = d[...]
        do[rows, :] = grad
        for h in range(3):
            cols = slice(h * HD, (h + 1) * HD)
            inner[rows, h : h + 1] = jnp.sum(grad[:, cols].astype(F32) * mixed_ref[rows, cols], axis=-1, keepdims=True)
    stat[0] = lse_ref[...].T
    stat[1] = inner[...].T
    total, queries = kv_ref.shape[0], q_ref.shape[0]
    count = count_ref[0]
    step = 256
    valid = lax.broadcasted_iota(jnp.int32, (128, step), 0) + (total - 128) < count
    for h in range(3):
        cols = slice(h * HD, (h + 1) * HD)
        keys = kv_ref[:, cols]
        values = kv_ref[:, 192 + h * HD : 192 + (h + 1) * HD]
        turned = keys.astype(F32).T.astype(BF)
        d_keys = jnp.zeros((total, HD), F32)
        d_values = jnp.zeros((total, HD), F32)
        for block in range(queries // step):
            rows = slice(block * step, (block + 1) * step)
            query = q_ref[rows, cols]
            grad = do[rows, cols]
            scores = dot_nt(keys, query)
            last = jnp.where(valid, scores[total - 128 :], -1000000000.0)
            scores = jnp.concatenate([scores[: total - 128], last], axis=0)
            probs = jnp.exp(scores - stat[0, h : h + 1, rows])
            d_probs = dot_nt(values, grad)
            d_scores = (probs * (d_probs - stat[1, h : h + 1, rows])).astype(BF)
            d_values = d_values + dot_nn(probs.astype(BF), grad)
            d_keys = d_keys + dot_nn(d_scores, query)
            d_query = dot_nn(turned, d_scores) * HD ** (-0.5)
            dq_ref[rows, cols] = d_query.T.astype(BF)
        dkv[:, cols] = d_keys.astype(BF)
        dkv[:, 192 + h * HD : 192 + (h + 1) * HD] = d_values.astype(BF)
    for pair in range(4):
        for side, ref in ((0, own_ref), (1, other_ref)):
            block = (xor_bit(y, pair & 2) * 2 + xor_bit(c, side)) * 2 + xor_bit(half, pair & 1)
            ref[pair] = dkv[pl.ds(pl.multiple_of(block * tokens, 64), tokens), :]


def attend_back(count, pieces, kv, q, mixed, lse):
    tokens = pieces[0].shape[0]
    outs = [((4 * tokens, 192), BF), ((4, tokens, 384), BF), ((4, tokens, 384), BF)]
    scratch = [
        pltpu.VMEM((4 * tokens, 192), BF),
        pltpu.VMEM((4 * tokens, 128), F32),
        pltpu.VMEM((2, 128, 4 * tokens), F32),
        pltpu.VMEM((8 * tokens, 384), BF),
    ]
    return call(
        attend_back_kernel, outs, scratch, [SPEC_S] + [SPEC_V] * 8, (count, *pieces, kv, q, mixed, lse),
        flops=10 * 4 * tokens * 8 * tokens * 192 * 4, name="attend_back",
    )


def project_back_kernel(n_a, d0, d1, d2, d3, da_ref, x_ref, vec_ref, *refs):
    a_refs, refs = refs[:n_a], refs[n_a:]
    dx_ref, dqkv_ref, sums_ref, bias_ref, w, sems = refs
    load = Loader(a_refs, ORDERS_A if n_a == 12 else (ORDER_A,), w, sems, 0, 640)
    load.start()
    _, y, _, ten = place()
    hat, rstd = norm_parts(x_ref[...].astype(F32))
    for rz in range(4):
        load.wait(rz)
    grad = jnp.zeros(hat.shape, F32)
    for pair, d in enumerate((d0, d1, d2, d3)):
        g = group_of(y, ten, pair)
        piece = d[...]
        dqkv_ref[g] = piece
        bias_ref[g] = jnp.sum(piece.astype(F32), axis=0, keepdims=True)
        grad = grad + dot_nt(piece, w[g][:, :576])
    dx_ref[...] = da_ref[...] + norm_back(hat, rstd, vec_ref[0:1, :], grad)
    sums_ref[0:1, :] = jnp.sum(grad * hat, axis=0, keepdims=True)
    sums_ref[1:2, :] = jnp.sum(grad, axis=0, keepdims=True)
    sums_ref[2:8, :] = jnp.zeros((6, hat.shape[1]), F32)


def project_back(pieces, da, x, vec, a):
    tokens = x.shape[0]
    outs = [((tokens, 768), F32), ((4, tokens, 576), BF), ((8, 768), F32), ((4, 1, 576), F32)]
    scratch = [pltpu.VMEM((4, 768, 640), BF), pltpu.SemaphoreType.DMA((8 * len(a),))]
    return call(
        partial(project_back_kernel, len(a)), outs, scratch, [SPEC_V] * 7 + [SPEC_A] * len(a), (*pieces, da, x, vec, *a),
        flops=2 * tokens * 768 * 2304, name="project_back",
    )


def emit(value, rz, order, outs):
    for xy in range(4):
        part, at = part_of((16 if xy & 2 else 0) | (8 if xy & 1 else 0) | rz, order)
        outs[part][at] = value[xy * 96 : (xy + 1) * 96].astype(BF)


def weigh_kernel(order, l_own, l_got, r_own, r_got, *outs):
    _, _, _, ten = place()
    for rz in range(4):
        z = xor_two(ten, rz)
        emit(dot_nn(l_own[...], r_own[z]) + dot_nn(l_got[...], r_got[z]), rz, order, outs)


def weigh(order, l_own, l_got, r_own, r_got, name):
    outs = [((n, 96, 768), BF) for n in (8, 4, 2, 1, 1)]
    return call(
        partial(weigh_kernel, order), outs, [], [SPEC_V] * 4, (l_own, l_got, r_own, r_got),
        flops=4 * r_own.shape[1] * 384 * 3072, name=name,
    )


def weigh_attention_kernel(order, n_own, n_got, a_own, a_got, q_own, q_got, m_own, m_got, *outs):
    _, _, _, ten = place()
    for rz in range(4):
        z = xor_two(ten, rz)
        qkv = dot_nn(n_own[...], q_own[z]) + dot_nn(n_got[...], q_got[z])
        out = dot_nn(a_own[...], m_own[z]) + dot_nn(a_got[...], m_got[z])
        emit(jnp.concatenate([qkv, out], axis=1), rz, order, outs)


def weigh_attention(order, args):
    outs = [((n, 96, 768), BF) for n in (8, 4, 2, 1, 1)]
    return call(
        partial(weigh_attention_kernel, order), outs, [], [SPEC_V] * 8, args,
        flops=4 * args[4].shape[1] * 384 * 3072, name="weigh_attention",
    )


def spread_kernel(p0, p1, p2, p3, out_ref):
    ten = lax.axis_index("tensor")
    for rz, p in enumerate((p0, p1, p2, p3)):
        out_ref[xor_two(ten, rz)] = p[...].astype(out_ref.dtype)


def spread(block, dtype, shape):
    first = swap(block, "z1", shape)
    second = swap(block, "z2", shape)
    third = swap(first, "z2", shape)
    tokens, width = block.shape
    out = call(
        spread_kernel, [((4, tokens, width), dtype)], [], [SPEC_V] * 4, (block, first, second, third), name="spread"
    )[0]
    return out.reshape(2, 1, 2 * tokens, width)


def small_params(vectors, qv_bias, expand_bias, shape):
    dp_size, seq_size, ten_size = shape
    if dp_size == 2:
        pad = lambda v: jnp.pad(v, ((0, 0), (0, 0), (0, 128 - v.shape[2])))
        rows = jnp.concatenate(
            [pad(vectors), pad(expand_bias[:, None]), pad(qv_bias.reshape(LAYERS, 1, 48))], axis=1
        ).reshape(1, LAYERS * 8, 128)
        for bit in ("z1", "z2", "c", "y", "x"):
            rows = jnp.concatenate([rows, swap(rows, bit, shape)], axis=0)
        x, y, c, ten = place()
        me = ((x * 2 + y) * 2 + c) * 4 + ten
        order = jnp.bitwise_xor(jnp.arange(32, dtype=jnp.int32), me)
        pick = (order[:, None] == jnp.arange(32, dtype=jnp.int32)[None, :]).astype(BF)
        every = jnp.dot(pick, rows.reshape(32, -1), preferred_element_type=F32)
        every = every.reshape(8, 4, LAYERS, 8, 128)
        vec = every[:, 0, :, :6, :96].transpose(1, 2, 0, 3).reshape(LAYERS, 6, 768)
        eb = every[:, :, :, 6, :96].transpose(2, 1, 0, 3).reshape(LAYERS, 4, 1, 768)
        qv = every[:, :, :, 7, :48].reshape(8, 4, LAYERS, 2, 24).transpose(2, 3, 1, 0, 4).reshape(LAYERS, 2, 4, 192)
    else:
        vec = lax.all_gather(vectors, ("dp", "seq"), axis=2, tiled=True).astype(F32)
        eb = lax.all_gather(expand_bias, ("tensor", "dp", "seq"), axis=1, tiled=True)
        eb = eb.astype(F32).reshape(LAYERS, 4, 1, 768)
        qv = lax.all_gather(qv_bias, ("tensor", "dp", "seq"), axis=2, tiled=True)
        qv = qv.astype(F32).reshape(LAYERS, 2, 4, 192)
    qvb = jnp.concatenate([jnp.zeros_like(qv[:, 0]), qv[:, 1], qv[:, 0]], axis=-1)[:, :, None, :]
    return jnp.pad(vec, ((0, 0), (0, 2), (0, 0))), qvb, eb


def body(shape, features, upstream, key_mask, vectors, proj_qkv, qv_bias, proj_out, expand_weight, expand_bias, shrink_weight):
    dp_size, seq_size, ten_size = shape
    dp, seq, ten = lax.axis_index("dp"), lax.axis_index("seq"), lax.axis_index("tensor")
    tokens = features.shape[2] // 2
    at = (lax.div(ten, 2), 0, lax.rem(ten, 2) * tokens, 0)
    x0 = lax.dynamic_slice(features, at, (1, 1, tokens, 768)).reshape(tokens, 768)
    dy0 = lax.dynamic_slice(upstream, at, (1, 1, tokens, 768)).reshape(tokens, 768)
    count = jnp.sum(lax.dynamic_slice(key_mask, (lax.div(ten, 2), 0, 0), (1, 1, key_mask.shape[2])), axis=(1, 2))

    width = proj_qkv.shape[1]
    wa = jnp.concatenate(
        [
            proj_qkv[:, :, 1],
            proj_qkv[:, :, 2],
            proj_qkv[:, :, 0],
            proj_out.transpose(0, 2, 1),
        ],
        axis=-1,
    )
    we = expand_weight
    ws = shrink_weight.transpose(0, 2, 1)
    if dp_size != 2:
        start = (lax.rem(dp, 2) * 4 + seq) * 96
        wa, we, ws = (
            lax.dynamic_slice_in_dim(lax.all_gather(w, ("dp", "seq"), axis=1, tiled=True), start, 96, axis=1)
            for w in (wa, we, ws)
        )
    vec, qvb, eb = small_params(vectors, qv_bias, expand_bias, shape)
    a_w = [
        [g for n, order in enumerate(ORDERS_A) for g in gather_block(wa[0, n * 32 : (n + 1) * 32], order, shape)],
        gather_block(wa[1], ORDER_A, shape),
    ]
    e_w = [gather_block(we[d], ORDER_E, shape) for d in range(LAYERS)]
    s_w = [gather_block(ws[d], ORDER_S, shape) for d in range(LAYERS)]

    state = x0
    kept = []
    for d in range(LAYERS):
        *pieces, n_own, n_other = project(state, vec[d], qvb[d], a_w[d], tokens)
        pieces = [pieces[0]] + [swap_group(pieces[p], p, shape) for p in (1, 2, 3)]
        others = [swap(p[:, :384], "c", shape) for p in pieces]
        *mixed, kv, q, mixed_wide, lse = attend(count, pieces, others)
        mixed = [mixed[0]] + [swap_group(mixed[p], p, shape) for p in (1, 2, 3)]
        x_in = state
        state, after, mixed_all, m_own, m_other, active, slope = mlp(mixed, x_in, vec[d], eb[d], a_w[d], e_w[d], s_w[d])
        kept.append((x_in, n_own, n_other, kv, q, mixed_wide, lse, after, mixed_all, m_own, m_other, active, slope))
    encoded = spread(state.astype(BF), BF, shape)

    grad = dy0
    g_a, g_e, g_s = [None] * LAYERS, [None] * LAYERS, [None] * LAYERS
    small = [None] * LAYERS
    for d in reversed(range(LAYERS)):
        x_in, n_own, n_other, kv, q, mixed_wide, lse, after, mixed_all, m_own, m_other, active, slope = kept[d]
        *d_mixed, d_after, d_hid, z_own, z_other, da_own, da_other, sums_two, ebs = mlp_back(
            grad, after, vec[d], slope, a_w[d], e_w[d], s_w[d]
        )
        d_mixed = [d_mixed[0]] + [swap_group(d_mixed[p], p, shape) for p in (1, 2, 3)]
        order_e, order_s = ORDER_E[::-1], ORDER_S[::-1]
        parts = weigh(order_e, m_own, swap(m_other, "c", shape), d_hid, swap(d_hid, "c", shape), "weigh_expand")
        g_e[d] = scatter_sum(parts, order_e, shape)
        parts = weigh(order_s, z_own, swap(z_other, "c", shape), active, swap(active, "c", shape), "weigh_shrink")
        g_s[d] = scatter_sum(parts, order_s, shape)
        dq, own, other = attend_back(count, d_mixed, kv, q, mixed_wide, lse)
        d_kv = (own.astype(F32) + swap(other, "c", shape).astype(F32)).astype(BF)
        back = [jnp.concatenate([d_kv[p], dq[p * tokens : (p + 1) * tokens]], axis=1) for p in range(4)]
        back = [back[0]] + [swap_group(back[p], p, shape) for p in (1, 2, 3)]
        grad, d_qkv, sums_one, qvs = project_back(back, d_after, x_in, vec[d], a_w[d])
        order_a = ORDER_A[::-1]
        parts = weigh_attention(
            order_a,
            (
                n_own,
                swap(n_other, "c", shape),
                da_own,
                swap(da_other, "c", shape),
                d_qkv,
                swap(d_qkv, "c", shape),
                mixed_all,
                swap(mixed_all, "c", shape),
            ),
        )
        g_a[d] = scatter_sum(parts, order_a, shape)
        total = jnp.concatenate(
            [sums_one[:2], sums_two[:4], ebs.reshape(4, 768), jnp.pad(qvs.reshape(4, 576), ((0, 2), (0, 192)))], axis=0
        )
        if dp_size == 2:
            for bit in ("c", "x", "y", "z1", "z2"):
                total = total + swap(total, bit, shape)
        else:
            total = lax.psum(total, AXES)
        small[d] = total
    grad_features = spread(grad.astype(BF), F32, shape)

    if dp_size != 2:
        start = (lax.rem(dp, 2) * 4 + seq) * 96

        def down(block):
            whole = lax.dynamic_update_slice_in_dim(jnp.zeros((768, 768), F32), block, start, axis=0)
            return lax.psum_scatter(whole, ("dp", "seq"), scatter_dimension=0, tiled=True)

        g_a, g_e, g_s = ([down(g) for g in gs] for gs in (g_a, g_e, g_s))
    ga, ge, gs = jnp.stack(g_a), jnp.stack(g_e), jnp.stack(g_s)
    g_small = jnp.stack(small)
    mine = dp * seq_size + seq
    grad_vectors = lax.dynamic_slice_in_dim(g_small[:, :6], mine * width, width, axis=2)
    eb_width, qv_width = expand_bias.shape[1], qv_bias.shape[2]
    grad_eb = lax.dynamic_slice_in_dim(
        lax.dynamic_index_in_dim(g_small[:, 6:10], ten, axis=1, keepdims=False), mine * eb_width, eb_width, axis=1
    )
    qv = lax.dynamic_index_in_dim(g_small[:, 10:14], ten, axis=1, keepdims=False)
    grad_qv = jnp.stack(
        [
            lax.dynamic_slice_in_dim(qv[:, 384:576], mine * qv_width, qv_width, axis=1),
            lax.dynamic_slice_in_dim(qv[:, 192:384], mine * qv_width, qv_width, axis=1),
        ],
        axis=1,
    )
    grad_qkv = jnp.stack([ga[:, :, 384:576], ga[:, :, :192], ga[:, :, 192:384]], axis=2)
    return (
        encoded,
        grad_features,
        grad_vectors,
        grad_qkv,
        grad_qv,
        ga[:, :, 576:].transpose(0, 2, 1),
        ge,
        grad_eb,
        gs.transpose(0, 2, 1),
    )


def solution(mesh):
    placed = (
        P(None, "dp", "seq", None),
        P(None, "dp", "seq", None),
        P(None, "dp", None),
        P(None, None, ("dp", "seq")),
        P(None, ("dp", "seq"), None, "tensor"),
        P(None, None, ("tensor", "dp", "seq")),
        P(None, "tensor", ("dp", "seq")),
        P(None, ("dp", "seq"), "tensor"),
        P(None, ("tensor", "dp", "seq")),
        P(None, "tensor", ("dp", "seq")),
    )
    shape = tuple(mesh.shape[axis] for axis in AXES)
    return jax.shard_map(
        partial(body, shape),
        mesh=mesh,
        in_specs=placed,
        out_specs=(
            P(None, "dp", "seq", None),
            P(None, "dp", "seq", None),
            P(None, None, ("dp", "seq")),
            P(None, ("dp", "seq"), None, "tensor"),
            P(None, None, ("tensor", "dp", "seq")),
            P(None, "tensor", ("dp", "seq")),
            P(None, ("dp", "seq"), "tensor"),
            P(None, ("tensor", "dp", "seq")),
            P(None, "tensor", ("dp", "seq")),
        ),
        check_vma=False,
    )
```

time: 1420 us -> 628 us (0.44)
  waiting for transfers between devices: 848 us -> 284 us
  blocking collectives: 176 us -> 0 us
  matrix products: 143 us -> 0.22 us
  starting transfers between devices: 3.13 us -> 129 us
  Pallas kernels: 0 us -> 123 us
  local copies, waits for them, and re-layouts: 131 us -> 46.1 us
  other arithmetic: 88.8 us -> 35.5 us
  between operations: 21.7 us -> 3.3 us
    psum x7 -> x0, waiting for transfers between devices: 612 us -> none  [the longest x4 328 us: branch_total(): return lax.psum(partial_term, 'tensor')]
    ppermute x0 -> x143, waiting for transfers between devices: none -> 284 us  [the longest x119 218 us: swap(): return lax.ppermute(value, AXES, pairs)]
    reduce_scatter x9 -> x0, waiting for transfers between devices: 179 us -> none  [the longest x4 94.6 us: backward_layer(): lax.psum_scatter(value_term, 'seq', scatter_dimension=1, tiled=True)]
    all_gather x16 -> x0, blocking collectives: 149 us -> none  [the longest x4 31.5 us: forward_layer(): lax.all_gather(value_rows, 'seq', axis=1, tiled=True)]
    dot_general x64 -> x1, matrix products: 134 us -> 0.22 us  [small_params(): every = jnp.dot(pick, rows.reshape(32, -1), preferred_element_type=F32)]
    ppermute x0 -> x143, starting transfers between devices: none -> 129 us  [the longest x119 99.7 us: swap(): return lax.ppermute(value, AXES, pairs)]
    pallas_call x0 -> x20, Pallas kernels: none -> 123 us  [call(): pl.pallas_call(kernel, out_shape=[jax.ShapeDtypeStruct(s, d) for s, d in...]
    unnamed x30 -> x0, waiting for transfers between devices: 57 us -> none
  transfers between devices with their start and end apart: 25 -> 143, of which waited for: 15 -> 64; matrix products, arithmetic and copies ran while one was open for 15% -> 8% of each run, Pallas kernels for 0% -> 10%
where the time goes in v1:
time: 628 us; the launch traced here: 622 us
  waiting for transfers between devices  284 us (45%)
  starting transfers between devices  129 us (21%)
  Pallas kernels  123 us (20%)
  local copies, waits for them, and re-layouts  46.1 us (7%)
  other arithmetic  35.5 us (6%)
    ppermute x119, waiting for transfers between devices, swap(): return lax.ppermute(value, AXES, pairs)  218 us
    pallas_call x20, Pallas kernels, call(): pl.pallas_call(kernel, out_shape=[jax.ShapeDtypeStruct(s, d) for s, d in...  123 us
    ppermute x119, starting transfers between devices, swap(): return lax.ppermute(value, AXES, pairs)  99.7 us
    ppermute x24, waiting for transfers between devices, swap_group(): return lax.ppermute(value, AXES, pairs)  66.5 us
    unnamed x305, local copies, waits for them, and re-layouts  36.1 us
    ppermute x24, starting transfers between devices, swap_group(): return lax.ppermute(value, AXES, pairs)  29.5 us
    convert_element_type x36, other arithmetic, scatter_sum(): got = swap(parts[step].astype(BF), order[step], mesh_shape).astype(F32)  14.9 us
    concatenate x24, other arithmetic, gather_block(): cur = jnp.concatenate([cur, swap(cur, bit, mesh_shape)], axis=0)  13.7 us
  transfers between devices with their start and end apart: 143, of which 64 were waited for; matrix products, arithmetic and copies ran while one was open for 8% of the time, Pallas kernels for 10%

profile of v1, /device:TPU:0, one launch (start us, length us, event | category | flops | bytes accessed | tf_op | source)
XLA Modules:
  0.0 621.7 jit_solution(4376364473217054638)
XLA Ops:
  18.3 6.6 %collective-permute-done.1 = bf16[2,16,128]{2,1,0:T(8,128)(2,1)S(1)} collective-permute-done((bf16[2,16,128]{2,1,0:T(8,128)(2,1)S(1)}, bf16[2,16,128]{2,1,0:T(8,128)(2,1)S(1)}, u32[]{:S(2)}, u32[]{:S(2)}) %collective-permute-start.1) | collective-permute-done | bytes 8224 | tf_op jit(solution)/shard_map/ppermute | solution.py:46
  72.9 5.5 collective-permute-done.14.refs_5_
  90.7 4.5 project.2
  95.6 8.0 %collective-permute-done.46 = bf16[2,96,768]{2,1,0:T(8,128)(2,1)S(1)} collective-permute-done((bf16[2,96,768]{2,1,0:T(8,128)(2,1)S(1)}, bf16[2,96,768]{2,1,0:T(8,128)(2,1)S(1)}, u32[]{:S(2)}, u32[]{:S(2)}) %collective-permute-start.46) | collective-permute-done | bytes 294944 | tf_op jit(solution)/shard_map/ppermute | solution.py:46
  124.9 7.2 %attend.2 = (bf16[192,192]{1,0:T(8,128)(2,1)S(1)}, bf16[192,192]{1,0:T(8,128)(2,1)S(1)}, bf16[192,192]{1,0:T(8,128)(2,1)S(1)}, bf16[192,192]{1,0:T(8,128)(2,1)S(...) custom-call(s32[1]{0:T(128)} %bitcast.count_ref, ...), custom_call_target="tpu_custom_call" | custom-call | flops 3623878656 | bytes 4000000 | tf_op jit(solution)/shard_map/attend/pallas_call | solution.py:180
  133.6 21.7 %collective-permute-done.47 = bf16[4,96,768]{2,1,0:T(8,128)(2,1)S(1)} collective-permute-done((bf16[4,96,768]{2,1,0:T(8,128)(2,1)S(1)}, bf16[4,96,768]{2,1,0:T(8,128)(2,1)S(1)}, u32[]{:S(2)}, u32[]{:S(2)}) %collective-permute-start.47) | collective-permute-done | bytes 589856 | tf_op jit(solution)/shard_map/ppermute | solution.py:46
  160.3 7.6 %collective-permute-done.69 = bf16[4,96,768]{2,1,0:T(8,128)(2,1)S(1)} collective-permute-done((bf16[4,96,768]{2,1,0:T(8,128)(2,1)S(1)}, bf16[4,96,768]{2,1,0:T(8,128)(2,1)S(1)}, u32[]{:S(2)}, u32[]{:S(2)}) %collective-permute-start.69) | collective-permute-done | bytes 589856 | tf_op jit(solution)/shard_map/ppermute | solution.py:46
  171.7 27.7 %collective-permute-done.32.m3 = bf16[192,192]{1,0:T(8,128)(2,1)S(1)} collective-permute-done((bf16[192,192]{1,0:T(8,128)(2,1)S(1)}, bf16[192,192]{1,0:T(8,128)(2,1)S(1)}, u32[]{:S(2)}, u32[]{:S(2)}) %collective-permute-start.32) | collective-permute-done | bytes 73760 | tf_op jit(solution)/shard_map/ppermute | solution.py:58
  227.2 13.4 %mlp.2 = (f32[192,768]{1,0:T(8,128)}, f32[192,768]{1,0:T(8,128)}, bf16[4,192,192]{2,1,0:T(8,128)(2,1)S(1)}, bf16[384,192]{1,0:T(8,128)(2,1)S(1)}, bf16[384,192]{...) custom-call(bf16[192,192]{1,0:T(8,128)(2,1)S(1)} %copy-done.61, ...), custom_call_target="tpu_custom_call" | custom-call | flops 2038431744 | bytes 4000000 | tf_op jit(solution)/shard_map/mlp/pallas_call | solution.py:180
  256.8 7.5 %collective-permute-done.53.p3 = bf16[192,576]{1,0:T(8,128)(2,1)S(1)} collective-permute-done((bf16[192,576]{1,0:T(8,128)(2,1)S(1)}, bf16[192,576]{1,0:T(8,128)(2,1)S(1)}, u32[]{:S(2)}, u32[]{:S(2)}) %collective-permute-start.53) | collective-permute-done | bytes 221216 | tf_op jit(solution)/shard_map/ppermute | solution.py:58
  268.4 7.2 %attend.3 = (bf16[192,192]{1,0:T(8,128)(2,1)S(1)}, bf16[192,192]{1,0:T(8,128)(2,1)S(1)}, bf16[192,192]{1,0:T(8,128)(2,1)S(1)}, bf16[192,192]{1,0:T(8,128)(2,1)S(...) custom-call(s32[1]{0:T(128)} %bitcast.count_ref, ...), custom_call_target="tpu_custom_call" | custom-call | flops 3623878656 | bytes 4000000 | tf_op jit(solution)/shard_map/attend/pallas_call | solution.py:180
  286.8 11.8 %mlp.3 = (f32[192,768]{1,0:T(8,128)S(1)}, f32[192,768]{1,0:T(8,128)S(1)}, bf16[4,192,192]{2,1,0:T(8,128)(2,1)S(1)}, bf16[384,192]{1,0:T(8,128)(2,1)S(1)}, bf16[3...) custom-call(bf16[192,192]{1,0:T(8,128)(2,1)S(1)} %get-tuple-element.132.m0, ...), custom_call_target="tpu_custom_call" | custom-call | flops 2038431744 | bytes 4000000 | tf_op jit(solution)/shard_map/mlp/pallas_call | solution.py:180
  298.7 10.9 %mlp_back.2 = (bf16[192,192]{1,0:T(8,128)(2,1)S(1)}, bf16[192,192]{1,0:T(8,128)(2,1)S(1)}, bf16[192,192]{1,0:T(8,128)(2,1)S(1)}, bf16[192,192]{1,0:T(8,128)(2,1)...) custom-call(bf16[192,768]{1,0:T(8,128)(2,1)S(1)} %dynamic-slice_bitc, ...), custom_call_target="tpu_custom_call" | custom-call | flops 2038431744 | bytes 4000000 | tf_op jit(solution)/shard_map/mlp_back/pallas_call | solution.py:180
  318.8 10.9 %attend_back.2 = (bf16[768,192]{1,0:T(8,128)(2,1)S(1)}, bf16[4,192,384]{2,1,0:T(8,128)(2,1)S(1)}, bf16[4,192,384]{2,1,0:T(8,128)(2,1)S(1)}) custom-call(s32[1]{0:T(128)} %bitcast.count_ref, bf16[192,192]{1,0:T(8,128)(2,1)S(1)} %get-tuple-element.139.d0, bf16[192,192]{1,0:T(8,128)(2,1)S(1)} %collective-permute-done.76.d1, ...), custom_call_target="tpu_custom_call" | custom-call | flops 9059696640 | bytes 4000000 | tf_op jit(solution)/shard_map/attend_back/pallas_call | solution.py:180
  335.9 6.0 collective-permute-done.82.d3
  341.9 4.4 collective-permute-done.81.d2
  351.2 11.6 %mlp_back.3 = (bf16[192,192]{1,0:T(8,128)(2,1)S(1)}, bf16[192,192]{1,0:T(8,128)(2,1)S(1)}, bf16[192,192]{1,0:T(8,128)(2,1)S(1)}, bf16[192,192]{1,0:T(8,128)(2,1)...) custom-call(f32[192,768]{1,0:T(8,128)} %copy-done.51, ...), custom_call_target="tpu_custom_call" | custom-call | flops 2038431744 | bytes 4000000 | tf_op jit(solution)/shard_map/mlp_back/pallas_call | solution.py:180
  370.8 10.7 %attend_back.3 = (bf16[768,192]{1,0:T(8,128)(2,1)S(1)}, bf16[4,192,384]{2,1,0:T(8,128)(2,1)S(1)}, bf16[4,192,384]{2,1,0:T(8,128)(2,1)S(1)}) custom-call(s32[1]{0:T(128)} %bitcast.count_ref, bf16[192,192]{1,0:T(8,128)(2,1)S(1)} %get-tuple-element.154.d0, bf16[192,192]{1,0:T(8,128)(2,1)S(1)} %collective-permute-done.83.d1, ...), custom_call_target="tpu_custom_call" | custom-call | flops 9059696640 | bytes 4000000 | tf_op jit(solution)/shard_map/attend_back/pallas_call | solution.py:180
  393.4 6.6 %collective-permute-done.100 = f32[16,768]{1,0:T(8,128)S(1)} collective-permute-done((f32[16,768]{1,0:T(8,128)S(1)}, f32[16,768]{1,0:T(8,128)S(1)}, u32[]{:S(2)}, u32[]{:S(2)}) %collective-permute-start.100) | collective-permute-done | bytes 49184 | tf_op jit(solution)/shard_map/ppermute | solution.py:46
  403.6 6.5 %project_back.3 = (f32[192,768]{1,0:T(8,128)}, bf16[4,192,576]{2,1,0:T(8,128)(2,1)}, f32[8,768]{1,0:T(8,128)S(1)}, f32[4,1,576]{2,1,0:T(1,128)S(1)}) custom-call(bf16[192,576]{1,0:T(8,128)(2,1)S(1)} %pad_maximum_fusion.24.d0, bf16[192,576]{1,0:T(8,128)(2,1)S(1)} %collective-permute-done.87.d1, bf16[192,576]{1,0:T(8,128)(2,1)S(1)} %collective-permute-done.88.d2, ...), custom_call_target="tpu_custom_call" | custom-call | flops 679477248 | bytes 4000000 | tf_op jit(solution)/shard_map/project_back/pallas_call | solution.py:180
  410.1 11.9 %collective-permute-done.74.p2 = bf16[192,768]{1,0:T(8,128)(2,1)S(1)} collective-permute-done((bf16[192,768]{1,0:T(8,128)(2,1)S(1)}, bf16[192,768]{1,0:T(8,128)(2,1)S(1)}, u32[]{:S(2)}, u32[]{:S(2)}) %collective-permute-start.74) | collective-permute-done | bytes 294944 | tf_op jit(solution)/shard_map/ppermute | solution.py:46
  422.1 5.8 collective-permute-done.75.p3
  464.2 8.6 %collective-permute-done.90.p1 = bf16[192,768]{1,0:T(8,128)(2,1)S(1)} collective-permute-done((bf16[192,768]{1,0:T(8,128)(2,1)S(1)}, bf16[192,768]{1,0:T(8,128)(2,1)S(1)}, u32[]{:S(2)}, u32[]{:S(2)}) %collective-permute-start.90) | collective-permute-done | bytes 294944 | tf_op jit(solution)/shard_map/ppermute | solution.py:46
  472.7 7.5 %collective-permute-done.133 = bf16[8,96,768]{2,1,0:T(8,128)(2,1)} collective-permute-done((bf16[8,96,768]{2,1,0:T(8,128)(2,1)}, bf16[8,96,768]{2,1,0:T(8,128)(2,1)}, u32[]{:S(2)}, u32[]{:S(2)}) %collective-permute-start.133) | collective-permute-done | bytes 1179680 | tf_op jit(solution)/shard_map/ppermute | solution.py:46
  488.7 6.3 %collective-permute-done.92.p3 = bf16[192,768]{1,0:T(8,128)(2,1)S(1)} collective-permute-done((bf16[192,768]{1,0:T(8,128)(2,1)S(1)}, bf16[192,768]{1,0:T(8,128)(2,1)S(1)}, u32[]{:S(2)}, u32[]{:S(2)}) %collective-permute-start.92) | collective-permute-done | bytes 294944 | tf_op jit(solution)/shard_map/ppermute | solution.py:46
  496.7 8.1 %collective-permute-done.139 = bf16[8,96,768]{2,1,0:T(8,128)(2,1)} collective-permute-done((bf16[8,96,768]{2,1,0:T(8,128)(2,1)}, bf16[8,96,768]{2,1,0:T(8,128)(2,1)}, u32[]{:S(2)}, u32[]{:S(2)}) %collective-permute-start.139) | collective-permute-done | bytes 1179680 | tf_op jit(solution)/shard_map/ppermute | solution.py:46
  516.1 6.5 %collective-permute-done.134 = bf16[4,96,768]{2,1,0:T(8,128)(2,1)S(1)} collective-permute-done((bf16[4,96,768]{2,1,0:T(8,128)(2,1)}, bf16[4,96,768]{2,1,0:T(8,128)(2,1)S(1)}, u32[]{:S(2)}, u32[]{:S(2)}) %collective-permute-start.134) | collective-permute-done | bytes 589856 | tf_op jit(solution)/shard_map/ppermute | solution.py:46
  527.6 32.6 %collective-permute-done.140 = bf16[4,96,768]{2,1,0:T(8,128)(2,1)S(1)} collective-permute-done((bf16[4,96,768]{2,1,0:T(8,128)(2,1)}, bf16[4,96,768]{2,1,0:T(8,128)(2,1)S(1)}, u32[]{:S(2)}, u32[]{:S(2)}) %collective-permute-start.140) | collective-permute-done | bytes 589856 | tf_op jit(solution)/shard_map/ppermute | solution.py:46
  565.7 5.5 collective-permute-done.136
  578.3 4.3 collective-permute-done.129
  584.6 5.8 collective-permute-done.130
  611.9 6.0 collective-permute-done.124
  (733 shorter events, 313.2 us)
Async XLA Ops:
  26.7 33.6 %collective-permute-start.45 = (bf16[1,96,768]{2,1,0:T(8,128)(2,1)S(1)}, bf16[1,96,768]{2,1,0:T(8,128)(2,1)}, u32[]{:S(2)}, u32[]{:S(2)}) collective-permute-start(bf16[1,96,768]{2,1,0:T(8,128)(2,1)S(1)} %pad_maximum_fusion.32), channel_id=1, source_target_pairs={{0,2},{1,3},{2,0},{3,1},{4,6},{5,7},{6,4},{7,5},{8,10},{9,11},{10,... | collective-permute-start | bytes 442376 | tf_op jit(solution)/shard_map/ppermute | solution.py:46
  88.9 30.6 %collective-permute-start.41 = (bf16[4,96,768]{2,1,0:T(8,128)(2,1)S(1)}, bf16[4,96,768]{2,1,0:T(8,128)(2,1)S(1)}, u32[]{:S(2)}, u32[]{:S(2)}) collective-permute-start(bf16[4,96,768]{2,1,0:T(8,128)(2,1)S(1)} %pad_maximum_fusion.6), channel_id=1, source_target_pairs={{0,8},{1,9},{2,10},{3,11},{4,12},{5,13},{6,14},{7,15},{8,0},{9,1},... | collective-permute-start | bytes 1769480 | tf_op jit(solution)/shard_map/ppermute | solution.py:46
  108.9 90.4 %collective-permute-start.36 = (bf16[8,96,768]{2,1,0:T(8,128)(2,1)S(1)}, bf16[8,96,768]{2,1,0:T(8,128)(2,1)S(1)}, u32[]{:S(2)}, u32[]{:S(2)}) collective-permute-start(bf16[8,96,768]{2,1,0:T(8,128)(2,1)S(1)} %pad_maximum_fusion.refs_12_), channel_id=1, source_target_pairs={{0,8},{1,9},{2,10},{3,11},{4,12},{5,13},{6,14},{7,15},{8,0},{9,1},... | collective-permute-start | bytes 3538952 | tf_op jit(solution)/shard_map/ppermute | solution.py:46
  119.4 35.9 %collective-permute-start.47 = (bf16[4,96,768]{2,1,0:T(8,128)(2,1)S(1)}, bf16[4,96,768]{2,1,0:T(8,128)(2,1)S(1)}, u32[]{:S(2)}, u32[]{:S(2)}) collective-permute-start(bf16[4,96,768]{2,1,0:T(8,128)(2,1)S(1)} %pad_maximum_fusion.7), channel_id=1, source_target_pairs={{0,8},{1,9},{2,10},{3,11},{4,12},{5,13},{6,14},{7,15},{8,0},{9,1},... | collective-permute-start | bytes 1769480 | tf_op jit(solution)/shard_map/ppermute | solution.py:46
  120.0 37.7 %collective-permute-start.63 = (bf16[4,96,768]{2,1,0:T(8,128)(2,1)S(1)}, bf16[4,96,768]{2,1,0:T(8,128)(2,1)S(1)}, u32[]{:S(2)}, u32[]{:S(2)}) collective-permute-start(bf16[4,96,768]{2,1,0:T(8,128)(2,1)S(1)} %pad_maximum_fusion.8), channel_id=1, source_target_pairs={{0,16},{1,17},{2,18},{3,19},{4,20},{5,21},{6,22},{7,23},{8,24},{9,... | collective-permute-start | bytes 1769480 | tf_op jit(solution)/shard_map/ppermute | solution.py:46
  121.6 46.3 %collective-permute-start.69 = (bf16[4,96,768]{2,1,0:T(8,128)(2,1)S(1)}, bf16[4,96,768]{2,1,0:T(8,128)(2,1)S(1)}, u32[]{:S(2)}, u32[]{:S(2)}) collective-permute-start(bf16[4,96,768]{2,1,0:T(8,128)(2,1)S(1)} %pad_maximum_fusion.9), channel_id=1, source_target_pairs={{0,8},{1,9},{2,10},{3,11},{4,12},{5,13},{6,14},{7,15},{8,0},{9,1},... | collective-permute-start | bytes 1769480 | tf_op jit(solution)/shard_map/ppermute | solution.py:46
  124.3 75.6 %collective-permute-start.42 = (bf16[8,96,768]{2,1,0:T(8,128)(2,1)S(1)}, bf16[8,96,768]{2,1,0:T(8,128)(2,1)}, u32[]{:S(2)}, u32[]{:S(2)}) collective-permute-start(bf16[8,96,768]{2,1,0:T(8,128)(2,1)S(1)} %pad_maximum_fusion.1.refs_16_), channel_id=1, source_target_pairs={{0,16},{1,17},{2,18},{3,19},{4,20},{5,21},{6,22},{7,23},{8,24},{9,... | collective-permute-start | bytes 3538952 | tf_op jit(solution)/shard_map/ppermute | solution.py:46
  167.9 32.1 %collective-permute-start.37 = (bf16[8,96,768]{2,1,0:T(8,128)(2,1)S(1)}, bf16[8,96,768]{2,1,0:T(8,128)(2,1)S(1)}, u32[]{:S(2)}, u32[]{:S(2)}) collective-permute-start(bf16[8,96,768]{2,1,0:T(8,128)(2,1)S(1)} %pad_maximum_fusion.refs_12_), channel_id=1, source_target_pairs={{0,4},{1,5},{2,6},{3,7},{4,0},{5,1},{6,2},{7,3},{8,12},{9,13},{10,... | collective-permute-start | bytes 3538952 | tf_op jit(solution)/shard_map/ppermute | solution.py:46
  167.9 32.5 %collective-permute-start.48 = (bf16[8,96,768]{2,1,0:T(8,128)(2,1)S(1)}, bf16[8,96,768]{2,1,0:T(8,128)(2,1)S(1)}, u32[]{:S(2)}, u32[]{:S(2)}) collective-permute-start(bf16[8,96,768]{2,1,0:T(8,128)(2,1)S(1)} %pad_maximum_fusion.2.refs_0_), channel_id=1, source_target_pairs={{0,1},{1,0},{2,3},{3,2},{4,5},{5,4},{6,7},{7,6},{8,9},{9,8},{10,11... | collective-permute-start | bytes 3538952 | tf_op jit(solution)/shard_map/ppermute | solution.py:46
  169.8 29.6 %collective-permute-start.32 = (bf16[192,192]{1,0:T(8,128)(2,1)S(1)}, bf16[192,192]{1,0:T(8,128)(2,1)S(1)}, u32[]{:S(2)}, u32[]{:S(2)}) collective-permute-start(bf16[192,192]{1,0:T(8,128)(2,1)S(1)} %get-tuple-element.126), channel_id=1, source_target_pairs={{0,9},{1,8},{2,11},{3,10},{4,13},{5,12},{6,15},{7,14},{8,1},{9,0},... | collective-permute-start | bytes 221192 | tf_op jit(solution)/shard_map/ppermute | solution.py:58
  200.0 42.8 %collective-permute-start.49 = (bf16[8,96,768]{2,1,0:T(8,128)(2,1)S(1)}, bf16[8,96,768]{2,1,0:T(8,128)(2,1)S(1)}, u32[]{:S(2)}, u32[]{:S(2)}) collective-permute-start(bf16[8,96,768]{2,1,0:T(8,128)(2,1)S(1)} %pad_maximum_fusion.2.refs_0_), channel_id=1, source_target_pairs={{0,4},{1,5},{2,6},{3,7},{4,0},{5,1},{6,2},{7,3},{8,12},{9,13},{10,... | collective-permute-start | bytes 3538952 | tf_op jit(solution)/shard_map/ppermute | solution.py:46
  200.4 42.4 %collective-permute-start.50 = (bf16[8,96,768]{2,1,0:T(8,128)(2,1)S(1)}, bf16[8,96,768]{2,1,0:T(8,128)(2,1)}, u32[]{:S(2)}, u32[]{:S(2)}) collective-permute-start(bf16[8,96,768]{2,1,0:T(8,128)(2,1)S(1)} %collective-permute-done.48.refs_1_), channel_id=1, source_target_pairs={{0,4},{1,5},{2,6},{3,7},{4,0},{5,1},{6,2},{7,3},{8,12},{9,13},{10,... | collective-permute-start | bytes 3538952 | tf_op jit(solution)/shard_map/ppermute | solution.py:46
  202.8 46.9 %collective-permute-start.64 = (bf16[8,96,768]{2,1,0:T(8,128)(2,1)}, bf16[8,96,768]{2,1,0:T(8,128)(2,1)}, u32[]{:S(2)}, u32[]{:S(2)}) collective-permute-start(bf16[8,96,768]{2,1,0:T(8,128)(2,1)} %pad_maximum_fusion.3.refs_4_), channel_id=1, source_target_pairs={{0,8},{1,9},{2,10},{3,11},{4,12},{5,13},{6,14},{7,15},{8,0},{9,1},... | collective-permute-start | bytes 3538952 | tf_op jit(solution)/shard_map/ppermute | solution.py:46
  207.3 42.9 %collective-permute-start.70 = (bf16[8,96,768]{2,1,0:T(8,128)(2,1)}, bf16[8,96,768]{2,1,0:T(8,128)(2,1)}, u32[]{:S(2)}, u32[]{:S(2)}) collective-permute-start(bf16[8,96,768]{2,1,0:T(8,128)(2,1)} %pad_maximum_fusion.4.refs_8_), channel_id=1, source_target_pairs={{0,16},{1,17},{2,18},{3,19},{4,20},{5,21},{6,22},{7,23},{8,24},{9,... | collective-permute-start | bytes 3538952 | tf_op jit(solution)/shard_map/ppermute | solution.py:46
  249.7 30.4 %collective-permute-start.65 = (bf16[8,96,768]{2,1,0:T(8,128)(2,1)}, bf16[8,96,768]{2,1,0:T(8,128)(2,1)S(1)}, u32[]{:S(2)}, u32[]{:S(2)}) collective-permute-start(bf16[8,96,768]{2,1,0:T(8,128)(2,1)} %pad_maximum_fusion.3.refs_4_), channel_id=1, source_target_pairs={{0,4},{1,5},{2,6},{3,7},{4,0},{5,1},{6,2},{7,3},{8,12},{9,13},{10,... | collective-permute-start | bytes 3538952 | tf_op jit(solution)/shard_map/ppermute | solution.py:46
  250.2 30.4 %collective-permute-start.71 = (bf16[8,96,768]{2,1,0:T(8,128)(2,1)}, bf16[8,96,768]{2,1,0:T(8,128)(2,1)S(1)}, u32[]{:S(2)}, u32[]{:S(2)}) collective-permute-start(bf16[8,96,768]{2,1,0:T(8,128)(2,1)} %pad_maximum_fusion.4.refs_8_), channel_id=1, source_target_pairs={{0,4},{1,5},{2,6},{3,7},{4,0},{5,1},{6,2},{7,3},{8,12},{9,13},{10,... | collective-permute-start | bytes 3538952 | tf_op jit(solution)/shard_map/ppermute | solution.py:46
  251.0 31.9 %collective-permute-start.66 = (bf16[8,96,768]{2,1,0:T(8,128)(2,1)}, bf16[8,96,768]{2,1,0:T(8,128)(2,1)}, u32[]{:S(2)}, u32[]{:S(2)}) collective-permute-start(bf16[8,96,768]{2,1,0:T(8,128)(2,1)} %collective-permute-done.64.refs_5_), channel_id=1, source_target_pairs={{0,4},{1,5},{2,6},{3,7},{4,0},{5,1},{6,2},{7,3},{8,12},{9,13},{10,... | collective-permute-start | bytes 3538952 | tf_op jit(solution)/shard_map/ppermute | solution.py:46
  255.0 27.9 %collective-permute-start.72 = (bf16[8,96,768]{2,1,0:T(8,128)(2,1)}, bf16[8,96,768]{2,1,0:T(8,128)(2,1)}, u32[]{:S(2)}, u32[]{:S(2)}) collective-permute-start(bf16[8,96,768]{2,1,0:T(8,128)(2,1)} %collective-permute-done.70.refs_9_), channel_id=1, source_target_pairs={{0,4},{1,5},{2,6},{3,7},{4,0},{5,1},{6,2},{7,3},{8,12},{9,13},{10,... | collective-permute-start | bytes 3538952 | tf_op jit(solution)/shard_map/ppermute | solution.py:46
  382.2 47.4 %collective-permute-start.132 = (bf16[4,192,768]{2,1,0:T(8,128)(2,1)}, bf16[4,192,768]{2,1,0:T(8,128)(2,1)}, u32[]{:S(2)}, u32[]{:S(2)}) collective-permute-start(bf16[4,192,768]{2,1,0:T(8,128)(2,1)} %get-tuple-element.215.r_own), channel_id=1, source_target_pairs={{0,4},{1,5},{2,6},{3,7},{4,0},{5,1},{6,2},{7,3},{8,12},{9,13},{10,... | collective-permute-start | bytes 3538952 | tf_op jit(solution)/shard_map/ppermute | solution.py:46
  401.5 39.4 %collective-permute-start.138 = (bf16[4,192,768]{2,1,0:T(8,128)(2,1)}, bf16[4,192,768]{2,1,0:T(8,128)(2,1)}, u32[]{:S(2)}, u32[]{:S(2)}) collective-permute-start(bf16[4,192,768]{2,1,0:T(8,128)(2,1)} %get-tuple-element.223.r_own), channel_id=1, source_target_pairs={{0,4},{1,5},{2,6},{3,7},{4,0},{5,1},{6,2},{7,3},{8,12},{9,13},{10,... | collective-permute-start | bytes 3538952 | tf_op jit(solution)/shard_map/ppermute | solution.py:46
  401.5 39.5 %collective-permute-start.126 = (bf16[4,192,768]{2,1,0:T(8,128)(2,1)}, bf16[4,192,768]{2,1,0:T(8,128)(2,1)}, u32[]{:S(2)}, u32[]{:S(2)}) collective-permute-start(bf16[4,192,768]{2,1,0:T(8,128)(2,1)} %get-tuple-element.207.r_own), channel_id=1, source_target_pairs={{0,4},{1,5},{2,6},{3,7},{4,0},{5,1},{6,2},{7,3},{8,12},{9,13},{10,... | collective-permute-start | bytes 3538952 | tf_op jit(solution)/shard_map/ppermute | solution.py:46
  451.2 29.1 %collective-permute-start.133 = (bf16[8,96,768]{2,1,0:T(8,128)(2,1)}, bf16[8,96,768]{2,1,0:T(8,128)(2,1)}, u32[]{:S(2)}, u32[]{:S(2)}) collective-permute-start(bf16[8,96,768]{2,1,0:T(8,128)(2,1)} %get-tuple-element.217), channel_id=1, source_target_pairs={{0,16},{1,17},{2,18},{3,19},{4,20},{5,21},{6,22},{7,23},{8,24},{9,... | collective-permute-start | bytes 3538952 | tf_op jit(solution)/shard_map/ppermute | solution.py:46
  452.0 52.8 %collective-permute-start.139 = (bf16[8,96,768]{2,1,0:T(8,128)(2,1)}, bf16[8,96,768]{2,1,0:T(8,128)(2,1)}, u32[]{:S(2)}, u32[]{:S(2)}) collective-permute-start(bf16[8,96,768]{2,1,0:T(8,128)(2,1)} %get-tuple-element.225), channel_id=1, source_target_pairs={{0,16},{1,17},{2,18},{3,19},{4,20},{5,21},{6,22},{7,23},{8,24},{9,... | collective-permute-start | bytes 3538952 | tf_op jit(solution)/shard_map/ppermute | solution.py:46
  458.7 47.6 %collective-permute-start.127 = (bf16[8,96,768]{2,1,0:T(8,128)(2,1)}, bf16[8,96,768]{2,1,0:T(8,128)(2,1)}, u32[]{:S(2)}, u32[]{:S(2)}) collective-permute-start(bf16[8,96,768]{2,1,0:T(8,128)(2,1)} %get-tuple-element.209), channel_id=1, source_target_pairs={{0,8},{1,9},{2,10},{3,11},{4,12},{5,13},{6,14},{7,15},{8,0},{9,1},... | collective-permute-start | bytes 3538952 | tf_op jit(solution)/shard_map/ppermute | solution.py:46
  472.7 40.8 %collective-permute-start.105 = (bf16[4,192,576]{2,1,0:T(8,128)(2,1)S(1)}, bf16[4,192,576]{2,1,0:T(8,128)(2,1)S(1)}, u32[]{:S(2)}, u32[]{:S(2)}) collective-permute-start(bf16[4,192,576]{2,1,0:T(8,128)(2,1)S(1)} %copy-done.45), channel_id=1, source_target_pairs={{0,4},{1,5},{2,6},{3,7},{4,0},{5,1},{6,2},{7,3},{8,12},{9,13},{10,... | collective-permute-start | bytes 2654216 | tf_op jit(solution)/shard_map/ppermute | solution.py:46
  485.8 38.9 %collective-permute-start.115 = (bf16[8,96,768]{2,1,0:T(8,128)(2,1)S(1)}, bf16[8,96,768]{2,1,0:T(8,128)(2,1)}, u32[]{:S(2)}, u32[]{:S(2)}) collective-permute-start(bf16[8,96,768]{2,1,0:T(8,128)(2,1)S(1)} %copy-done.70), channel_id=1, source_target_pairs={{0,1},{1,0},{2,3},{3,2},{4,5},{5,4},{6,7},{7,6},{8,9},{9,8},{10,11... | collective-permute-start | bytes 3538952 | tf_op jit(solution)/shard_map/ppermute | solution.py:46
  511.5 64.3 %collective-permute-start.121 = (bf16[8,96,768]{2,1,0:T(8,128)(2,1)S(1)}, bf16[8,96,768]{2,1,0:T(8,128)(2,1)}, u32[]{:S(2)}, u32[]{:S(2)}) collective-permute-start(bf16[8,96,768]{2,1,0:T(8,128)(2,1)S(1)} %get-tuple-element.201), channel_id=1, source_target_pairs={{0,8},{1,9},{2,10},{3,11},{4,12},{5,13},{6,14},{7,15},{8,0},{9,1},... | collective-permute-start | bytes 3538952 | tf_op jit(solution)/shard_map/ppermute | solution.py:46
  512.6 47.6 %collective-permute-start.140 = (bf16[4,96,768]{2,1,0:T(8,128)(2,1)}, bf16[4,96,768]{2,1,0:T(8,128)(2,1)S(1)}, u32[]{:S(2)}, u32[]{:S(2)}) collective-permute-start(bf16[4,96,768]{2,1,0:T(8,128)(2,1)} %fusion), channel_id=1, source_target_pairs={{0,8},{1,9},{2,10},{3,11},{4,12},{5,13},{6,14},{7,15},{8,0},{9,1},... | collective-permute-start | bytes 1769480 | tf_op jit(solution)/shard_map/ppermute | solution.py:46
  513.5 47.8 %collective-permute-start.128 = (bf16[4,96,768]{2,1,0:T(8,128)(2,1)}, bf16[4,96,768]{2,1,0:T(8,128)(2,1)S(1)}, u32[]{:S(2)}, u32[]{:S(2)}) collective-permute-start(bf16[4,96,768]{2,1,0:T(8,128)(2,1)} %fusion.2), channel_id=1, source_target_pairs={{0,16},{1,17},{2,18},{3,19},{4,20},{5,21},{6,22},{7,23},{8,24},{9,... | collective-permute-start | bytes 1769480 | tf_op jit(solution)/shard_map/ppermute | solution.py:46
  522.7 68.7 %collective-permute-start.107 = (bf16[8,96,768]{2,1,0:T(8,128)(2,1)S(1)}, bf16[8,96,768]{2,1,0:T(8,128)(2,1)S(1)}, u32[]{:S(2)}, u32[]{:S(2)}) collective-permute-start(bf16[8,96,768]{2,1,0:T(8,128)(2,1)S(1)} %get-tuple-element.182), channel_id=1, source_target_pairs={{0,1},{1,0},{2,3},{3,2},{4,5},{5,4},{6,7},{7,6},{8,9},{9,8},{10,11... | collective-permute-start | bytes 3538952 | tf_op jit(solution)/shard_map/ppermute | solution.py:46
  524.7 37.6 %collective-permute-start.135 = (bf16[2,96,768]{2,1,0:T(8,128)(2,1)S(1)}, bf16[2,96,768]{2,1,0:T(8,128)(2,1)S(1)}, u32[]{:S(2)}, u32[]{:S(2)}) collective-permute-start(bf16[2,96,768]{2,1,0:T(8,128)(2,1)S(1)} %fusion.7), channel_id=1, source_target_pairs={{0,1},{1,0},{2,3},{3,2},{4,5},{5,4},{6,7},{7,6},{8,9},{9,8},{10,11... | collective-permute-start | bytes 884744 | tf_op jit(solution)/shard_map/ppermute | solution.py:46
  560.2 30.2 %collective-permute-start.116 = (bf16[4,96,768]{2,1,0:T(8,128)(2,1)S(1)}, bf16[4,96,768]{2,1,0:T(8,128)(2,1)S(1)}, u32[]{:S(2)}, u32[]{:S(2)}) collective-permute-start(bf16[4,96,768]{2,1,0:T(8,128)(2,1)S(1)} %fusion.4), channel_id=1, source_target_pairs={{0,8},{1,9},{2,10},{3,11},{4,12},{5,13},{6,14},{7,15},{8,0},{9,1},... | collective-permute-start | bytes 1769480 | tf_op jit(solution)/shard_map/ppermute | solution.py:46
  (253 other events, 2998.9 us)

commit v2 on v1

--- a/solution.py
+++ b/solution.py
@@ -12,13 +12,17 @@
 AXES = ("dp", "seq", "tensor")
 BF = jnp.bfloat16
 F32 = jnp.float32
-VMEM_LIMIT = 48 * 1024 * 1024
+LIMIT = 48
+COST = 3.0e8
 
 BITS = {"x": 16, "y": 8, "c": 4, "z2": 2, "z1": 1}
 
 ORDER_E = ("z2", "z1", "x", "y")
-ORDER_S = ("z2", "z1", "y", "x")
-ORDERS_A = (("z2", "z1", "x", "y"), ("z2", "x", "y", "z1"), ("z2", "y", "z1", "x"))
+ORDER_S = ("z2", "y", "z1", "x")
+ORDER_A = ("z2", "x", "y", "z1")
+SUM_A = (("x", "y", "z1", "z2"), ("y", "x", "z1", "z2"))
+RING = (0, 1, 3, 2)
+
 
 SPEC_V = pl.BlockSpec(memory_space=pltpu.VMEM)
 SPEC_S = pl.BlockSpec(memory_space=pltpu.SMEM)
@@ -58,23 +62,78 @@
     return lax.ppermute(value, AXES, pairs)
 
 
-def gather_block(block, order, mesh_shape):
-    cur = block[None]
-    for bit in order[:3]:
-        cur = jnp.concatenate([cur, swap(cur, bit, mesh_shape)], axis=0)
-    more = swap(cur, order[3], mesh_shape)
-    return [cur, more, swap(cur, "c", mesh_shape), swap(more, "c", mesh_shape)]
-
-
-def scatter_sum(parts, order, mesh_shape):
-    parts = list(parts)
-    for step in range(4):
-        got = swap(parts[step].astype(BF), order[step], mesh_shape).astype(F32)
+def fence(*values):
+    return lax.optimization_barrier(values)
+
+
+class Gatherer:
+    def __init__(self, blocks, orders, mesh_shape):
+        self.cur, self.orders, self.mesh_shape, self.step = [b[None] for b in blocks], orders, mesh_shape, 0
+
+    def go(self):
+        got = [swap(c, o[self.step], self.mesh_shape) for c, o in zip(self.cur, self.orders)]
+        self.step += 1
+        if self.step < 4:
+            self.cur = list(fence(*(jnp.concatenate([c, g], axis=0) for c, g in zip(self.cur, got))))
+        else:
+            self.more = list(fence(*got))
+
+    def wait(self, *values):
+        count = len(self.cur)
+        out = fence(*self.cur, *values)
+        self.cur = list(out[:count])
+        return out[count:]
+
+    def before(self, *values):
+        now = self.more if self.step == 4 else self.cur
+        count = len(now)
+        out = fence(*now, *values)
+        if self.step == 4:
+            self.more = list(out[:count])
+        else:
+            self.cur = list(out[:count])
+        return out[count:]
+
+    def core(self):
+        turned = [[swap(v, "c", self.mesh_shape) for v in pair] for pair in zip(self.cur, self.more)]
+        return [[c, m, *t] for c, m, t in zip(self.cur, self.more, turned)]
+
+
+class Reducer:
+    def __init__(self, parts, order, mesh_shape):
+        self.parts, self.order, self.mesh_shape, self.step = list(parts), order, mesh_shape, 0
+
+    def send(self):
+        return swap(self.parts[self.step].astype(BF), self.order[self.step], self.mesh_shape)
+
+    def take(self, got):
+        step = self.step
         for later in range(step + 1, 5):
             size = 8 >> later if later < 4 else 1
             start = size if later < 4 else 0
-            parts[later] = parts[later].astype(F32) + got[start : start + size]
-    return parts[4][0]
+            self.parts[later] = self.parts[later].astype(F32) + got[start : start + size].astype(F32)
+        self.step += 1
+
+    def finish(self):
+        return self.parts[4][0]
+
+
+class Together:
+    def __init__(self, sums):
+        self.sums = sums
+
+    def wait(self, *values):
+        out = list(fence(*(r.parts[r.step] for r in self.sums), *values))
+        for r in self.sums:
+            r.parts[r.step] = out.pop(0)
+        return out
+
+    def go(self, *others):
+        got = [r.send() for r in self.sums]
+        out = fence(*got, *others)
+        for r, g in zip(self.sums, out):
+            r.take(g)
+        return out[len(got) :]
 
 
 def part_of(rel, order):
@@ -113,36 +172,40 @@
 
 
 class Loader:
-    def __init__(self, refs, orders, scratch, sems, col=0, width=None):
+    def __init__(self, refs, orders, scratch, sems, row=0, col=0, width=768):
         x, y, c, ten = place()
-        self.copies = {rz: [] for rz in range(4)}
-        count = 0
-        rows = 96 // len(orders)
-        for n, order in enumerate(orders):
-            for a in range(4):
-                ref = refs[n * 4 + a]
-                for j in range(8):
-                    rel = sum(BITS[order[k]] for k in range(3) if j & (1 << k))
-                    rel |= BITS[order[3]] if a & 1 else 0
-                    rel |= BITS["c"] if a & 2 else 0
-                    row = row_block(x, y, c, rel) * 96 + n * rows
-                    dst = scratch.at[xor_two(ten, rel & 3), pl.ds(pl.multiple_of(row, 32), rows)]
-                    src = ref.at[j] if width is None else ref.at[j, :, pl.ds(col, width)]
-                    self.copies[rel & 3].append(pltpu.make_async_copy(src, dst, sems.at[count]))
-                    count += 1
-        self.ten = ten
+        self.copies = {k: [] for k in range(4)}
+        self.ten = None if len(refs) == 1 else ten
+        if len(refs) == 1:
+            for n in range(32):
+                block, key = divmod(n, 4)
+                dst = scratch.at[key, pl.ds(block * 96, 96)]
+                src = refs[0].at[n, pl.ds(row, 96), pl.ds(col, width)]
+                self.copies[key].append(pltpu.make_async_copy(src, dst, sems.at[n]))
+            return
+        rows = 96 * 4 // len(refs)
+        for n in range(8 * len(refs)):
+            a, j = divmod(n, 8)
+            order = orders[a // 4]
+            rel = sum(BITS[order[k]] for k in range(3) if j & (1 << k))
+            rel |= BITS[order[3]] if a & 1 else 0
+            rel |= BITS["c"] if a & 2 else 0
+            to = pl.multiple_of(row_block(x, y, c, rel) * 96 + a // 4 * rows, 32)
+            dst = scratch.at[xor_two(ten, rel & 3), pl.ds(to, rows)]
+            src = refs[a].at[j, pl.ds(0, rows), pl.ds(col, width)]
+            self.copies[rel & 3].append(pltpu.make_async_copy(src, dst, sems.at[n]))
 
     def start(self):
-        for rz in range(4):
-            for copy in self.copies[rz]:
+        for k in range(4):
+            for copy in self.copies[k]:
                 copy.start()
 
-    def wait(self, rz):
-        for copy in self.copies[rz]:
+    def wait(self, k):
+        for copy in self.copies[k]:
             copy.wait()
 
-    def index(self, rz):
-        return xor_two(self.ten, rz)
+    def index(self, k):
+        return k if self.ten is None else xor_two(self.ten, k)
 
 
 def dot_nn(left, right):
@@ -167,38 +230,41 @@
     return rstd * (scaled - first - hat * second)
 
 
-def put_transposed(value, turned, own_ref, other_ref):
+def put_transposed(value, turned, own_ref, other_ref, absolute=False):
     x, y, c, _ = place()
     turned[...] = value.T
     for xy in range(4):
         for side, ref in ((0, own_ref), (4, other_ref)):
-            row = row_block(x, y, c, (16 if xy & 2 else 0) | (8 if xy & 1 else 0) | side) * 96
+            if absolute:
+                row = (2 * xy + xor_bit(c, side)) * 96
+            else:
+                row = row_block(x, y, c, (16 if xy & 2 else 0) | (8 if xy & 1 else 0) | side) * 96
             ref[pl.ds(xy * 96, 96), :] = turned[pl.ds(pl.multiple_of(row, 32), 96), :].astype(BF)
 
 
-def call(kernel, outs, scratch, specs, args, flops=0, name=None):
+def call(kernel, outs, scratch, specs, args, micros=1, name=None, ties=(), limit=LIMIT):
     return pl.pallas_call(
-        kernel,
+        lambda *refs: kernel(*refs[len(ties) :]),
         out_shape=[jax.ShapeDtypeStruct(s, d) for s, d in outs],
-        in_specs=specs,
+        in_specs=[SPEC_A] * len(ties) + list(specs),
         out_specs=[SPEC_V] * len(outs),
         scratch_shapes=scratch,
-        compiler_params=pltpu.CompilerParams(vmem_limit_bytes=VMEM_LIMIT),
-        cost_estimate=pl.CostEstimate(flops=flops, bytes_accessed=4000000, transcendentals=0),
+        compiler_params=pltpu.CompilerParams(vmem_limit_bytes=limit * 1024 * 1024),
+        cost_estimate=pl.CostEstimate(flops=int(micros * COST), bytes_accessed=1000, transcendentals=0),
         name=name,
-    )(*args)
+    )(*ties, *args)
 
 
 def project_kernel(n_a, x_ref, vec_ref, bias_ref, *refs):
     a_refs, refs = refs[:n_a], refs[n_a:]
     outs, (own_ref, other_ref, w, turned, sems) = refs[:4], refs[4:]
-    load = Loader(a_refs, ORDERS_A if n_a == 12 else (ORDER_A,), w, sems, 0, 640)
+    load = Loader(a_refs, (ORDER_A,), w, sems, 0, 0, 640)
     load.start()
     _, y, _, ten = place()
     hat, _ = norm_parts(x_ref[...].astype(F32))
     normed = hat * vec_ref[0:1, :] + vec_ref[1:2, :]
     low = normed.astype(BF)
-    put_transposed(normed, turned, own_ref, other_ref)
+    put_transposed(normed, turned, own_ref, other_ref, n_a == 1)
     for rz in range(4):
         load.wait(rz)
     for pair in range(4):
@@ -207,15 +273,12 @@
         outs[pair][...] = packed.astype(BF)
 
 
-ORDER_A = ("z2", "x", "y", "z1")
-
-
-def project(x, vec, bias, a, tokens):
+def project(x, vec, bias, a, tokens, ties=()):
     outs = [((tokens, 576), BF)] * 4 + [((384, tokens), BF)] * 2
-    scratch = [pltpu.VMEM((4, 768, 640), BF), pltpu.VMEM((768, tokens), F32), pltpu.SemaphoreType.DMA((8 * len(a),))]
+    scratch = [pltpu.VMEM((4, 768, 640), BF), pltpu.VMEM((768, tokens), F32), pltpu.SemaphoreType.DMA((32,))]
     return call(
         partial(project_kernel, len(a)), outs, scratch, [SPEC_V] * 3 + [SPEC_A] * len(a), (x, vec, bias, *a),
-        flops=2 * tokens * 768 * 2304, name="project",
+        micros=4, name="project", ties=ties,
     )
 
 
@@ -250,7 +313,7 @@
             lse_ref[rows, h : h + 1] = highest + jnp.log(weight)
 
 
-def attend(count, pieces, others):
+def attend(count, pieces, others, ties=()):
     tokens = pieces[0].shape[0]
     outs = [((tokens, 192), BF)] * 4 + [
         ((8 * tokens, 384), BF),
@@ -260,16 +323,17 @@
     ]
     return call(
         attend_kernel, outs, [], [SPEC_S] + [SPEC_V] * 8, (count, *pieces, *others),
-        flops=4 * 4 * tokens * 8 * tokens * 192 * 4, name="attend",
-    )
-
-
-def mlp_kernel(n_a, m0, m1, m2, m3, x_ref, vec_ref, eb_ref, *refs):
-    a_refs, e_refs, s_refs, refs = refs[:n_a], refs[n_a : n_a + 4], refs[n_a + 4 : n_a + 8], refs[n_a + 8 :]
+        micros=7, name="attend", ties=ties,
+    )
+
+
+def mlp_kernel(n_a, n_e, m0, m1, m2, m3, x_ref, vec_ref, eb_ref, *refs):
+    a_refs, e_refs = refs[:n_a], refs[n_a : n_a + n_e]
+    s_refs, refs = refs[n_a + n_e : n_a + 2 * n_e], refs[n_a + 2 * n_e :]
     (x_out, after_ref, mixed_ref, own_ref, other_ref, active_ref, slope_ref, wo, we, ws, turned, sa, se, ss) = refs
-    load_a = Loader(a_refs, ORDERS_A if n_a == 12 else (ORDER_A,), wo, sa, 512, 256)
-    load_e = Loader(e_refs, (ORDER_E,), we, se)
-    load_s = Loader(s_refs, (ORDER_S,), ws, ss)
+    load_a = Loader(a_refs, (ORDER_A,), wo, sa, 0, 512, 256)
+    load_e = Loader(e_refs, (ORDER_E,), we, se, 96)
+    load_s = Loader(s_refs, (ORDER_S,), ws, ss, 192)
     load_a.start()
     load_e.start()
     load_s.start()
@@ -286,7 +350,7 @@
     hat, _ = norm_parts(after)
     normed = hat * vec_ref[3:4, :] + vec_ref[4:5, :]
     low = normed.astype(BF)
-    put_transposed(normed, turned, own_ref, other_ref)
+    put_transposed(normed, turned, own_ref, other_ref, True)
     out = after + vec_ref[5:6, :]
     for rz in range(4):
         z = load_e.index(rz)
@@ -301,7 +365,7 @@
     x_out[...] = out
 
 
-def mlp(pieces, x, vec, eb, a, e, s):
+def mlp(pieces, x, vec, eb, a, e, s, ties=()):
     tokens = x.shape[0]
     outs = [
         ((tokens, 768), F32),
@@ -317,23 +381,24 @@
         pltpu.VMEM((4, 768, 768), BF),
         pltpu.VMEM((4, 768, 768), BF),
         pltpu.VMEM((768, tokens), F32),
-        pltpu.SemaphoreType.DMA((8 * len(a),)),
+        pltpu.SemaphoreType.DMA((32,)),
         pltpu.SemaphoreType.DMA((32,)),
         pltpu.SemaphoreType.DMA((32,)),
     ]
     return call(
-        partial(mlp_kernel, len(a)), outs, scratch, [SPEC_V] * 7 + [SPEC_A] * (len(a) + 8), (*pieces, x, vec, eb, *a, *e, *s),
-        flops=2 * tokens * 768 * 6912, name="mlp",
-    )
-
-
-def mlp_back_kernel(n_a, dy_ref, after_ref, vec_ref, slope_ref, *refs):
-    a_refs, e_refs, s_refs, refs = refs[:n_a], refs[n_a : n_a + 4], refs[n_a + 4 : n_a + 8], refs[n_a + 8 :]
+        partial(mlp_kernel, len(a), len(e)), outs, scratch, [SPEC_V] * 7 + [SPEC_A] * (len(a) + 2 * len(e)), (*pieces, x, vec, eb, *a, *e, *s),
+        micros=12, name="mlp", ties=ties,
+    )
+
+
+def mlp_back_kernel(n_a, n_e, dy_ref, after_ref, vec_ref, slope_ref, *refs):
+    a_refs, e_refs = refs[:n_a], refs[n_a : n_a + n_e]
+    s_refs, refs = refs[n_a + n_e : n_a + 2 * n_e], refs[n_a + 2 * n_e :]
     d_out, refs = refs[:4], refs[4:]
-    (da_ref, hid_ref, z_own, z_other, a_own, a_other, sums_ref, ebs_ref, wo, we, ws, turned, sa, se, ss) = refs
-    load_a = Loader(a_refs, ORDERS_A if n_a == 12 else (ORDER_A,), wo, sa, 512, 256)
-    load_e = Loader(e_refs, (ORDER_E,), we, se)
-    load_s = Loader(s_refs, (ORDER_S,), ws, ss)
+    (da_ref, hid_ref, a_own, a_other, sums_ref, ebs_ref, z_own, z_other, wo, we, ws, turned, sa, se, ss) = refs
+    load_a = Loader(a_refs, (ORDER_A,), wo, sa, 0, 512, 256)
+    load_e = Loader(e_refs, (ORDER_E,), we, se, 96)
+    load_s = Loader(s_refs, (ORDER_S,), ws, ss, 192)
     load_s.start()
     load_e.start()
     load_a.start()
@@ -341,7 +406,7 @@
     dy = dy_ref[...].astype(F32)
     dz = dy.astype(BF)
     dz_wide = dz.astype(F32)
-    put_transposed(dz_wide, turned, z_own, z_other)
+    put_transposed(dz_wide, turned, z_own, z_other, True)
     grad = jnp.zeros(dy.shape, F32)
     for rz in range(4):
         z = load_s.index(rz)
@@ -357,7 +422,7 @@
     da_ref[...] = d_after
     da = d_after.astype(BF)
     da_wide = da.astype(F32)
-    put_transposed(da_wide, turned, a_own, a_other)
+    put_transposed(da_wide, turned, a_own, a_other, n_e == 1)
     sums_ref[0:1, :] = jnp.sum(da_wide, axis=0, keepdims=True)
     sums_ref[1:2, :] = jnp.sum(grad * hat, axis=0, keepdims=True)
     sums_ref[2:3, :] = jnp.sum(grad, axis=0, keepdims=True)
@@ -370,30 +435,30 @@
         d_out[pair][...] = dot_nn(da, wo[g])[:, 64:].astype(BF)
 
 
-def mlp_back(dy, after, vec, slope, a, e, s):
+def mlp_back(dy, after, vec, slope, a, e, s, ties=()):
     tokens = dy.shape[0]
     outs = [((tokens, 192), BF)] * 4 + [
         ((tokens, 768), F32),
         ((4, tokens, 768), BF),
         ((384, tokens), BF),
         ((384, tokens), BF),
+        ((8, 768), F32),
+        ((4, 1, 768), F32),
         ((384, tokens), BF),
         ((384, tokens), BF),
-        ((8, 768), F32),
-        ((4, 1, 768), F32),
     ]
     scratch = [
         pltpu.VMEM((4, 768, 256), BF),
         pltpu.VMEM((4, 768, 768), BF),
         pltpu.VMEM((4, 768, 768), BF),
         pltpu.VMEM((768, tokens), F32),
-        pltpu.SemaphoreType.DMA((8 * len(a),)),
+        pltpu.SemaphoreType.DMA((32,)),
         pltpu.SemaphoreType.DMA((32,)),
         pltpu.SemaphoreType.DMA((32,)),
     ]
     return call(
-        partial(mlp_back_kernel, len(a)), outs, scratch, [SPEC_V] * 4 + [SPEC_A] * (len(a) + 8),
-        (dy, after, vec, slope, *a, *e, *s), flops=2 * tokens * 768 * 6912, name="mlp_back",
+        partial(mlp_back_kernel, len(a), len(e)), outs, scratch, [SPEC_V] * 4 + [SPEC_A] * (len(a) + 2 * len(e)),
+        (dy, after, vec, slope, *a, *e, *s), micros=11, name="mlp_back", ties=ties,
     )
 
 
@@ -444,7 +509,7 @@
             ref[pair] = dkv[pl.ds(pl.multiple_of(block * tokens, 64), tokens), :]
 
 
-def attend_back(count, pieces, kv, q, mixed, lse):
+def attend_back(count, pieces, kv, q, mixed, lse, ties=()):
     tokens = pieces[0].shape[0]
     outs = [((4 * tokens, 192), BF), ((4, tokens, 384), BF), ((4, tokens, 384), BF)]
     scratch = [
@@ -455,17 +520,23 @@
     ]
     return call(
         attend_back_kernel, outs, scratch, [SPEC_S] + [SPEC_V] * 8, (count, *pieces, kv, q, mixed, lse),
-        flops=10 * 4 * tokens * 8 * tokens * 192 * 4, name="attend_back",
-    )
-
-
-def project_back_kernel(n_a, d0, d1, d2, d3, da_ref, x_ref, vec_ref, *refs):
-    a_refs, refs = refs[:n_a], refs[n_a:]
-    dx_ref, dqkv_ref, sums_ref, bias_ref, w, sems = refs
-    load = Loader(a_refs, ORDERS_A if n_a == 12 else (ORDER_A,), w, sems, 0, 640)
+        micros=11, name="attend_back", ties=ties,
+    )
+
+
+def project_back_kernel(n_a, n_high, d0, d1, d2, d3, da_ref, x_ref, vec_ref, two_ref, ebs_ref, *refs):
+    high_refs, a_refs, refs = refs[:n_high], refs[n_high : n_high + n_a], refs[n_high + n_a :]
+    dx_ref, dqkv_ref, sums_ref, w, sems = refs
+    load = Loader(a_refs, (ORDER_A,), w, sems, 0, 0, 640)
     load.start()
     _, y, _, ten = place()
     hat, rstd = norm_parts(x_ref[...].astype(F32))
+    sums_ref[2:6, :] = two_ref[0:4, :]
+    sums_ref[10:16, :] = jnp.zeros((6, hat.shape[1]), F32)
+    for z in range(4):
+        sums_ref[6 + z : 7 + z, :] = ebs_ref[z]
+    if n_high:
+        sums_ref[16:32, :] = high_refs[0][...]
     for rz in range(4):
         load.wait(rz)
     grad = jnp.zeros(hat.shape, F32)
@@ -473,105 +544,140 @@
         g = group_of(y, ten, pair)
         piece = d[...]
         dqkv_ref[g] = piece
-        bias_ref[g] = jnp.sum(piece.astype(F32), axis=0, keepdims=True)
+        sums_ref[pl.ds(10 + g, 1), :576] = jnp.sum(piece.astype(F32), axis=0, keepdims=True)
         grad = grad + dot_nt(piece, w[g][:, :576])
     dx_ref[...] = da_ref[...] + norm_back(hat, rstd, vec_ref[0:1, :], grad)
     sums_ref[0:1, :] = jnp.sum(grad * hat, axis=0, keepdims=True)
     sums_ref[1:2, :] = jnp.sum(grad, axis=0, keepdims=True)
-    sums_ref[2:8, :] = jnp.zeros((6, hat.shape[1]), F32)
-
-
-def project_back(pieces, da, x, vec, a):
+
+
+def project_back(pieces, da, x, vec, two, ebs, high, a, ties=()):
     tokens = x.shape[0]
-    outs = [((tokens, 768), F32), ((4, tokens, 576), BF), ((8, 768), F32), ((4, 1, 576), F32)]
-    scratch = [pltpu.VMEM((4, 768, 640), BF), pltpu.SemaphoreType.DMA((8 * len(a),))]
+    outs = [((tokens, 768), F32), ((4, tokens, 576), BF), ((16 + 16 * len(high), 768), F32)]
+    scratch = [pltpu.VMEM((4, 768, 640), BF), pltpu.SemaphoreType.DMA((32,))]
     return call(
-        partial(project_back_kernel, len(a)), outs, scratch, [SPEC_V] * 7 + [SPEC_A] * len(a), (*pieces, da, x, vec, *a),
-        flops=2 * tokens * 768 * 2304, name="project_back",
-    )
-
-
-def emit(value, rz, order, outs):
+        partial(project_back_kernel, len(a), len(high)),
+        outs,
+        scratch,
+        [SPEC_V] * (9 + len(high)) + [SPEC_A] * len(a),
+        (*pieces, da, x, vec, two, ebs, *high, *a),
+        micros=4,
+        name="project_back",
+        ties=ties,
+    )
+
+
+def emit(value, rz, orders, outs):
+    rows = 96 // len(orders)
     for xy in range(4):
-        part, at = part_of((16 if xy & 2 else 0) | (8 if xy & 1 else 0) | rz, order)
-        outs[part][at] = value[xy * 96 : (xy + 1) * 96].astype(BF)
-
-
-def weigh_kernel(order, l_own, l_got, r_own, r_got, *outs):
-    _, _, _, ten = place()
-    for rz in range(4):
-        z = xor_two(ten, rz)
-        emit(dot_nn(l_own[...], r_own[z]) + dot_nn(l_got[...], r_got[z]), rz, order, outs)
-
-
-def weigh(order, l_own, l_got, r_own, r_got, name):
-    outs = [((n, 96, 768), BF) for n in (8, 4, 2, 1, 1)]
-    return call(
-        partial(weigh_kernel, order), outs, [], [SPEC_V] * 4, (l_own, l_got, r_own, r_got),
-        flops=4 * r_own.shape[1] * 384 * 3072, name=name,
-    )
-
-
-def weigh_attention_kernel(order, n_own, n_got, a_own, a_got, q_own, q_got, m_own, m_got, *outs):
+        for n, order in enumerate(orders):
+            part, at = part_of((16 if xy & 2 else 0) | (8 if xy & 1 else 0) | rz, order)
+            outs[n * 5 + part][at] = value[xy * 96 + n * rows : xy * 96 + (n + 1) * rows].astype(BF)
+
+
+def weigh_high_kernel(row, both, n_in, *refs):
+    left, right = refs[: n_in // 2], refs[n_in // 2 : n_in]
+    out_ref, part, sem = refs[-3:]
+    for z in range(4):
+        first = dot_nn(left[0][...], right[0][z]) + dot_nn(left[1][...], right[1][z])
+        second = dot_nn(left[2][...], right[2][z]) + dot_nn(left[3][...], right[3][z])
+        for at, xy in enumerate(RING):
+            rows = slice(xy * 96, (xy + 1) * 96)
+            if both:
+                part[at * 4 + z, 0:96] = first[rows].astype(BF)
+                part[at * 4 + z, 96:192] = second[rows].astype(BF)
+            else:
+                part[at * 4 + z] = jnp.concatenate([first[rows], second[rows]], axis=1).astype(BF)
+    copy = pltpu.make_async_copy(part, out_ref.at[:, pl.ds(row, part.shape[1])], sem)
+    copy.start()
+    copy.wait()
+
+
+def weigh_high(args, rows, row, both, into=None):
+    more = [] if into is None else [into]
+    return pl.pallas_call(
+        partial(weigh_high_kernel, row, both, len(args)),
+        out_shape=jax.ShapeDtypeStruct((16, rows, 768), BF),
+        in_specs=[SPEC_V] * len(args) + [SPEC_A] * len(more),
+        out_specs=SPEC_A,
+        scratch_shapes=[pltpu.VMEM((16, 192 if both else 96, 768), BF), pltpu.SemaphoreType.DMA],
+        input_output_aliases={len(args): 0} if more else {},
+        compiler_params=pltpu.CompilerParams(vmem_limit_bytes=LIMIT * 1024 * 1024),
+        cost_estimate=pl.CostEstimate(flops=int(5 * COST), bytes_accessed=1000, transcendentals=0),
+        name="weigh_both" if both else "weigh_attention_high",
+    )(*args, *more)
+
+
+def sum_plane(chunks, mesh_shape):
+    dp_size, seq_size, ten_size = mesh_shape
+    groups = [
+        [((h + (xy >> 1)) * seq_size + 2 * (xy & 1) + c) * ten_size + t for xy in RING]
+        for h in range(0, dp_size, 2)
+        for c in range(2)
+        for t in range(ten_size)
+    ]
+    rows = chunks.shape[1]
+    return lax.psum_scatter(
+        chunks.reshape(16 * rows, 768), AXES, scatter_dimension=0, axis_index_groups=groups, tiled=True
+    )
+
+
+def sum_line(chunks):
+    return lax.psum_scatter(chunks, "tensor", scatter_dimension=0, tiled=True).astype(F32)
+
+
+def weigh_attention_kernel(orders, n_own, n_got, a_own, a_got, q_own, q_got, m_own, m_got, *outs):
     _, _, _, ten = place()
     for rz in range(4):
         z = xor_two(ten, rz)
         qkv = dot_nn(n_own[...], q_own[z]) + dot_nn(n_got[...], q_got[z])
         out = dot_nn(a_own[...], m_own[z]) + dot_nn(a_got[...], m_got[z])
-        emit(jnp.concatenate([qkv, out], axis=1), rz, order, outs)
-
-
-def weigh_attention(order, args):
-    outs = [((n, 96, 768), BF) for n in (8, 4, 2, 1, 1)]
+        emit(jnp.concatenate([qkv, out], axis=1), rz, orders, outs)
+
+
+def weigh_attention(orders, args, ties=()):
+    outs = [((n, 96 // len(orders), 768), BF) for _ in orders for n in (8, 4, 2, 1, 1)]
     return call(
-        partial(weigh_attention_kernel, order), outs, [], [SPEC_V] * 8, args,
-        flops=4 * args[4].shape[1] * 384 * 3072, name="weigh_attention",
-    )
-
-
-def spread_kernel(p0, p1, p2, p3, out_ref):
+        partial(weigh_attention_kernel, orders), outs, [], [SPEC_V] * 8, args,
+        micros=3, name="weigh_attention", ties=ties,
+    )
+
+
+def spread_kernel(*refs):
     ten = lax.axis_index("tensor")
-    for rz, p in enumerate((p0, p1, p2, p3)):
-        out_ref[xor_two(ten, rz)] = p[...].astype(out_ref.dtype)
-
-
-def spread(block, dtype, shape):
-    first = swap(block, "z1", shape)
-    second = swap(block, "z2", shape)
-    third = swap(first, "z2", shape)
-    tokens, width = block.shape
-    out = call(
-        spread_kernel, [((4, tokens, width), dtype)], [], [SPEC_V] * 4, (block, first, second, third), name="spread"
-    )[0]
-    return out.reshape(2, 1, 2 * tokens, width)
-
-
-def small_params(vectors, qv_bias, expand_bias, shape):
-    dp_size, seq_size, ten_size = shape
-    if dp_size == 2:
-        pad = lambda v: jnp.pad(v, ((0, 0), (0, 0), (0, 128 - v.shape[2])))
-        rows = jnp.concatenate(
-            [pad(vectors), pad(expand_bias[:, None]), pad(qv_bias.reshape(LAYERS, 1, 48))], axis=1
-        ).reshape(1, LAYERS * 8, 128)
-        for bit in ("z1", "z2", "c", "y", "x"):
-            rows = jnp.concatenate([rows, swap(rows, bit, shape)], axis=0)
-        x, y, c, ten = place()
-        me = ((x * 2 + y) * 2 + c) * 4 + ten
-        order = jnp.bitwise_xor(jnp.arange(32, dtype=jnp.int32), me)
-        pick = (order[:, None] == jnp.arange(32, dtype=jnp.int32)[None, :]).astype(BF)
-        every = jnp.dot(pick, rows.reshape(32, -1), preferred_element_type=F32)
-        every = every.reshape(8, 4, LAYERS, 8, 128)
-        vec = every[:, 0, :, :6, :96].transpose(1, 2, 0, 3).reshape(LAYERS, 6, 768)
-        eb = every[:, :, :, 6, :96].transpose(2, 1, 0, 3).reshape(LAYERS, 4, 1, 768)
-        qv = every[:, :, :, 7, :48].reshape(8, 4, LAYERS, 2, 24).transpose(2, 3, 1, 0, 4).reshape(LAYERS, 2, 4, 192)
-    else:
-        vec = lax.all_gather(vectors, ("dp", "seq"), axis=2, tiled=True).astype(F32)
-        eb = lax.all_gather(expand_bias, ("tensor", "dp", "seq"), axis=1, tiled=True)
-        eb = eb.astype(F32).reshape(LAYERS, 4, 1, 768)
-        qv = lax.all_gather(qv_bias, ("tensor", "dp", "seq"), axis=2, tiled=True)
-        qv = qv.astype(F32).reshape(LAYERS, 2, 4, 192)
+    for n in range(2):
+        for at, rz in enumerate((0, 2, 1, 3)):
+            refs[8 + n][xor_two(ten, rz)] = refs[n * 4 + at][...].astype(refs[8 + n].dtype)
+
+
+def spread(left, left_type, right, right_type):
+    tokens, width = left[0].shape
+    outs = [((4, tokens, width), left_type), ((4, tokens, width), right_type)]
+    done = call(spread_kernel, outs, [], [SPEC_V] * 8, (*left, *right), name="spread")
+    return [d.reshape(2, 1, 2 * tokens, width) for d in done]
+
+
+def small_params(every):
+    vec = every[:, 0, :, :6].transpose(1, 2, 0, 3).reshape(LAYERS, 6, 768)
+    eb = every[:, :, :, 6].transpose(2, 1, 0, 3).reshape(LAYERS, 4, 1, 768)
+    qv = every[:, :, :, 7, :48].reshape(8, 4, LAYERS, 2, 24).transpose(2, 3, 1, 0, 4).reshape(LAYERS, 2, 4, 192)
     qvb = jnp.concatenate([jnp.zeros_like(qv[:, 0]), qv[:, 1], qv[:, 0]], axis=-1)[:, :, None, :]
     return jnp.pad(vec, ((0, 0), (0, 2), (0, 0))), qvb, eb
+
+
+def small_everywhere(chunks, order):
+    x, y, c, ten = place()
+    me = ((x * 2 + y) * 2 + c) * 4 + ten
+    rels = []
+    for a in range(4):
+        for j in range(8):
+            rel = sum(BITS[order[k]] for k in range(3) if j & (1 << k))
+            rels.append(rel | (BITS[order[3]] if a & 1 else 0) | (BITS["c"] if a & 2 else 0))
+    device = jnp.bitwise_xor(jnp.asarray(rels, jnp.int32), me)
+    pick = (jnp.arange(32, dtype=jnp.int32)[:, None] == device[None, :]).astype(BF)
+    rows = jnp.concatenate([chunk[:, 96:98].reshape(8, -1) for chunk in chunks], axis=0)
+    every = jnp.dot(pick, rows, preferred_element_type=F32)
+    return every.reshape(8, 4, LAYERS, 8, 96)
 
 
 def body(shape, features, upstream, key_mask, vectors, proj_qkv, qv_bias, proj_out, expand_weight, expand_bias, shrink_weight):
@@ -601,13 +707,39 @@
             lax.dynamic_slice_in_dim(lax.all_gather(w, ("dp", "seq"), axis=1, tiled=True), start, 96, axis=1)
             for w in (wa, we, ws)
         )
-    vec, qvb, eb = small_params(vectors, qv_bias, expand_bias, shape)
-    a_w = [
-        [g for n, order in enumerate(ORDERS_A) for g in gather_block(wa[0, n * 32 : (n + 1) * 32], order, shape)],
-        gather_block(wa[1], ORDER_A, shape),
+    if dp_size == 2:
+        small = jnp.concatenate(
+            [
+                vectors.reshape(LAYERS, -1),
+                expand_bias,
+                qv_bias.reshape(LAYERS, -1),
+                jnp.zeros((LAYERS, 48), BF),
+            ],
+            axis=1,
+        )
+    else:
+        small = jnp.zeros((LAYERS, 768), BF)
+    first = jnp.concatenate([wa[0], small, jnp.zeros((6, 768), BF)], axis=0)
+    whole = [
+        [(d * seq_size + s) * ten_size + t for d in range(h, h + 2) for s in range(seq_size) for t in range(ten_size)]
+        for h in range(0, dp_size, 2)
     ]
-    e_w = [gather_block(we[d], ORDER_E, shape) for d in range(LAYERS)]
-    s_w = [gather_block(ws[d], ORDER_S, shape) for d in range(LAYERS)]
+    low_layer = Gatherer((first, we[0], ws[0]), (ORDER_A, ORDER_E, ORDER_S), shape)
+    for _ in range(3):
+        low_layer.go()
+    (block,) = low_layer.before(jnp.concatenate([wa[1], we[1], ws[1]], axis=0))
+    high = lax.all_gather(block, AXES, axis_index_groups=None if dp_size == 2 else whole)
+    low_layer.go()
+    a_w, e_w, s_w = ((w, [high]) for w in low_layer.core())
+    if dp_size == 2:
+        vec, qvb, eb = small_params(small_everywhere(a_w[0], ORDER_A))
+    else:
+        vec = lax.all_gather(vectors, ("dp", "seq"), axis=2, tiled=True).reshape(LAYERS, 6, 8, 96)
+        eb = lax.all_gather(expand_bias, ("tensor", "dp", "seq"), axis=1, tiled=True).reshape(LAYERS, 1, 4, 8, 96)
+        qv = lax.all_gather(qv_bias, ("tensor", "dp", "seq"), axis=2, tiled=True).reshape(LAYERS, 2, 4, 8, 24)
+        vec = jnp.broadcast_to(vec[:, :, None], (LAYERS, 6, 4, 8, 96))
+        qv = jnp.pad(qv.transpose(0, 2, 3, 1, 4).reshape(LAYERS, 1, 4, 8, 48), ((0, 0),) * 4 + ((0, 48),))
+        vec, qvb, eb = small_params(jnp.concatenate([vec, eb, qv], axis=1).transpose(3, 2, 0, 1, 4).astype(F32))
 
     state = x0
     kept = []
@@ -620,52 +752,78 @@
         x_in = state
         state, after, mixed_all, m_own, m_other, active, slope = mlp(mixed, x_in, vec[d], eb[d], a_w[d], e_w[d], s_w[d])
         kept.append((x_in, n_own, n_other, kv, q, mixed_wide, lse, after, mixed_all, m_own, m_other, active, slope))
-    encoded = spread(state.astype(BF), BF, shape)
+    encoded = [state.astype(BF)]
 
     grad = dy0
-    g_a, g_e, g_s = [None] * LAYERS, [None] * LAYERS, [None] * LAYERS
-    small = [None] * LAYERS
-    for d in reversed(range(LAYERS)):
+    for d in (1, 0):
         x_in, n_own, n_other, kv, q, mixed_wide, lse, after, mixed_all, m_own, m_other, active, slope = kept[d]
-        *d_mixed, d_after, d_hid, z_own, z_other, da_own, da_other, sums_two, ebs = mlp_back(
+        d0, d1, d2, d3, d_after, d_hid, da_own, da_other, sums_two, ebs, z_own, z_other = mlp_back(
             grad, after, vec[d], slope, a_w[d], e_w[d], s_w[d]
         )
-        d_mixed = [d_mixed[0]] + [swap_group(d_mixed[p], p, shape) for p in (1, 2, 3)]
-        order_e, order_s = ORDER_E[::-1], ORDER_S[::-1]
-        parts = weigh(order_e, m_own, swap(m_other, "c", shape), d_hid, swap(d_hid, "c", shape), "weigh_expand")
-        g_e[d] = scatter_sum(parts, order_e, shape)
-        parts = weigh(order_s, z_own, swap(z_other, "c", shape), active, swap(active, "c", shape), "weigh_shrink")
-        g_s[d] = scatter_sum(parts, order_s, shape)
-        dq, own, other = attend_back(count, d_mixed, kv, q, mixed_wide, lse)
+        d_mixed = [d0] + [swap_group(v, p + 1, shape) for p, v in enumerate((d1, d2, d3))]
+        m_got, hid_got, z_got, active_got = (swap(v, "c", shape) for v in (m_other, d_hid, z_other, active))
+        given = (m_own, m_got, z_own, z_got, d_hid, hid_got, active, active_got)
+        if d:
+            chunks = weigh_high(given, 192, 0, True)
+            high_sum = sum_plane(chunks, shape)
+            encoded[0], *d_mixed = fence(encoded[0], *d_mixed)
+            encoded.append(swap(encoded[0], "z2", shape))
+        else:
+            chunks = weigh_high(given, 288, 0, True, chunks)
+            low_sum = sum_line(sum_plane(chunks, shape))
+            encoded[1], *d_mixed = fence(encoded[1], *d_mixed)
+            encoded.append(swap(encoded[1], "z1", shape))
+        dq, own, other = attend_back(count, d_mixed, kv, q, mixed_wide, lse, [chunks])
+        if d:
+            *encoded, other = fence(*encoded, other)
+        else:
+            *encoded, high_sum, other = fence(*encoded, high_sum, other)
         d_kv = (own.astype(F32) + swap(other, "c", shape).astype(F32)).astype(BF)
         back = [jnp.concatenate([d_kv[p], dq[p * tokens : (p + 1) * tokens]], axis=1) for p in range(4)]
         back = [back[0]] + [swap_group(back[p], p, shape) for p in (1, 2, 3)]
-        grad, d_qkv, sums_one, qvs = project_back(back, d_after, x_in, vec[d], a_w[d])
-        order_a = ORDER_A[::-1]
-        parts = weigh_attention(
-            order_a,
-            (
-                n_own,
-                swap(n_other, "c", shape),
-                da_own,
-                swap(da_other, "c", shape),
-                d_qkv,
-                swap(d_qkv, "c", shape),
-                mixed_all,
-                swap(mixed_all, "c", shape),
-            ),
+        if d:
+            encoded[0], *back = fence(encoded[0], *back)
+            got_z = swap(encoded[0], "z1", shape)
+        grad, d_qkv, total = project_back(back, d_after, x_in, vec[d], sums_two, ebs, [] if d else [high_total], a_w[d])
+        given = (
+            n_own,
+            swap(n_other, "c", shape),
+            da_own,
+            swap(da_other, "c", shape),
+            d_qkv,
+            swap(d_qkv, "c", shape),
+            mixed_all,
+            swap(mixed_all, "c", shape),
         )
-        g_a[d] = scatter_sum(parts, order_a, shape)
-        total = jnp.concatenate(
-            [sums_one[:2], sums_two[:4], ebs.reshape(4, 768), jnp.pad(qvs.reshape(4, 576), ((0, 2), (0, 192)))], axis=0
-        )
+        if d:
+            high_total = total
+            chunks = weigh_high(given, 288, 192, False)
+            chunks, got_z, high_sum, grad = fence(chunks, got_z, high_sum, grad)
+            high_sum = sum_line(high_sum)
+            encoded.append(got_z)
+    if dp_size == 2:
+        total = total + swap(total, "c", shape)
+    else:
+        total = lax.psum(total, AXES)
+    parts = weigh_attention(SUM_A, given)
+    sums_a = [Reducer(parts[n * 5 : n * 5 + 5], order, shape) for n, order in enumerate(SUM_A)]
+    features_grad = [grad.astype(BF)]
+    last = Together(sums_a)
+    total, features_grad[0] = last.wait(total, features_grad[0])
+    for step, bit in enumerate(("x", "y", "z1", "z2")):
+        got = [swap(total, bit, shape)] if dp_size == 2 else []
+        if step == 0:
+            got.append(swap(features_grad[0], "z2", shape))
+        elif step == 1:
+            got += [swap(v, "z1", shape) for v in features_grad]
+        got = list(last.go(*got))
         if dp_size == 2:
-            for bit in ("c", "x", "y", "z1", "z2"):
-                total = total + swap(total, bit, shape)
-        else:
-            total = lax.psum(total, AXES)
-        small[d] = total
-    grad_features = spread(grad.astype(BF), F32, shape)
+            total = total + got.pop(0)
+        features_grad += got
+    small = total.reshape(LAYERS, 16, 768)
+    encoded, grad_features = spread(encoded, BF, features_grad, F32)
+    g_a = [jnp.concatenate([r.finish() for r in sums_a], axis=0), low_sum[192:]]
+    g_e, g_s = ([low_sum[:96], high_sum[:96]], [low_sum[96:192], high_sum[96:]])
 
     if dp_size != 2:
         start = (lax.rem(dp, 2) * 4 + seq) * 96
@@ -676,7 +834,7 @@
 
         g_a, g_e, g_s = ([down(g) for g in gs] for gs in (g_a, g_e, g_s))
     ga, ge, gs = jnp.stack(g_a), jnp.stack(g_e), jnp.stack(g_s)
-    g_small = jnp.stack(small)
+    g_small = small
     mine = dp * seq_size + seq
     grad_vectors = lax.dynamic_slice_in_dim(g_small[:, :6], mine * width, width, axis=2)
     eb_width, qv_width = expand_bias.shape[1], qv_bias.shape[2]

time: 628 us -> 537 us (0.86)
  starting transfers between devices: 129 us -> 73.6 us
  waiting for transfers between devices: 284 us -> 249 us
  other arithmetic: 35.5 us -> 22.4 us
  between operations: 3.3 us -> 15.7 us
  Pallas kernels: 123 us -> 114 us
    ppermute x119 -> x63, waiting for transfers between devices: 218 us -> 153 us  [swap(): return lax.ppermute(value, AXES, pairs)]
    ppermute x119 -> x63, starting transfers between devices: 99.7 us -> 46.2 us  [swap(): return lax.ppermute(value, AXES, pairs)]
    ppermute x24, waiting for transfers between devices: 66.5 us -> 87.8 us  [swap_group(): return lax.ppermute(value, AXES, pairs)]
    pallas_call x20 -> x17, Pallas kernels: 123 us -> 114 us  [the longest x14 99.7 us: call(): pl.pallas_call(lambda *refs: kernel(*refs[len(ties):]), out_shape=[jax.Sh...]
    unnamed x305 -> x262, local copies, waits for them, and re-layouts: 36.1 us -> 44.3 us
    concatenate x29 -> x10, other arithmetic: 13.7 us -> 6.61 us  [the longest x9 5.82 us: go(): jnp.concatenate([c, g], axis=0)]
    reduce_scatter x0 -> x4, waiting for transfers between devices: none -> 7.1 us  [the longest x2 7.08 us: sum_plane(): lax.psum_scatter(chunks.reshape(16 * rows, 768), AXES, scatter_dimension=...]
    convert_element_type x38 -> x10, other arithmetic: 14.9 us -> 10.3 us  [the longest x6 7.38 us: send(): self.parts[self.step].astype(BF)]
  transfers between devices with their start and end apart: 143 -> 92, of which waited for: 64 -> 51; matrix products, arithmetic and copies ran while one was open for 8% -> 5% of each run, Pallas kernels for 10% -> 14%
where the time goes in v2:
time: 537 us; the launch traced here: 526 us
  waiting for transfers between devices  249 us (46%)
  Pallas kernels  114 us (21%)
  starting transfers between devices  73.6 us (14%)
  local copies, waits for them, and re-layouts  51 us (9%)
  other arithmetic  22.4 us (4%)
  between operations  15.7 us (3%)
    ppermute x63, waiting for transfers between devices, swap(): return lax.ppermute(value, AXES, pairs)  153 us
    pallas_call x14, Pallas kernels, call(): pl.pallas_call(lambda *refs: kernel(*refs[len(ties):]), out_shape=[jax.Sh...  99.7 us
    ppermute x24, waiting for transfers between devices, swap_group(): return lax.ppermute(value, AXES, pairs)  87.8 us
    ppermute x63, starting transfers between devices, swap(): return lax.ppermute(value, AXES, pairs)  46.2 us
    unnamed x262, local copies, waits for them, and re-layouts  44.3 us
    ppermute x24, starting transfers between devices, swap_group(): return lax.ppermute(value, AXES, pairs)  27.1 us
    pallas_call x3, Pallas kernels, weigh_high(): pl.pallas_call(partial(weigh_high_kernel, row, both, len(args)), out_shap...  14.4 us
  transfers between devices with their start and end apart: 92, of which 51 were waited for; matrix products, arithmetic and copies ran while one was open for 5% of the time, Pallas kernels for 14%

profile of v2, /device:TPU:0, one launch (start us, length us, event | category | flops | bytes accessed | tf_op | source)
XLA Modules:
  0.0 526.4 jit_solution(7443212739475751559)
XLA Ops:
  8.6 4.1 collective-permute-start.1
  16.4 10.7 %collective-permute-done.1 = bf16[1,96,768]{2,1,0:T(8,128)(2,1)S(1)} collective-permute-done((bf16[1,96,768]{2,1,0:T(8,128)(2,1)S(1)}, bf16[1,96,768]{2,1,0:T(8,128)(2,1)S(1)}, u32[]{:S(2)}, u32[]{:S(2)}) %collective-permute-start.1) | collective-permute-done | bytes 147488 | tf_op jit(solution)/shard_map/ppermute | solution.py:50
  36.7 4.5 collective-permute-done.5
  47.3 10.8 %collective-permute-done.8 = bf16[4,96,768]{2,1,0:T(8,128)(2,1)} collective-permute-done((bf16[4,96,768]{2,1,0:T(8,128)(2,1)S(1)}, bf16[4,96,768]{2,1,0:T(8,128)(2,1)}, u32[]{:S(2)}, u32[]{:S(2)}) %collective-permute-start.8) | collective-permute-done | bytes 589856 | tf_op jit(solution)/shard_map/ppermute | solution.py:50
  66.1 26.7 %collective-permute-done.10.refs_12_.refs_9_ = bf16[8,96,768]{2,1,0:T(8,128)(2,1)} collective-permute-done((bf16[8,96,768]{2,1,0:T(8,128)(2,1)}, bf16[8,96,768]{2,1,0:T(8,128)(2,1)}, u32[]{:S(2)}, u32[]{:S(2)}) %collective-permute-start.10) | collective-permute-done | bytes 1179680 | tf_op jit(solution)/shard_map/ppermute | solution.py:50
  93.1 7.9 %collective-permute-done.9.refs_4_.refs_8_.refs_5_.refs_11_ = bf16[8,104,768]{2,1,0:T(8,128)(2,1)} collective-permute-done((bf16[8,104,768]{2,1,0:T(8,128)(2,1)S(1)}, bf16[8,104,768]{2,1,0:T(8,128)(2,1)}, u32[]{:S(2)}, u32[]{:S(2)}) %collective-permute-start.9) | collective-permute-done | bytes 1277984 | tf_op jit(solution)/shard_map/ppermute | solution.py:50
  111.6 14.7 %collective-permute-done.14.refs_2_ = bf16[192,576]{1,0:T(8,128)(2,1)S(1)} collective-permute-done((bf16[192,576]{1,0:T(8,128)(2,1)S(1)}, bf16[192,576]{1,0:T(8,128)(2,1)S(1)}, u32[]{:S(2)}, u32[]{:S(2)}) %collective-permute-start.14) | collective-permute-done | bytes 221216 | tf_op jit(solution)/shard_map/ppermute | solution.py:62
  126.6 9.0 %collective-permute-done.16.refs_4_ = bf16[192,576]{1,0:T(8,128)(2,1)S(1)} collective-permute-done((bf16[192,576]{1,0:T(8,128)(2,1)S(1)}, bf16[192,576]{1,0:T(8,128)(2,1)S(1)}, u32[]{:S(2)}, u32[]{:S(2)}) %collective-permute-start.16) | collective-permute-done | bytes 221216 | tf_op jit(solution)/shard_map/ppermute | solution.py:62
  140.0 7.8 %attend.2 = (bf16[192,192]{1,0:T(8,128)(2,1)S(1)}, bf16[192,192]{1,0:T(8,128)(2,1)}, bf16[192,192]{1,0:T(8,128)(2,1)}, bf16[192,192]{1,0:T(8,128)(2,1)S(1)}, bf1...) custom-call(s32[1]{0:T(128)} %bitcast.refs_0_.refs_1_, ...), custom_call_target="tpu_custom_call" | custom-call | flops 2100000000 | bytes 1000 | tf_op jit(solution)/shard_map/attend/pallas_call | solution.py:246
  156.5 5.8 %collective-permute-done.21.refs_1_ = bf16[192,192]{1,0:T(8,128)(2,1)S(1)} collective-permute-done((bf16[192,192]{1,0:T(8,128)(2,1)}, bf16[192,192]{1,0:T(8,128)(2,1)S(1)}, u32[]{:S(2)}, u32[]{:S(2)}) %collective-permute-start.21) | collective-permute-done | bytes 73760 | tf_op jit(solution)/shard_map/ppermute | solution.py:62
  167.7 10.3 %mlp.2 = (f32[192,768]{1,0:T(8,128)S(1)}, f32[192,768]{1,0:T(8,128)S(1)}, bf16[4,192,192]{2,1,0:T(8,128)(2,1)S(1)}, bf16[384,192]{1,0:T(8,128)(2,1)S(1)}, bf16[3...) custom-call(bf16[192,192]{1,0:T(8,128)(2,1)S(1)} %get-tuple-element.179.refs_0_, ...), custom_call_target="tpu_custom_call" | custom-call | flops 3600000000 | bytes 1000 | tf_op jit(solution)/shard_map/mlp/pallas_call | solution.py:246
  190.6 5.2 collective-permute-done.28.refs_2_
  196.5 4.7 collective-permute-done.30.refs_4_
  202.6 7.9 %attend.3 = (bf16[192,192]{1,0:T(8,128)(2,1)S(1)}, bf16[192,192]{1,0:T(8,128)(2,1)}, bf16[192,192]{1,0:T(8,128)(2,1)}, bf16[192,192]{1,0:T(8,128)(2,1)}, bf16[15...) custom-call(s32[1]{0:T(128)} %bitcast.refs_0_.refs_1_, ...), custom_call_target="tpu_custom_call" | custom-call | flops 2100000000 | bytes 1000 | tf_op jit(solution)/shard_map/attend/pallas_call | solution.py:246
  225.3 11.5 %mlp.3 = (f32[192,768]{1,0:T(8,128)S(1)}, f32[192,768]{1,0:T(8,128)S(1)}, bf16[4,192,192]{2,1,0:T(8,128)(2,1)S(1)}, bf16[384,192]{1,0:T(8,128)(2,1)S(1)}, bf16[3...) custom-call(bf16[192,192]{1,0:T(8,128)(2,1)S(1)} %copy-done.44, ...), custom_call_target="tpu_custom_call" | custom-call | flops 3600000000 | bytes 1000 | tf_op jit(solution)/shard_map/mlp/pallas_call | solution.py:246
  238.3 10.1 %mlp_back.2 = (bf16[192,192]{1,0:T(8,128)(2,1)S(1)}, bf16[192,192]{1,0:T(8,128)(2,1)S(1)}, bf16[192,192]{1,0:T(8,128)(2,1)S(1)}, bf16[192,192]{1,0:T(8,128)(2,1)...) custom-call(bf16[192,768]{1,0:T(8,128)(2,1)S(1)} %dynamic-slice_bitc, ...), custom_call_target="tpu_custom_call" | custom-call | flops 3300000000 | bytes 1000 | tf_op jit(solution)/shard_map/mlp_back/pallas_call | solution.py:246
  257.6 5.0 weigh_both.2.refs_0_
  278.0 10.4 %attend_back.2 = (bf16[768,192]{1,0:T(8,128)(2,1)S(1)}, bf16[4,192,384]{2,1,0:T(8,128)(2,1)S(1)}, bf16[4,192,384]{2,1,0:T(8,128)(2,1)S(1)}) custom-call(bf16[16,192,768]{2,1,0:T(8,128)(2,1)} %weigh_both.2.refs_0_, s32[1]{0:T(128)} %bitcast.refs_0_.refs_1_, bf16[192,192]{1,0:T(8,128)(2,1)S(1)} %copy-done.75, ...), custom_call_target="tpu_custom_call" | custom-call | flops 3300000000 | bytes 1000 | tf_op jit(solution)/shard_map/attend_back/pallas_call | solution.py:246
  294.5 6.0 %collective-permute-done.49.refs_3_ = bf16[192,576]{1,0:T(8,128)(2,1)S(1)} collective-permute-done((bf16[192,576]{1,0:T(8,128)(2,1)S(1)}, bf16[192,576]{1,0:T(8,128)(2,1)S(1)}, u32[]{:S(2)}, u32[]{:S(2)}) %collective-permute-start.49) | collective-permute-done | bytes 221216 | tf_op jit(solution)/shard_map/ppermute | solution.py:62
  300.5 9.9 %collective-permute-done.48.refs_2_ = bf16[192,576]{1,0:T(8,128)(2,1)S(1)} collective-permute-done((bf16[192,576]{1,0:T(8,128)(2,1)S(1)}, bf16[192,576]{1,0:T(8,128)(2,1)S(1)}, u32[]{:S(2)}, u32[]{:S(2)}) %collective-permute-start.48) | collective-permute-done | bytes 221216 | tf_op jit(solution)/shard_map/ppermute | solution.py:62
  310.6 4.7 project_back.2
  328.1 10.3 %mlp_back.3 = (bf16[192,192]{1,0:T(8,128)(2,1)S(1)}, bf16[192,192]{1,0:T(8,128)(2,1)S(1)}, bf16[192,192]{1,0:T(8,128)(2,1)S(1)}, bf16[192,192]{1,0:T(8,128)(2,1)...) custom-call(f32[192,768]{1,0:T(8,128)S(1)} %copy-done.15, ...), custom_call_target="tpu_custom_call" | custom-call | flops 3300000000 | bytes 1000 | tf_op jit(solution)/shard_map/mlp_back/pallas_call | solution.py:246
  345.4 6.1 %weigh_both.3.refs_0_ = bf16[16,288,768]{2,1,0:T(8,128)(2,1)} custom-call(bf16[384,192]{1,0:T(8,128)(2,1)S(1)} %copy-done.30, bf16[384,192]{1,0:T(8,128)(2,1)S(1)} %collective-permute-done.59.refs_1_, bf16[384,192]{1,0:T(8,128)(2,1)S(1)} %get-tuple-element.250.refs_2_, ...), custom_call_target="tpu_custom_call", output_to_operand_aliasing={{}: (8, {})} | custom-call | flops 1500000000 | bytes 1000 | tf_op jit(solution)/shard_map/weigh_both/pallas_call | solution.py:598
  366.7 10.4 %attend_back.3 = (bf16[768,192]{1,0:T(8,128)(2,1)S(1)}, bf16[4,192,384]{2,1,0:T(8,128)(2,1)S(1)}, bf16[4,192,384]{2,1,0:T(8,128)(2,1)S(1)}) custom-call(bf16[16,288,768]{2,1,0:T(8,128)(2,1)} %weigh_both.3.refs_0_, s32[1]{0:T(128)} %bitcast.refs_0_.refs_1_, bf16[192,192]{1,0:T(8,128)(2,1)S(1)} %copy-done.73, ...), custom_call_target="tpu_custom_call" | custom-call | flops 3300000000 | bytes 1000 | tf_op jit(solution)/shard_map/attend_back/pallas_call | solution.py:246
  386.1 6.0 %collective-permute-done.68.refs_3_ = bf16[192,576]{1,0:T(8,128)(2,1)S(1)} collective-permute-done((bf16[192,576]{1,0:T(8,128)(2,1)S(1)}, bf16[192,576]{1,0:T(8,128)(2,1)S(1)}, u32[]{:S(2)}, u32[]{:S(2)}) %collective-permute-start.68) | collective-permute-done | bytes 221216 | tf_op jit(solution)/shard_map/ppermute | solution.py:62
  392.1 9.7 %collective-permute-done.67.refs_2_ = bf16[192,576]{1,0:T(8,128)(2,1)S(1)} collective-permute-done((bf16[192,576]{1,0:T(8,128)(2,1)S(1)}, bf16[192,576]{1,0:T(8,128)(2,1)S(1)}, u32[]{:S(2)}, u32[]{:S(2)}) %collective-permute-start.67) | collective-permute-done | bytes 221216 | tf_op jit(solution)/shard_map/ppermute | solution.py:62
  401.9 4.1 project_back.3
  411.9 6.0 %collective-permute-start.72 = (bf16[8,48,768]{2,1,0:T(8,128)(2,1)S(1)}, bf16[8,48,768]{2,1,0:T(8,128)(2,1)S(1)}, u32[]{:S(2)}, u32[]{:S(2)}) collective-permute-start(bf16[8,48,768]{2,1,0:T(8,128)(2,1)S(1)} %get-tuple-element.286), channel_id=1, source_target_pairs={{0,16},{1,17},{2,18},{3,19},{4,20},{5,21},{6,22},{7,23},{8,24},{9,... | collective-permute-start | bytes 1769480 | tf_op jit(solution)/shard_map/ppermute | solution.py:50
  419.7 23.4 %collective-permute-done.74 = f32[32,768]{1,0:T(8,128)S(1)} collective-permute-done((f32[32,768]{1,0:T(8,128)S(1)}, f32[32,768]{1,0:T(8,128)S(1)}, u32[]{:S(2)}, u32[]{:S(2)}) %collective-permute-start.74) | collective-permute-done | bytes 98336 | tf_op jit(solution)/shard_map/ppermute | solution.py:50
  447.6 5.7 %reduce-scatter.9.cloned.1.call-done = bf16[1152,768]{1,0:T(8,128)(2,1)} async-done(((bf16[4608,768]{1,0:T(8,128)(2,1)}), bf16[1152,768]{1,0:T(8,128)(2,1)}) %reduce-scatter.9.cloned.1.call-update) | async-done | bytes 1769488 | tf_op jit(solution)/shard_map/reduce_scatter | solution.py:620
  458.2 7.3 %collective-permute-done.78 = f32[32,768]{1,0:T(8,128)S(1)} collective-permute-done((f32[32,768]{1,0:T(8,128)S(1)}, f32[32,768]{1,0:T(8,128)S(1)}, u32[]{:S(2)}, u32[]{:S(2)}) %collective-permute-start.78) | collective-permute-done | bytes 98336 | tf_op jit(solution)/shard_map/ppermute | solution.py:50
  473.2 22.0 %collective-permute-done.83 = f32[32,768]{1,0:T(8,128)S(1)} collective-permute-done((f32[32,768]{1,0:T(8,128)S(1)}, f32[32,768]{1,0:T(8,128)S(1)}, u32[]{:S(2)}, u32[]{:S(2)}) %collective-permute-start.83) | collective-permute-done | bytes 98336 | tf_op jit(solution)/shard_map/ppermute | solution.py:50
  (534 shorter events, 211.8 us)
Async XLA Ops:
  7.2 175.1 %all-gather.3.cloned.1.call-start = ((), (), s32[]{:S(2)}) async-start(), calls=%async_computation.8 | async-start | bytes 14598144 | tf_op jit(solution)/shard_map/all_gather | solution.py:731
  8.6 18.5 %collective-permute-start.1 = (bf16[1,96,768]{2,1,0:T(8,128)(2,1)S(1)}, bf16[1,96,768]{2,1,0:T(8,128)(2,1)S(1)}, u32[]{:S(2)}, u32[]{:S(2)}) collective-permute-start(bf16[1,96,768]{2,1,0:T(8,128)(2,1)S(1)} %get-tuple-element.379), channel_id=1, source_target_pairs={{0,2},{1,3},{2,0},{3,1},{4,6},{5,7},{6,4},{7,5},{8,10},{9,11},{10,... | collective-permute-start | bytes 442376 | tf_op jit(solution)/shard_map/ppermute | solution.py:50
  12.7 17.6 %collective-permute-start.2 = (bf16[1,96,768]{2,1,0:T(8,128)(2,1)S(1)}, bf16[1,96,768]{2,1,0:T(8,128)(2,1)S(1)}, u32[]{:S(2)}, u32[]{:S(2)}) collective-permute-start(bf16[1,96,768]{2,1,0:T(8,128)(2,1)S(1)} %get-tuple-element.363), channel_id=1, source_target_pairs={{0,2},{1,3},{2,0},{3,1},{4,6},{5,7},{6,4},{7,5},{8,10},{9,11},{10,... | collective-permute-start | bytes 442376 | tf_op jit(solution)/shard_map/ppermute | solution.py:50
  13.5 19.4 %collective-permute-start = (bf16[1,104,768]{2,1,0:T(8,128)(2,1)S(1)}, bf16[1,104,768]{2,1,0:T(8,128)(2,1)S(1)}, u32[]{:S(2)}, u32[]{:S(2)}) collective-permute-start(bf16[1,104,768]{2,1,0:T(8,128)(2,1)S(1)} %maximum_bitcast_fusion.2), channel_id=1, source_target_pairs={{0,2},{1,3},{2,0},{3,1},{4,6},{5,7},{6,4},{7,5},{8,10},{9,11},{10,... | collective-permute-start | bytes 479240 | tf_op jit(solution)/shard_map/ppermute | solution.py:50
  63.7 263.2 %reduce-scatter.5.cloned.1.call-start = ((), (), s32[]{:S(2)}) async-start(), calls=%async_computation.4 | async-start | bytes 5898240 | tf_op jit(solution)/shard_map/reduce_scatter | solution.py:620
  63.7 37.2 %collective-permute-start.9 = (bf16[8,104,768]{2,1,0:T(8,128)(2,1)S(1)}, bf16[8,104,768]{2,1,0:T(8,128)(2,1)}, u32[]{:S(2)}, u32[]{:S(2)}) collective-permute-start(bf16[8,104,768]{2,1,0:T(8,128)(2,1)S(1)} %pad_maximum_fusion.refs_3_.refs_7_.refs_4_.refs_10_), channel_id=1, source_target_pairs={{0,1},{1,0},{2,3},{3,2},{4,5},{5,4},{6,7},{7,6},{8,9},{9,8},{10,11... | collective-permute-start | bytes 3833864 | tf_op jit(solution)/shard_map/ppermute | solution.py:50
  64.1 28.8 %collective-permute-start.10 = (bf16[8,96,768]{2,1,0:T(8,128)(2,1)}, bf16[8,96,768]{2,1,0:T(8,128)(2,1)}, u32[]{:S(2)}, u32[]{:S(2)}) collective-permute-start(bf16[8,96,768]{2,1,0:T(8,128)(2,1)} %pad_maximum_fusion.1.refs_11_.refs_8_), channel_id=1, source_target_pairs={{0,8},{1,9},{2,10},{3,11},{4,12},{5,13},{6,14},{7,15},{8,0},{9,1},... | collective-permute-start | bytes 3538952 | tf_op jit(solution)/shard_map/ppermute | solution.py:50
  64.6 28.5 %collective-permute-start.11 = (bf16[8,96,768]{2,1,0:T(8,128)(2,1)}, bf16[8,96,768]{2,1,0:T(8,128)(2,1)}, u32[]{:S(2)}, u32[]{:S(2)}) collective-permute-start(bf16[8,96,768]{2,1,0:T(8,128)(2,1)} %pad_maximum_fusion.2.refs_15_.refs_12_), channel_id=1, source_target_pairs={{0,16},{1,17},{2,18},{3,19},{4,20},{5,21},{6,22},{7,23},{8,24},{9,... | collective-permute-start | bytes 3538952 | tf_op jit(solution)/shard_map/ppermute | solution.py:50
  66.1 36.6 %collective-permute-start.12 = (bf16[8,104,768]{2,1,0:T(8,128)(2,1)S(1)}, bf16[8,104,768]{2,1,0:T(8,128)(2,1)}, u32[]{:S(2)}, u32[]{:S(2)}) collective-permute-start(bf16[8,104,768]{2,1,0:T(8,128)(2,1)S(1)} %pad_maximum_fusion.refs_3_.refs_7_.refs_4_.refs_10_), channel_id=1, source_target_pairs={{0,4},{1,5},{2,6},{3,7},{4,0},{5,1},{6,2},{7,3},{8,12},{9,13},{10,... | collective-permute-start | bytes 3833864 | tf_op jit(solution)/shard_map/ppermute | solution.py:50
  101.1 51.2 %collective-permute-start.24 = (bf16[8,96,768]{2,1,0:T(8,128)(2,1)}, bf16[8,96,768]{2,1,0:T(8,128)(2,1)}, u32[]{:S(2)}, u32[]{:S(2)}) collective-permute-start(bf16[8,96,768]{2,1,0:T(8,128)(2,1)} %pad_maximum_fusion.1.refs_11_.refs_8_), channel_id=1, source_target_pairs={{0,4},{1,5},{2,6},{3,7},{4,0},{5,1},{6,2},{7,3},{8,12},{9,13},{10,... | collective-permute-start | bytes 3538952 | tf_op jit(solution)/shard_map/ppermute | solution.py:50
  101.6 52.6 %collective-permute-start.26 = (bf16[8,96,768]{2,1,0:T(8,128)(2,1)}, bf16[8,96,768]{2,1,0:T(8,128)(2,1)}, u32[]{:S(2)}, u32[]{:S(2)}) collective-permute-start(bf16[8,96,768]{2,1,0:T(8,128)(2,1)} %pad_maximum_fusion.2.refs_15_.refs_12_), channel_id=1, source_target_pairs={{0,4},{1,5},{2,6},{3,7},{4,0},{5,1},{6,2},{7,3},{8,12},{9,13},{10,... | collective-permute-start | bytes 3538952 | tf_op jit(solution)/shard_map/ppermute | solution.py:50
  109.6 16.7 %collective-permute-start.14 = (bf16[192,576]{1,0:T(8,128)(2,1)S(1)}, bf16[192,576]{1,0:T(8,128)(2,1)S(1)}, u32[]{:S(2)}, u32[]{:S(2)}) collective-permute-start(bf16[192,576]{1,0:T(8,128)(2,1)S(1)} %get-tuple-element.176), channel_id=1, source_target_pairs={{0,1},{1,0},{2,3},{3,2},{4,5},{5,4},{6,7},{7,6},{8,9},{9,8},{10,11... | collective-permute-start | bytes 663560 | tf_op jit(solution)/shard_map/ppermute | solution.py:62
  111.4 45.1 %collective-permute-start.25 = (bf16[8,96,768]{2,1,0:T(8,128)(2,1)}, bf16[8,96,768]{2,1,0:T(8,128)(2,1)}, u32[]{:S(2)}, u32[]{:S(2)}) collective-permute-start(bf16[8,96,768]{2,1,0:T(8,128)(2,1)} %collective-permute-done.10.refs_12_.refs_9_), channel_id=1, source_target_pairs={{0,4},{1,5},{2,6},{3,7},{4,0},{5,1},{6,2},{7,3},{8,12},{9,13},{10,... | collective-permute-start | bytes 3538952 | tf_op jit(solution)/shard_map/ppermute | solution.py:50
  126.3 30.2 %collective-permute-start.27 = (bf16[8,96,768]{2,1,0:T(8,128)(2,1)}, bf16[8,96,768]{2,1,0:T(8,128)(2,1)}, u32[]{:S(2)}, u32[]{:S(2)}) collective-permute-start(bf16[8,96,768]{2,1,0:T(8,128)(2,1)} %collective-permute-done.11.refs_16_.refs_13_), channel_id=1, source_target_pairs={{0,4},{1,5},{2,6},{3,7},{4,0},{5,1},{6,2},{7,3},{8,12},{9,13},{10,... | collective-permute-start | bytes 3538952 | tf_op jit(solution)/shard_map/ppermute | solution.py:50
  262.8 115.2 %reduce-scatter.7.cloned.1.call-start = ((), (), s32[]{:S(2)}) async-start(), calls=%async_computation.5 | async-start | bytes 1474560 | tf_op jit(solution)/shard_map/reduce_scatter | solution.py:626
  271.3 17.0 %collective-permute-start.41 = (bf16[192,768]{1,0:T(8,128)(2,1)S(1)}, bf16[192,768]{1,0:T(8,128)(2,1)S(1)}, u32[]{:S(2)}, u32[]{:S(2)}) collective-permute-start(bf16[192,768]{1,0:T(8,128)(2,1)S(1)} %convert_element_type.135.refs_0_), channel_id=1, source_target_pairs={{0,2},{1,3},{2,0},{3,1},{4,6},{5,7},{6,4},{7,5},{8,10},{9,11},{10,... | collective-permute-start | bytes 884744 | tf_op jit(solution)/shard_map/ppermute | solution.py:50
  292.1 18.4 %collective-permute-start.48 = (bf16[192,576]{1,0:T(8,128)(2,1)S(1)}, bf16[192,576]{1,0:T(8,128)(2,1)S(1)}, u32[]{:S(2)}, u32[]{:S(2)}) collective-permute-start(bf16[192,576]{1,0:T(8,128)(2,1)S(1)} %pad_maximum_fusion.15), channel_id=1, source_target_pairs={{0,8},{1,9},{2,10},{3,11},{4,12},{5,13},{6,14},{7,15},{8,0},{9,1},... | collective-permute-start | bytes 663560 | tf_op jit(solution)/shard_map/ppermute | solution.py:62
  293.2 17.3 %collective-permute-start.47 = (bf16[192,576]{1,0:T(8,128)(2,1)S(1)}, bf16[192,576]{1,0:T(8,128)(2,1)S(1)}, u32[]{:S(2)}, u32[]{:S(2)}) collective-permute-start(bf16[192,576]{1,0:T(8,128)(2,1)S(1)} %pad_maximum_fusion.14), channel_id=1, source_target_pairs={{0,1},{1,0},{2,3},{3,2},{4,5},{5,4},{6,7},{7,6},{8,9},{9,8},{10,11... | collective-permute-start | bytes 663560 | tf_op jit(solution)/shard_map/ppermute | solution.py:62
  326.9 126.4 %reduce-scatter.9.cloned.1.call-start = ((), (), s32[]{:S(2)}) async-start(), calls=%async_computation.6 | async-start | bytes 8847360 | tf_op jit(solution)/shard_map/reduce_scatter | solution.py:620
  326.9 18.2 %collective-permute-start.62 = (bf16[4,192,768]{2,1,0:T(8,128)(2,1)}, bf16[4,192,768]{2,1,0:T(8,128)(2,1)S(1)}, u32[]{:S(2)}, u32[]{:S(2)}) collective-permute-start(bf16[4,192,768]{2,1,0:T(8,128)(2,1)} %get-tuple-element.253.refs_6_), channel_id=1, source_target_pairs={{0,4},{1,5},{2,6},{3,7},{4,0},{5,1},{6,2},{7,3},{8,12},{9,13},{10,... | collective-permute-start | bytes 3538952 | tf_op jit(solution)/shard_map/ppermute | solution.py:50
  351.6 163.2 %reduce-scatter.11.cloned.1.call-start = ((), (), s32[]{:S(2)}) async-start(), calls=%async_computation.7 | async-start | bytes 2211840 | tf_op jit(solution)/shard_map/reduce_scatter | solution.py:626
  363.1 16.7 %collective-permute-start.58 = (bf16[192,768]{1,0:T(8,128)(2,1)S(1)}, bf16[192,768]{1,0:T(8,128)(2,1)}, u32[]{:S(2)}, u32[]{:S(2)}) collective-permute-start(bf16[192,768]{1,0:T(8,128)(2,1)S(1)} %copy-done.25), channel_id=1, source_target_pairs={{0,1},{1,0},{2,3},{3,2},{4,5},{5,4},{6,7},{7,6},{8,9},{9,8},{10,11... | collective-permute-start | bytes 884744 | tf_op jit(solution)/shard_map/ppermute | solution.py:50
  383.8 18.0 %collective-permute-start.67 = (bf16[192,576]{1,0:T(8,128)(2,1)S(1)}, bf16[192,576]{1,0:T(8,128)(2,1)S(1)}, u32[]{:S(2)}, u32[]{:S(2)}) collective-permute-start(bf16[192,576]{1,0:T(8,128)(2,1)S(1)} %pad_maximum_fusion.19), channel_id=1, source_target_pairs={{0,8},{1,9},{2,10},{3,11},{4,12},{5,13},{6,14},{7,15},{8,0},{9,1},... | collective-permute-start | bytes 663560 | tf_op jit(solution)/shard_map/ppermute | solution.py:62
  411.9 31.2 %collective-permute-start.72 = (bf16[8,48,768]{2,1,0:T(8,128)(2,1)S(1)}, bf16[8,48,768]{2,1,0:T(8,128)(2,1)S(1)}, u32[]{:S(2)}, u32[]{:S(2)}) collective-permute-start(bf16[8,48,768]{2,1,0:T(8,128)(2,1)S(1)} %get-tuple-element.286), channel_id=1, source_target_pairs={{0,16},{1,17},{2,18},{3,19},{4,20},{5,21},{6,22},{7,23},{8,24},{9,... | collective-permute-start | bytes 1769480 | tf_op jit(solution)/shard_map/ppermute | solution.py:50
  418.0 28.5 %collective-permute-start.73 = (bf16[8,48,768]{2,1,0:T(8,128)(2,1)S(1)}, bf16[8,48,768]{2,1,0:T(8,128)(2,1)S(1)}, u32[]{:S(2)}, u32[]{:S(2)}) collective-permute-start(bf16[8,48,768]{2,1,0:T(8,128)(2,1)S(1)} %get-tuple-element.287), channel_id=1, source_target_pairs={{0,8},{1,9},{2,10},{3,11},{4,12},{5,13},{6,14},{7,15},{8,0},{9,1},... | collective-permute-start | bytes 1769480 | tf_op jit(solution)/shard_map/ppermute | solution.py:50
  418.6 24.6 %collective-permute-start.75 = (bf16[192,768]{1,0:T(8,128)(2,1)S(1)}, bf16[192,768]{1,0:T(8,128)(2,1)S(1)}, u32[]{:S(2)}, u32[]{:S(2)}) collective-permute-start(bf16[192,768]{1,0:T(8,128)(2,1)S(1)} %convert_element_type.143.refs_4_), channel_id=1, source_target_pairs={{0,2},{1,3},{2,0},{3,1},{4,6},{5,7},{6,4},{7,5},{8,10},{9,11},{10,... | collective-permute-start | bytes 884744 | tf_op jit(solution)/shard_map/ppermute | solution.py:50
  418.6 24.5 %collective-permute-start.74 = (f32[32,768]{1,0:T(8,128)S(1)}, f32[32,768]{1,0:T(8,128)S(1)}, u32[]{:S(2)}, u32[]{:S(2)}) collective-permute-start(f32[32,768]{1,0:T(8,128)S(1)} %add.135), channel_id=1, source_target_pairs={{0,16},{1,17},{2,18},{3,19},{4,20},{5,21},{6,22},{7,23},{8,24},{9,... | collective-permute-start | bytes 294920 | tf_op jit(solution)/shard_map/ppermute | solution.py:50
  418.6 39.5 %collective-permute-start.79 = (bf16[192,768]{1,0:T(8,128)(2,1)S(1)}, bf16[192,768]{1,0:T(8,128)(2,1)S(1)}, u32[]{:S(2)}, u32[]{:S(2)}) collective-permute-start(bf16[192,768]{1,0:T(8,128)(2,1)S(1)} %convert_element_type.143.refs_4_), channel_id=1, source_target_pairs={{0,1},{1,0},{2,3},{3,2},{4,5},{5,4},{6,7},{7,6},{8,9},{9,8},{10,11... | collective-permute-start | bytes 884744 | tf_op jit(solution)/shard_map/ppermute | solution.py:50
  447.4 18.1 %collective-permute-start.77 = (bf16[4,48,768]{2,1,0:T(8,128)(2,1)}, bf16[4,48,768]{2,1,0:T(8,128)(2,1)}, u32[]{:S(2)}, u32[]{:S(2)}) collective-permute-start(bf16[4,48,768]{2,1,0:T(8,128)(2,1)} %add_convert_fusion.2), channel_id=1, source_target_pairs={{0,16},{1,17},{2,18},{3,19},{4,20},{5,21},{6,22},{7,23},{8,24},{9,... | collective-permute-start | bytes 884744 | tf_op jit(solution)/shard_map/ppermute | solution.py:50
  467.3 27.9 %collective-permute-start.82 = (bf16[2,48,768]{2,1,0:T(8,128)(2,1)}, bf16[2,48,768]{2,1,0:T(8,128)(2,1)S(1)}, u32[]{:S(2)}, u32[]{:S(2)}) collective-permute-start(bf16[2,48,768]{2,1,0:T(8,128)(2,1)} %add_convert_fusion.4), channel_id=1, source_target_pairs={{0,1},{1,0},{2,3},{3,2},{4,5},{5,4},{6,7},{7,6},{8,9},{9,8},{10,11... | collective-permute-start | bytes 442376 | tf_op jit(solution)/shard_map/ppermute | solution.py:50
  471.0 24.2 %collective-permute-start.81 = (bf16[2,48,768]{2,1,0:T(8,128)(2,1)}, bf16[2,48,768]{2,1,0:T(8,128)(2,1)S(1)}, u32[]{:S(2)}, u32[]{:S(2)}) collective-permute-start(bf16[2,48,768]{2,1,0:T(8,128)(2,1)} %add_convert_fusion.5), channel_id=1, source_target_pairs={{0,1},{1,0},{2,3},{3,2},{4,5},{5,4},{6,7},{7,6},{8,9},{9,8},{10,11... | collective-permute-start | bytes 442376 | tf_op jit(solution)/shard_map/ppermute | solution.py:50
  471.1 24.1 %collective-permute-start.83 = (f32[32,768]{1,0:T(8,128)S(1)}, f32[32,768]{1,0:T(8,128)S(1)}, u32[]{:S(2)}, u32[]{:S(2)}) collective-permute-start(f32[32,768]{1,0:T(8,128)S(1)} %add.139), channel_id=1, source_target_pairs={{0,1},{1,0},{2,3},{3,2},{4,5},{5,4},{6,7},{7,6},{8,9},{9,8},{10,11... | collective-permute-start | bytes 294920 | tf_op jit(solution)/shard_map/ppermute | solution.py:50
  (182 other events, 1744.2 us)
Sparse Core Ops, SparseCore 0:
  63.8 118.4 all-gather.2
  262.9 63.9 reduce-scatter.4
  329.2 32.6 reduce-scatter.6
  364.0 89.2 reduce-scatter.8
  455.5 47.7 reduce-scatter.10

commit v3 on v2

--- a/solution.py
+++ b/solution.py
@@ -264,7 +264,7 @@
     hat, _ = norm_parts(x_ref[...].astype(F32))
     normed = hat * vec_ref[0:1, :] + vec_ref[1:2, :]
     low = normed.astype(BF)
-    put_transposed(normed, turned, own_ref, other_ref, n_a == 1)
+    put_transposed(normed, turned, own_ref, other_ref)
     for rz in range(4):
         load.wait(rz)
     for pair in range(4):
@@ -282,7 +282,7 @@
     )
 
 
-def attend_kernel(count_ref, p0, p1, p2, p3, o0, o1, o2, o3, m0, m1, m2, m3, kv_ref, q_ref, mixed_ref, lse_ref):
+def attend_kernel(count_ref, p0, p1, p2, p3, o0, o1, o2, o3, m0, m1, m2, m3, kv_ref, q_ref, mixed_ref):
     _, y, c, ten = place()
     tokens = p0.shape[0]
     half = lax.rem(ten, 2)
@@ -295,6 +295,7 @@
     count = count_ref[0]
     ones = jnp.ones((total, HD), BF)
     valid = lax.broadcasted_iota(jnp.int32, (tokens, 128), 1) + (total - 128) < count
+    mixed_ref[:, 192:256] = jnp.zeros((4 * tokens, 64), F32)
     for h in range(3):
         keys = kv_ref[:, h * HD : (h + 1) * HD]
         values = jnp.concatenate([kv_ref[:, 192 + h * HD : 192 + (h + 1) * HD], ones], axis=1)
@@ -310,7 +311,7 @@
             mixed = both[:, :HD] / weight
             mixed_ref[rows, h * HD : (h + 1) * HD] = mixed
             m[:, h * HD : (h + 1) * HD] = mixed.astype(BF)
-            lse_ref[rows, h : h + 1] = highest + jnp.log(weight)
+            mixed_ref[rows, 192 + h : 193 + h] = highest + jnp.log(weight)
 
 
 def attend(count, pieces, others, ties=()):
@@ -318,8 +319,7 @@
     outs = [((tokens, 192), BF)] * 4 + [
         ((8 * tokens, 384), BF),
         ((4 * tokens, 192), BF),
-        ((4 * tokens, 192), F32),
-        ((4 * tokens, 128), F32),
+        ((4 * tokens, 256), F32),
     ]
     return call(
         attend_kernel, outs, [], [SPEC_S] + [SPEC_V] * 8, (count, *pieces, *others),
@@ -422,7 +422,7 @@
     da_ref[...] = d_after
     da = d_after.astype(BF)
     da_wide = da.astype(F32)
-    put_transposed(da_wide, turned, a_own, a_other, n_e == 1)
+    put_transposed(da_wide, turned, a_own, a_other)
     sums_ref[0:1, :] = jnp.sum(da_wide, axis=0, keepdims=True)
     sums_ref[1:2, :] = jnp.sum(grad * hat, axis=0, keepdims=True)
     sums_ref[2:3, :] = jnp.sum(grad, axis=0, keepdims=True)
@@ -462,7 +462,7 @@
     )
 
 
-def attend_back_kernel(count_ref, d0, d1, d2, d3, kv_ref, q_ref, mixed_ref, lse_ref, dq_ref, own_ref, other_ref, do, inner, stat, dkv):
+def attend_back_kernel(count_ref, d0, d1, d2, d3, kv_ref, q_ref, mixed_ref, dq_ref, own_ref, other_ref, do, inner, stat, dkv):
     _, y, c, ten = place()
     tokens = d0.shape[0]
     half = lax.rem(ten, 2)
@@ -474,7 +474,7 @@
         for h in range(3):
             cols = slice(h * HD, (h + 1) * HD)
             inner[rows, h : h + 1] = jnp.sum(grad[:, cols].astype(F32) * mixed_ref[rows, cols], axis=-1, keepdims=True)
-    stat[0] = lse_ref[...].T
+    stat[0] = mixed_ref[:, 128:256].T
     stat[1] = inner[...].T
     total, queries = kv_ref.shape[0], q_ref.shape[0]
     count = count_ref[0]
@@ -494,7 +494,7 @@
             scores = dot_nt(keys, query)
             last = jnp.where(valid, scores[total - 128 :], -1000000000.0)
             scores = jnp.concatenate([scores[: total - 128], last], axis=0)
-            probs = jnp.exp(scores - stat[0, h : h + 1, rows])
+            probs = jnp.exp(scores - stat[0, 64 + h : 65 + h, rows])
             d_probs = dot_nt(values, grad)
             d_scores = (probs * (d_probs - stat[1, h : h + 1, rows])).astype(BF)
             d_values = d_values + dot_nn(probs.astype(BF), grad)
@@ -509,7 +509,7 @@
             ref[pair] = dkv[pl.ds(pl.multiple_of(block * tokens, 64), tokens), :]
 
 
-def attend_back(count, pieces, kv, q, mixed, lse, ties=()):
+def attend_back(count, pieces, kv, q, mixed, ties=()):
     tokens = pieces[0].shape[0]
     outs = [((4 * tokens, 192), BF), ((4, tokens, 384), BF), ((4, tokens, 384), BF)]
     scratch = [
@@ -519,7 +519,7 @@
         pltpu.VMEM((8 * tokens, 384), BF),
     ]
     return call(
-        attend_back_kernel, outs, scratch, [SPEC_S] + [SPEC_V] * 8, (count, *pieces, kv, q, mixed, lse),
+        attend_back_kernel, outs, scratch, [SPEC_S] + [SPEC_V] * 7, (count, *pieces, kv, q, mixed),
         micros=11, name="attend_back", ties=ties,
     )
 
@@ -567,45 +567,18 @@
     )
 
 
-def emit(value, rz, orders, outs):
-    rows = 96 // len(orders)
-    for xy in range(4):
-        for n, order in enumerate(orders):
-            part, at = part_of((16 if xy & 2 else 0) | (8 if xy & 1 else 0) | rz, order)
-            outs[n * 5 + part][at] = value[xy * 96 + n * rows : xy * 96 + (n + 1) * rows].astype(BF)
-
-
-def weigh_high_kernel(row, both, n_in, *refs):
-    left, right = refs[: n_in // 2], refs[n_in // 2 : n_in]
-    out_ref, part, sem = refs[-3:]
+def weigh_both_kernel(m_own, m_got, z_own, z_got, h_own, h_got, a_own, a_got, out_ref):
     for z in range(4):
-        first = dot_nn(left[0][...], right[0][z]) + dot_nn(left[1][...], right[1][z])
-        second = dot_nn(left[2][...], right[2][z]) + dot_nn(left[3][...], right[3][z])
+        expand = dot_nn(m_own[...], h_own[z]) + dot_nn(m_got[...], h_got[z])
+        shrink = dot_nn(z_own[...], a_own[z]) + dot_nn(z_got[...], a_got[z])
         for at, xy in enumerate(RING):
             rows = slice(xy * 96, (xy + 1) * 96)
-            if both:
-                part[at * 4 + z, 0:96] = first[rows].astype(BF)
-                part[at * 4 + z, 96:192] = second[rows].astype(BF)
-            else:
-                part[at * 4 + z] = jnp.concatenate([first[rows], second[rows]], axis=1).astype(BF)
-    copy = pltpu.make_async_copy(part, out_ref.at[:, pl.ds(row, part.shape[1])], sem)
-    copy.start()
-    copy.wait()
-
-
-def weigh_high(args, rows, row, both, into=None):
-    more = [] if into is None else [into]
-    return pl.pallas_call(
-        partial(weigh_high_kernel, row, both, len(args)),
-        out_shape=jax.ShapeDtypeStruct((16, rows, 768), BF),
-        in_specs=[SPEC_V] * len(args) + [SPEC_A] * len(more),
-        out_specs=SPEC_A,
-        scratch_shapes=[pltpu.VMEM((16, 192 if both else 96, 768), BF), pltpu.SemaphoreType.DMA],
-        input_output_aliases={len(args): 0} if more else {},
-        compiler_params=pltpu.CompilerParams(vmem_limit_bytes=LIMIT * 1024 * 1024),
-        cost_estimate=pl.CostEstimate(flops=int(5 * COST), bytes_accessed=1000, transcendentals=0),
-        name="weigh_both" if both else "weigh_attention_high",
-    )(*args, *more)
+            out_ref[at * 4 + z, 0:96] = expand[rows].astype(BF)
+            out_ref[at * 4 + z, 96:192] = shrink[rows].astype(BF)
+
+
+def weigh_both(args):
+    return call(weigh_both_kernel, [((16, 192, 768), BF)], [], [SPEC_V] * 8, args, micros=5, name="weigh_both")[0]
 
 
 def sum_plane(chunks, mesh_shape):
@@ -626,34 +599,54 @@
     return lax.psum_scatter(chunks, "tensor", scatter_dimension=0, tiled=True).astype(F32)
 
 
-def weigh_attention_kernel(orders, n_own, n_got, a_own, a_got, q_own, q_got, m_own, m_got, *outs):
-    _, _, _, ten = place()
+def weigh_attention_kernel(total_ref, *refs):
+    x, y, c, ten = place()
+    low, high, outs, turned = refs[:8], refs[8:16], refs[16:26], refs[26]
+    turned[...] = jnp.concatenate([total_ref[...], jnp.zeros((96, 768), F32)], axis=0).T
     for rz in range(4):
         z = xor_two(ten, rz)
-        qkv = dot_nn(n_own[...], q_own[z]) + dot_nn(n_got[...], q_got[z])
-        out = dot_nn(a_own[...], m_own[z]) + dot_nn(a_got[...], m_got[z])
-        emit(jnp.concatenate([qkv, out], axis=1), rz, orders, outs)
-
-
-def weigh_attention(orders, args, ties=()):
-    outs = [((n, 96 // len(orders), 768), BF) for _ in orders for n in (8, 4, 2, 1, 1)]
+        values = []
+        for n_own, n_got, a_own, a_got, q_own, q_got, m_own, m_got in (low, high):
+            qkv = dot_nn(n_own[...], q_own[z]) + dot_nn(n_got[...], q_got[z])
+            out = dot_nn(a_own[...], m_own[z]) + dot_nn(a_got[...], m_got[z])
+            values.append(jnp.concatenate([qkv, out], axis=1).astype(BF))
+        for xy in range(4):
+            rel = (16 if xy & 2 else 0) | (8 if xy & 1 else 0) | rz
+            for n, order in enumerate(SUM_A):
+                part, at = part_of(rel, order)
+                lines = slice(xy * 96 + n * 48, xy * 96 + (n + 1) * 48)
+                for k, value in enumerate(values):
+                    outs[n * 5 + part][at, k * 48 : (k + 1) * 48, 0:768] = value[lines]
+            block = row_block(x, y, c, rel)
+            query = turned[pl.ds(pl.multiple_of(384 + block * 24, 8), 24), :][:, :32]
+            other = turned[pl.ds(pl.multiple_of(192 + block * 24, 8), 24), :][:, :32]
+            none = jnp.zeros((24, 32), F32)
+            pair = jnp.concatenate([none, query, other, none], axis=1)
+            more = turned[pl.ds(pl.multiple_of(block * 96, 32), 96), :]
+            more = more + jnp.concatenate([pair, jnp.zeros((72, 128), F32)], axis=0)
+            part, at = part_of(rel, SUM_A[0])
+            outs[part][at, :, 768:896] = more.astype(BF)
+
+
+def weigh_attention(total, low, high):
+    outs = [((n, 96, width), BF) for width in (896, 768) for n in (8, 4, 2, 1, 1)]
     return call(
-        partial(weigh_attention_kernel, orders), outs, [], [SPEC_V] * 8, args,
-        micros=3, name="weigh_attention", ties=ties,
-    )
-
-
-def spread_kernel(*refs):
+        weigh_attention_kernel, outs, [pltpu.VMEM((768, 128), F32)], [SPEC_V] * 17, (total, *low, *high), micros=6,
+        name="weigh_attention",
+    )
+
+
+def spread_kernel(p0, p1, p2, p3, first_ref, second_ref):
     ten = lax.axis_index("tensor")
-    for n in range(2):
-        for at, rz in enumerate((0, 2, 1, 3)):
-            refs[8 + n][xor_two(ten, rz)] = refs[n * 4 + at][...].astype(refs[8 + n].dtype)
-
-
-def spread(left, left_type, right, right_type):
-    tokens, width = left[0].shape
-    outs = [((4, tokens, width), left_type), ((4, tokens, width), right_type)]
-    done = call(spread_kernel, outs, [], [SPEC_V] * 8, (*left, *right), name="spread")
+    for rz, p in ((0, p0), (2, p1), (1, p2), (3, p3)):
+        first_ref[xor_two(ten, rz)] = p[0]
+        second_ref[xor_two(ten, rz)] = p[1].astype(F32)
+
+
+def spread(frames):
+    _, tokens, width = frames[0].shape
+    outs = [((4, tokens, width), BF), ((4, tokens, width), F32)]
+    done = call(spread_kernel, outs, [], [SPEC_V] * 4, frames, name="spread")
     return [d.reshape(2, 1, 2 * tokens, width) for d in done]
 
 
@@ -747,44 +740,40 @@
         *pieces, n_own, n_other = project(state, vec[d], qvb[d], a_w[d], tokens)
         pieces = [pieces[0]] + [swap_group(pieces[p], p, shape) for p in (1, 2, 3)]
         others = [swap(p[:, :384], "c", shape) for p in pieces]
-        *mixed, kv, q, mixed_wide, lse = attend(count, pieces, others)
+        *mixed, kv, q, mixed_wide = attend(count, pieces, others)
         mixed = [mixed[0]] + [swap_group(mixed[p], p, shape) for p in (1, 2, 3)]
         x_in = state
         state, after, mixed_all, m_own, m_other, active, slope = mlp(mixed, x_in, vec[d], eb[d], a_w[d], e_w[d], s_w[d])
-        kept.append((x_in, n_own, n_other, kv, q, mixed_wide, lse, after, mixed_all, m_own, m_other, active, slope))
-    encoded = [state.astype(BF)]
+        kept.append((x_in, n_own, n_other, kv, q, mixed_wide, after, mixed_all, m_own, m_other, active, slope))
+    encoded = state.astype(BF)
 
     grad = dy0
     for d in (1, 0):
-        x_in, n_own, n_other, kv, q, mixed_wide, lse, after, mixed_all, m_own, m_other, active, slope = kept[d]
+        x_in, n_own, n_other, kv, q, mixed_wide, after, mixed_all, m_own, m_other, active, slope = kept[d]
         d0, d1, d2, d3, d_after, d_hid, da_own, da_other, sums_two, ebs, z_own, z_other = mlp_back(
             grad, after, vec[d], slope, a_w[d], e_w[d], s_w[d]
         )
         d_mixed = [d0] + [swap_group(v, p + 1, shape) for p, v in enumerate((d1, d2, d3))]
         m_got, hid_got, z_got, active_got = (swap(v, "c", shape) for v in (m_other, d_hid, z_other, active))
-        given = (m_own, m_got, z_own, z_got, d_hid, hid_got, active, active_got)
         if d:
-            chunks = weigh_high(given, 192, 0, True)
+            d1, d2, d3, m_got, z_got, hid_got, active_got = fence(*d_mixed[1:], m_got, z_got, hid_got, active_got)
+            d_mixed = [d0, d1, d2, d3]
+            chunks = weigh_both((m_own, m_got, z_own, z_got, d_hid, hid_got, active, active_got))
             high_sum = sum_plane(chunks, shape)
-            encoded[0], *d_mixed = fence(encoded[0], *d_mixed)
-            encoded.append(swap(encoded[0], "z2", shape))
         else:
-            chunks = weigh_high(given, 288, 0, True, chunks)
-            low_sum = sum_line(sum_plane(chunks, shape))
-            encoded[1], *d_mixed = fence(encoded[1], *d_mixed)
-            encoded.append(swap(encoded[1], "z1", shape))
-        dq, own, other = attend_back(count, d_mixed, kv, q, mixed_wide, lse, [chunks])
-        if d:
-            *encoded, other = fence(*encoded, other)
-        else:
-            *encoded, high_sum, other = fence(*encoded, high_sum, other)
+            high_sum, *d_mixed = fence(high_sum, *d_mixed)
+            high_sum = sum_line(high_sum)
+        dq, own, other = attend_back(count, d_mixed, kv, q, mixed_wide, [chunks] if d else [])
         d_kv = (own.astype(F32) + swap(other, "c", shape).astype(F32)).astype(BF)
         back = [jnp.concatenate([d_kv[p], dq[p * tokens : (p + 1) * tokens]], axis=1) for p in range(4)]
+        if d == 0:
+            *back, m_got, z_got, hid_got, active_got = fence(*back, m_got, z_got, hid_got, active_got)
         back = [back[0]] + [swap_group(back[p], p, shape) for p in (1, 2, 3)]
-        if d:
-            encoded[0], *back = fence(encoded[0], *back)
-            got_z = swap(encoded[0], "z1", shape)
-        grad, d_qkv, total = project_back(back, d_after, x_in, vec[d], sums_two, ebs, [] if d else [high_total], a_w[d])
+        if d == 0:
+            chunks = weigh_both((m_own, m_got, z_own, z_got, d_hid, hid_got, active, active_got))
+            low_sum = sum_plane(chunks, shape)
+            high_sum, *back = fence(high_sum, *back)
+        grad, d_qkv, total = project_back(back, d_after, x_in, vec[d], sums_two, ebs, [] if d else [high_total], a_w[d], [chunks])
         given = (
             n_own,
             swap(n_other, "c", shape),
@@ -797,33 +786,37 @@
         )
         if d:
             high_total = total
-            chunks = weigh_high(given, 288, 192, False)
-            chunks, got_z, high_sum, grad = fence(chunks, got_z, high_sum, grad)
-            high_sum = sum_line(high_sum)
-            encoded.append(got_z)
+            high_given = given
     if dp_size == 2:
         total = total + swap(total, "c", shape)
+        embedded = total
     else:
+        embedded = jnp.zeros_like(total)
         total = lax.psum(total, AXES)
-    parts = weigh_attention(SUM_A, given)
+    parts = weigh_attention(embedded, given, high_given)
     sums_a = [Reducer(parts[n * 5 : n * 5 + 5], order, shape) for n, order in enumerate(SUM_A)]
-    features_grad = [grad.astype(BF)]
+    frames = [jnp.stack([encoded, grad.astype(BF)])]
     last = Together(sums_a)
-    total, features_grad[0] = last.wait(total, features_grad[0])
-    for step, bit in enumerate(("x", "y", "z1", "z2")):
-        got = [swap(total, bit, shape)] if dp_size == 2 else []
+    (frames[0],) = last.wait(frames[0])
+    for step in range(4):
+        got = []
         if step == 0:
-            got.append(swap(features_grad[0], "z2", shape))
+            got = [low_sum, swap(frames[0], "z2", shape)]
         elif step == 1:
-            got += [swap(v, "z1", shape) for v in features_grad]
+            got = [swap(v, "z1", shape) for v in frames]
+        elif step == 3:
+            got = [low_sum]
         got = list(last.go(*got))
-        if dp_size == 2:
-            total = total + got.pop(0)
-        features_grad += got
+        if step == 0:
+            low_sum = sum_line(got.pop(0))
+        elif step == 3:
+            low_sum = got.pop()
+        frames += got
     small = total.reshape(LAYERS, 16, 768)
-    encoded, grad_features = spread(encoded, BF, features_grad, F32)
-    g_a = [jnp.concatenate([r.finish() for r in sums_a], axis=0), low_sum[192:]]
-    g_e, g_s = ([low_sum[:96], high_sum[:96]], [low_sum[96:192], high_sum[96:]])
+    encoded, grad_features = spread(frames)
+    chunk, rest = (r.finish() for r in sums_a)
+    g_a = [jnp.concatenate([chunk[at : at + 48, :768], rest[at : at + 48]], axis=0) for at in (0, 48)]
+    g_e, g_s = ([low_sum[:96], high_sum[:96]], [low_sum[96:], high_sum[96:]])
 
     if dp_size != 2:
         start = (lax.rem(dp, 2) * 4 + seq) * 96
@@ -834,21 +827,27 @@
 
         g_a, g_e, g_s = ([down(g) for g in gs] for gs in (g_a, g_e, g_s))
     ga, ge, gs = jnp.stack(g_a), jnp.stack(g_e), jnp.stack(g_s)
-    g_small = small
-    mine = dp * seq_size + seq
-    grad_vectors = lax.dynamic_slice_in_dim(g_small[:, :6], mine * width, width, axis=2)
-    eb_width, qv_width = expand_bias.shape[1], qv_bias.shape[2]
-    grad_eb = lax.dynamic_slice_in_dim(
-        lax.dynamic_index_in_dim(g_small[:, 6:10], ten, axis=1, keepdims=False), mine * eb_width, eb_width, axis=1
-    )
-    qv = lax.dynamic_index_in_dim(g_small[:, 10:14], ten, axis=1, keepdims=False)
-    grad_qv = jnp.stack(
-        [
-            lax.dynamic_slice_in_dim(qv[:, 384:576], mine * qv_width, qv_width, axis=1),
-            lax.dynamic_slice_in_dim(qv[:, 192:384], mine * qv_width, qv_width, axis=1),
-        ],
-        axis=1,
-    )
+    if dp_size == 2:
+        turned = chunk[:, 768:864].T.reshape(3, LAYERS, 16, 96)
+        grad_vectors = turned[0, :, :6]
+        grad_eb = lax.dynamic_index_in_dim(turned[0, :, 6:10], ten, axis=1, keepdims=False)
+        pair = lax.dynamic_index_in_dim(turned[1:, :, 10:14], ten, axis=2, keepdims=False)
+        grad_qv = pair[:, :, :24].transpose(1, 0, 2)
+    else:
+        mine = dp * seq_size + seq
+        grad_vectors = lax.dynamic_slice_in_dim(small[:, :6], mine * width, width, axis=2)
+        eb_width, qv_width = expand_bias.shape[1], qv_bias.shape[2]
+        grad_eb = lax.dynamic_slice_in_dim(
+            lax.dynamic_index_in_dim(small[:, 6:10], ten, axis=1, keepdims=False), mine * eb_width, eb_width, axis=1
+        )
+        qv = lax.dynamic_index_in_dim(small[:, 10:14], ten, axis=1, keepdims=False)
+        grad_qv = jnp.stack(
+            [
+                lax.dynamic_slice_in_dim(qv[:, 384:576], mine * qv_width, qv_width, axis=1),
+                lax.dynamic_slice_in_dim(qv[:, 192:384], mine * qv_width, qv_width, axis=1),
+            ],
+            axis=1,
+        )
     grad_qkv = jnp.stack([ga[:, :, 384:576], ga[:, :, :192], ga[:, :, 192:384]], axis=2)
     return (
         encoded,

time: 537 us -> 533 us (level)
  starting transfers between devices: 73.6 us -> 63 us
  other arithmetic: 22.4 us -> 28.4 us
    pallas_call x14 -> x16, Pallas kernels: 99.7 us -> 115 us  [call(): pl.pallas_call(lambda *refs: kernel(*refs[len(ties):]), out_shape=[jax.Sh...]
    ppermute x63 -> x56, waiting for transfers between devices: 153 us -> 168 us  [swap(): return lax.ppermute(value, AXES, pairs)]
    pallas_call x3 -> x0, Pallas kernels: 14.4 us -> none  [weigh_high(): pl.pallas_call(partial(weigh_high_kernel, row, both, len(args)), out_shap...]
    ppermute x63 -> x56, starting transfers between devices: 46.2 us -> 35.9 us  [swap(): return lax.ppermute(value, AXES, pairs)]
    ppermute x24, waiting for transfers between devices: 87.8 us -> 79.5 us  [swap_group(): return lax.ppermute(value, AXES, pairs)]
    reduce_scatter x2, waiting for transfers between devices: 7.08 us -> 0.01 us  [sum_plane(): lax.psum_scatter(chunks.reshape(16 * rows, 768), AXES, scatter_dimension=...]
    reduce_scatter x2, waiting for transfers between devices: 0.02 us -> 5.66 us  [sum_line(): lax.psum_scatter(chunks, 'tensor', scatter_dimension=0, tiled=True)]
    unnamed x262 -> x221, local copies, waits for them, and re-layouts: 44.3 us -> 40.2 us
  transfers between devices with their start and end apart: 92 -> 85, of which waited for: 51 -> 52; matrix products, arithmetic and copies ran while one was open for 5% -> 6% of each run, Pallas kernels for 14% -> 15%
where the time goes in v3:
time: 533 us; the launch traced here: 523 us
  waiting for transfers between devices  254 us (48%)
  Pallas kernels  115 us (22%)
  starting transfers between devices  63 us (12%)
  local copies, waits for them, and re-layouts  47.8 us (9%)
  other arithmetic  28.4 us (5%)
  between operations  15.5 us (3%)
    ppermute x56, waiting for transfers between devices, swap(): return lax.ppermute(value, AXES, pairs)  168 us
    pallas_call x16, Pallas kernels, call(): pl.pallas_call(lambda *refs: kernel(*refs[len(ties):]), out_shape=[jax.Sh...  115 us
    ppermute x24, waiting for transfers between devices, swap_group(): return lax.ppermute(value, AXES, pairs)  79.5 us
    unnamed x221, local copies, waits for them, and re-layouts  40.2 us
    ppermute x56, starting transfers between devices, swap(): return lax.ppermute(value, AXES, pairs)  35.9 us
    ppermute x24, starting transfers between devices, swap_group(): return lax.ppermute(value, AXES, pairs)  26.9 us
    convert_element_type x6, other arithmetic, send(): self.parts[self.step].astype(BF)  10.9 us
  transfers between devices with their start and end apart: 85, of which 52 were waited for; matrix products, arithmetic and copies ran while one was open for 6% of the time, Pallas kernels for 15%

profile of v3, /device:TPU:0, one launch (start us, length us, event | category | flops | bytes accessed | tf_op | source)
XLA Modules:
  0.0 523.3 jit_solution(4672013032186190008)
XLA Ops:
  16.4 10.7 %collective-permute-done.1 = bf16[1,96,768]{2,1,0:T(8,128)(2,1)S(1)} collective-permute-done((bf16[1,96,768]{2,1,0:T(8,128)(2,1)S(1)}, bf16[1,96,768]{2,1,0:T(8,128)(2,1)S(1)}, u32[]{:S(2)}, u32[]{:S(2)}) %collective-permute-start.1) | collective-permute-done | bytes 147488 | tf_op jit(solution)/shard_map/ppermute | solution.py:50
  36.7 4.5 collective-permute-done.5
  47.3 10.8 %collective-permute-done.8 = bf16[4,96,768]{2,1,0:T(8,128)(2,1)} collective-permute-done((bf16[4,96,768]{2,1,0:T(8,128)(2,1)S(1)}, bf16[4,96,768]{2,1,0:T(8,128)(2,1)}, u32[]{:S(2)}, u32[]{:S(2)}) %collective-permute-start.8) | collective-permute-done | bytes 589856 | tf_op jit(solution)/shard_map/ppermute | solution.py:50
  66.1 26.7 %collective-permute-done.10.refs_12_.refs_9_ = bf16[8,96,768]{2,1,0:T(8,128)(2,1)} collective-permute-done((bf16[8,96,768]{2,1,0:T(8,128)(2,1)}, bf16[8,96,768]{2,1,0:T(8,128)(2,1)}, u32[]{:S(2)}, u32[]{:S(2)}) %collective-permute-start.10) | collective-permute-done | bytes 1179680 | tf_op jit(solution)/shard_map/ppermute | solution.py:50
  93.1 7.9 %collective-permute-done.9.refs_4_.refs_8_.refs_5_.refs_12_ = bf16[8,104,768]{2,1,0:T(8,128)(2,1)} collective-permute-done((bf16[8,104,768]{2,1,0:T(8,128)(2,1)S(1)}, bf16[8,104,768]{2,1,0:T(8,128)(2,1)}, u32[]{:S(2)}, u32[]{:S(2)}) %collective-permute-start.9) | collective-permute-done | bytes 1277984 | tf_op jit(solution)/shard_map/ppermute | solution.py:50
  111.6 14.7 %collective-permute-done.14.refs_2_ = bf16[192,576]{1,0:T(8,128)(2,1)S(1)} collective-permute-done((bf16[192,576]{1,0:T(8,128)(2,1)S(1)}, bf16[192,576]{1,0:T(8,128)(2,1)S(1)}, u32[]{:S(2)}, u32[]{:S(2)}) %collective-permute-start.14) | collective-permute-done | bytes 221216 | tf_op jit(solution)/shard_map/ppermute | solution.py:62
  126.6 9.0 %collective-permute-done.16.refs_4_ = bf16[192,576]{1,0:T(8,128)(2,1)S(1)} collective-permute-done((bf16[192,576]{1,0:T(8,128)(2,1)S(1)}, bf16[192,576]{1,0:T(8,128)(2,1)S(1)}, u32[]{:S(2)}, u32[]{:S(2)}) %collective-permute-start.16) | collective-permute-done | bytes 221216 | tf_op jit(solution)/shard_map/ppermute | solution.py:62
  140.0 7.7 %attend.2 = (bf16[192,192]{1,0:T(8,128)(2,1)S(1)}, bf16[192,192]{1,0:T(8,128)(2,1)}, bf16[192,192]{1,0:T(8,128)(2,1)S(1)}, bf16[192,192]{1,0:T(8,128)(2,1)S(1)},...) custom-call(s32[1]{0:T(128)} %bitcast.refs_0_.refs_1_, ...), custom_call_target="tpu_custom_call" | custom-call | flops 2100000000 | bytes 1000 | tf_op jit(solution)/shard_map/attend/pallas_call | solution.py:246
  155.7 6.4 %collective-permute-done.21.refs_1_ = bf16[192,192]{1,0:T(8,128)(2,1)S(1)} collective-permute-done((bf16[192,192]{1,0:T(8,128)(2,1)}, bf16[192,192]{1,0:T(8,128)(2,1)S(1)}, u32[]{:S(2)}, u32[]{:S(2)}) %collective-permute-start.21) | collective-permute-done | bytes 73760 | tf_op jit(solution)/shard_map/ppermute | solution.py:62
  167.7 10.2 %mlp.2 = (f32[192,768]{1,0:T(8,128)S(1)}, f32[192,768]{1,0:T(8,128)S(1)}, bf16[4,192,192]{2,1,0:T(8,128)(2,1)S(1)}, bf16[384,192]{1,0:T(8,128)(2,1)S(1)}, bf16[3...) custom-call(bf16[192,192]{1,0:T(8,128)(2,1)S(1)} %get-tuple-element.171.refs_0_, ...), custom_call_target="tpu_custom_call" | custom-call | flops 3600000000 | bytes 1000 | tf_op jit(solution)/shard_map/mlp/pallas_call | solution.py:246
  190.4 5.2 collective-permute-done.28.refs_2_
  196.3 4.8 collective-permute-done.30.refs_4_
  202.5 8.0 %attend.3 = (bf16[192,192]{1,0:T(8,128)(2,1)S(1)}, bf16[192,192]{1,0:T(8,128)(2,1)}, bf16[192,192]{1,0:T(8,128)(2,1)}, bf16[192,192]{1,0:T(8,128)(2,1)}, bf16[15...) custom-call(s32[1]{0:T(128)} %bitcast.refs_0_.refs_1_, ...), custom_call_target="tpu_custom_call" | custom-call | flops 2100000000 | bytes 1000 | tf_op jit(solution)/shard_map/attend/pallas_call | solution.py:246
  224.5 11.5 %mlp.3 = (f32[192,768]{1,0:T(8,128)S(1)}, f32[192,768]{1,0:T(8,128)S(1)}, bf16[4,192,192]{2,1,0:T(8,128)(2,1)S(1)}, bf16[384,192]{1,0:T(8,128)(2,1)S(1)}, bf16[3...) custom-call(bf16[192,192]{1,0:T(8,128)(2,1)S(1)} %copy-done.50, ...), custom_call_target="tpu_custom_call" | custom-call | flops 3600000000 | bytes 1000 | tf_op jit(solution)/shard_map/mlp/pallas_call | solution.py:246
  237.5 10.1 %mlp_back.2 = (bf16[192,192]{1,0:T(8,128)(2,1)S(1)}, bf16[192,192]{1,0:T(8,128)(2,1)S(1)}, bf16[192,192]{1,0:T(8,128)(2,1)S(1)}, bf16[192,192]{1,0:T(8,128)(2,1)...) custom-call(bf16[192,768]{1,0:T(8,128)(2,1)S(1)} %dynamic-slice_bitc, ...), custom_call_target="tpu_custom_call" | custom-call | flops 3300000000 | bytes 1000 | tf_op jit(solution)/shard_map/mlp_back/pallas_call | solution.py:246
  260.9 5.2 weigh_both.2.refs_0_
  270.5 10.4 %attend_back.2 = (bf16[768,192]{1,0:T(8,128)(2,1)S(1)}, bf16[4,192,384]{2,1,0:T(8,128)(2,1)S(1)}, bf16[4,192,384]{2,1,0:T(8,128)(2,1)S(1)}) custom-call(bf16[16,192,768]{2,1,0:T(8,128)(2,1)} %weigh_both.2.refs_0_, s32[1]{0:T(128)} %bitcast.refs_0_.refs_1_, bf16[192,192]{1,0:T(8,128)(2,1)S(1)} %copy-done.72, ...), custom_call_target="tpu_custom_call" | custom-call | flops 3300000000 | bytes 1000 | tf_op jit(solution)/shard_map/attend_back/pallas_call | solution.py:246
  287.0 6.0 %collective-permute-done.48.refs_4_ = bf16[192,576]{1,0:T(8,128)(2,1)S(1)} collective-permute-done((bf16[192,576]{1,0:T(8,128)(2,1)S(1)}, bf16[192,576]{1,0:T(8,128)(2,1)S(1)}, u32[]{:S(2)}, u32[]{:S(2)}) %collective-permute-start.48) | collective-permute-done | bytes 221216 | tf_op jit(solution)/shard_map/ppermute | solution.py:62
  293.0 9.7 %collective-permute-done.47.refs_3_ = bf16[192,576]{1,0:T(8,128)(2,1)S(1)} collective-permute-done((bf16[192,576]{1,0:T(8,128)(2,1)S(1)}, bf16[192,576]{1,0:T(8,128)(2,1)S(1)}, u32[]{:S(2)}, u32[]{:S(2)}) %collective-permute-start.47) | collective-permute-done | bytes 221216 | tf_op jit(solution)/shard_map/ppermute | solution.py:62
  302.8 4.6 project_back.2
  308.1 11.1 %mlp_back.3 = (bf16[192,192]{1,0:T(8,128)(2,1)S(1)}, bf16[192,192]{1,0:T(8,128)(2,1)S(1)}, bf16[192,192]{1,0:T(8,128)(2,1)S(1)}, bf16[192,192]{1,0:T(8,128)(2,1)...) custom-call(f32[192,768]{1,0:T(8,128)S(1)} %get-tuple-element.216.re, ...), custom_call_target="tpu_custom_call" | custom-call | flops 3300000000 | bytes 1000 | tf_op jit(solution)/shard_map/mlp_back/pallas_call | solution.py:246
  331.3 10.6 %attend_back.3 = (bf16[768,192]{1,0:T(8,128)(2,1)S(1)}, bf16[4,192,384]{2,1,0:T(8,128)(2,1)S(1)}, bf16[4,192,384]{2,1,0:T(8,128)(2,1)S(1)}) custom-call(s32[1]{0:T(128)} %bitcast.refs_0_.refs_1_, bf16[192,192]{1,0:T(8,128)(2,1)S(1)} %get-tuple-element.223.refs_1_, bf16[192,192]{1,0:T(8,128)(2,1)S(1)} %collective-permute-done.49.refs_2_, ...), custom_call_target="tpu_custom_call" | custom-call | flops 3300000000 | bytes 1000 | tf_op jit(solution)/shard_map/attend_back/pallas_call | solution.py:246
  347.9 4.9 weigh_both.3.refs_0_
  356.5 5.7 %reduce-scatter.7.cloned.1.call-done = bf16[192,768]{1,0:T(8,128)(2,1)} async-done(((bf16[768,768]{1,0:T(8,128)(2,1)}), bf16[192,768]{1,0:T(8,128)(2,1)}) %reduce-scatter.7.cloned.1.call-update) | async-done | bytes 294928 | tf_op jit(solution)/shard_map/reduce_scatter | solution.py:599
  364.0 5.9 %collective-permute-done.59.refs_4_ = bf16[192,576]{1,0:T(8,128)(2,1)S(1)} collective-permute-done((bf16[192,576]{1,0:T(8,128)(2,1)S(1)}, bf16[192,576]{1,0:T(8,128)(2,1)S(1)}, u32[]{:S(2)}, u32[]{:S(2)}) %collective-permute-start.59) | collective-permute-done | bytes 221216 | tf_op jit(solution)/shard_map/ppermute | solution.py:62
  370.0 4.3 project_back.3
  381.1 7.1 %weigh_attention.1 = (bf16[8,96,896]{2,1,0:T(8,128)(2,1)}, bf16[4,96,896]{2,1,0:T(8,128)(2,1)S(1)}, bf16[2,96,896]{2,1,0:T(8,128)(2,1)S(1)}, bf16[1,96,896]{2,1,...) custom-call(f32[32,768]{1,0:T(8,128)S(1)} %add.110.refs_0_, ...), custom_call_target="tpu_custom_call" | custom-call | flops 1800000000 | bytes 1000 | tf_op jit(solution)/shard_map/weigh_attention/pallas_call | solution.py:246
  398.4 25.0 %collective-permute-done.71.refs_1_ = bf16[2,192,768]{2,1,0:T(8,128)(2,1)S(1)} collective-permute-done((bf16[2,192,768]{2,1,0:T(8,128)(2,1)S(1)}, bf16[2,192,768]{2,1,0:T(8,128)(2,1)S(1)}, u32[]{:S(2)}, u32[]{:S(2)}) %collective-permute-start.71) | collective-permute-done | bytes 589856 | tf_op jit(solution)/shard_map/ppermute | solution.py:50
  423.4 11.8 %collective-permute-done.70 = bf16[8,96,768]{2,1,0:T(8,128)(2,1)} collective-permute-done((bf16[8,96,768]{2,1,0:T(8,128)(2,1)}, bf16[8,96,768]{2,1,0:T(8,128)(2,1)}, u32[]{:S(2)}, u32[]{:S(2)}) %collective-permute-start.70) | collective-permute-done | bytes 1179680 | tf_op jit(solution)/shard_map/ppermute | solution.py:50
  446.5 12.8 %collective-permute-done.73 = bf16[4,96,768]{2,1,0:T(8,128)(2,1)S(1)} collective-permute-done((bf16[4,96,768]{2,1,0:T(8,128)(2,1)S(1)}, bf16[4,96,768]{2,1,0:T(8,128)(2,1)S(1)}, u32[]{:S(2)}, u32[]{:S(2)}) %collective-permute-start.73) | collective-permute-done | bytes 589856 | tf_op jit(solution)/shard_map/ppermute | solution.py:50
  459.3 19.1 %collective-permute-done.75.refs_3_ = bf16[2,192,768]{2,1,0:T(8,128)(2,1)S(1)} collective-permute-done((bf16[2,192,768]{2,1,0:T(8,128)(2,1)S(1)}, bf16[2,192,768]{2,1,0:T(8,128)(2,1)S(1)}, u32[]{:S(2)}, u32[]{:S(2)}) %collective-permute-start.75) | collective-permute-done | bytes 589856 | tf_op jit(solution)/shard_map/ppermute | solution.py:50
  484.2 8.1 %collective-permute-done.77 = bf16[2,96,768]{2,1,0:T(8,128)(2,1)S(1)} collective-permute-done((bf16[2,96,768]{2,1,0:T(8,128)(2,1)}, bf16[2,96,768]{2,1,0:T(8,128)(2,1)S(1)}, u32[]{:S(2)}, u32[]{:S(2)}) %collective-permute-start.77) | collective-permute-done | bytes 294944 | tf_op jit(solution)/shard_map/ppermute | solution.py:50
  (477 shorter events, 197.3 us)
Async XLA Ops:
  7.2 175.2 %all-gather.3.cloned.1.call-start = ((), (), s32[]{:S(2)}) async-start(), calls=%async_computation.8 | async-start | bytes 14598144 | tf_op jit(solution)/shard_map/all_gather | solution.py:724
  8.6 18.5 %collective-permute-start.1 = (bf16[1,96,768]{2,1,0:T(8,128)(2,1)S(1)}, bf16[1,96,768]{2,1,0:T(8,128)(2,1)S(1)}, u32[]{:S(2)}, u32[]{:S(2)}) collective-permute-start(bf16[1,96,768]{2,1,0:T(8,128)(2,1)S(1)} %get-tuple-element.371), channel_id=1, source_target_pairs={{0,2},{1,3},{2,0},{3,1},{4,6},{5,7},{6,4},{7,5},{8,10},{9,11},{10,... | collective-permute-start | bytes 442376 | tf_op jit(solution)/shard_map/ppermute | solution.py:50
  12.7 17.6 %collective-permute-start.2 = (bf16[1,96,768]{2,1,0:T(8,128)(2,1)S(1)}, bf16[1,96,768]{2,1,0:T(8,128)(2,1)S(1)}, u32[]{:S(2)}, u32[]{:S(2)}) collective-permute-start(bf16[1,96,768]{2,1,0:T(8,128)(2,1)S(1)} %get-tuple-element.359), channel_id=1, source_target_pairs={{0,2},{1,3},{2,0},{3,1},{4,6},{5,7},{6,4},{7,5},{8,10},{9,11},{10,... | collective-permute-start | bytes 442376 | tf_op jit(solution)/shard_map/ppermute | solution.py:50
  13.5 19.4 %collective-permute-start = (bf16[1,104,768]{2,1,0:T(8,128)(2,1)S(1)}, bf16[1,104,768]{2,1,0:T(8,128)(2,1)S(1)}, u32[]{:S(2)}, u32[]{:S(2)}) collective-permute-start(bf16[1,104,768]{2,1,0:T(8,128)(2,1)S(1)} %maximum_bitcast_fusion.3), channel_id=1, source_target_pairs={{0,2},{1,3},{2,0},{3,1},{4,6},{5,7},{6,4},{7,5},{8,10},{9,11},{10,... | collective-permute-start | bytes 479240 | tf_op jit(solution)/shard_map/ppermute | solution.py:50
  44.1 13.9 %collective-permute-start.8 = (bf16[4,96,768]{2,1,0:T(8,128)(2,1)S(1)}, bf16[4,96,768]{2,1,0:T(8,128)(2,1)}, u32[]{:S(2)}, u32[]{:S(2)}) collective-permute-start(bf16[4,96,768]{2,1,0:T(8,128)(2,1)S(1)} %pad_maximum_fusion.5), channel_id=1, source_target_pairs={{0,1},{1,0},{2,3},{3,2},{4,5},{5,4},{6,7},{7,6},{8,9},{9,8},{10,11... | collective-permute-start | bytes 1769480 | tf_op jit(solution)/shard_map/ppermute | solution.py:50
  44.5 15.8 %collective-permute-start.7 = (bf16[4,96,768]{2,1,0:T(8,128)(2,1)S(1)}, bf16[4,96,768]{2,1,0:T(8,128)(2,1)}, u32[]{:S(2)}, u32[]{:S(2)}) collective-permute-start(bf16[4,96,768]{2,1,0:T(8,128)(2,1)S(1)} %pad_maximum_fusion.4), channel_id=1, source_target_pairs={{0,16},{1,17},{2,18},{3,19},{4,20},{5,21},{6,22},{7,23},{8,24},{9,... | collective-permute-start | bytes 1769480 | tf_op jit(solution)/shard_map/ppermute | solution.py:50
  46.0 16.4 %collective-permute-start.6 = (bf16[4,104,768]{2,1,0:T(8,128)(2,1)S(1)}, bf16[4,104,768]{2,1,0:T(8,128)(2,1)}, u32[]{:S(2)}, u32[]{:S(2)}) collective-permute-start(bf16[4,104,768]{2,1,0:T(8,128)(2,1)S(1)} %pad_maximum_fusion.3), channel_id=1, source_target_pairs={{0,8},{1,9},{2,10},{3,11},{4,12},{5,13},{6,14},{7,15},{8,0},{9,1},... | collective-permute-start | bytes 1916936 | tf_op jit(solution)/shard_map/ppermute | solution.py:50
  63.7 265.4 %reduce-scatter.5.cloned.1.call-start = ((), (), s32[]{:S(2)}) async-start(), calls=%async_computation.4 | async-start | bytes 5898240 | tf_op jit(solution)/shard_map/reduce_scatter | solution.py:593
  63.8 37.2 %collective-permute-start.9 = (bf16[8,104,768]{2,1,0:T(8,128)(2,1)S(1)}, bf16[8,104,768]{2,1,0:T(8,128)(2,1)}, u32[]{:S(2)}, u32[]{:S(2)}) collective-permute-start(bf16[8,104,768]{2,1,0:T(8,128)(2,1)S(1)} %pad_maximum_fusion.refs_3_.refs_7_.refs_4_.refs_11_), channel_id=1, source_target_pairs={{0,1},{1,0},{2,3},{3,2},{4,5},{5,4},{6,7},{7,6},{8,9},{9,8},{10,11... | collective-permute-start | bytes 3833864 | tf_op jit(solution)/shard_map/ppermute | solution.py:50
  64.1 28.8 %collective-permute-start.10 = (bf16[8,96,768]{2,1,0:T(8,128)(2,1)}, bf16[8,96,768]{2,1,0:T(8,128)(2,1)}, u32[]{:S(2)}, u32[]{:S(2)}) collective-permute-start(bf16[8,96,768]{2,1,0:T(8,128)(2,1)} %pad_maximum_fusion.1.refs_11_.refs_8_), channel_id=1, source_target_pairs={{0,8},{1,9},{2,10},{3,11},{4,12},{5,13},{6,14},{7,15},{8,0},{9,1},... | collective-permute-start | bytes 3538952 | tf_op jit(solution)/shard_map/ppermute | solution.py:50
  64.6 28.5 %collective-permute-start.11 = (bf16[8,96,768]{2,1,0:T(8,128)(2,1)}, bf16[8,96,768]{2,1,0:T(8,128)(2,1)}, u32[]{:S(2)}, u32[]{:S(2)}) collective-permute-start(bf16[8,96,768]{2,1,0:T(8,128)(2,1)} %pad_maximum_fusion.2.refs_15_.refs_12_), channel_id=1, source_target_pairs={{0,16},{1,17},{2,18},{3,19},{4,20},{5,21},{6,22},{7,23},{8,24},{9,... | collective-permute-start | bytes 3538952 | tf_op jit(solution)/shard_map/ppermute | solution.py:50
  66.1 36.6 %collective-permute-start.12 = (bf16[8,104,768]{2,1,0:T(8,128)(2,1)S(1)}, bf16[8,104,768]{2,1,0:T(8,128)(2,1)}, u32[]{:S(2)}, u32[]{:S(2)}) collective-permute-start(bf16[8,104,768]{2,1,0:T(8,128)(2,1)S(1)} %pad_maximum_fusion.refs_3_.refs_7_.refs_4_.refs_11_), channel_id=1, source_target_pairs={{0,4},{1,5},{2,6},{3,7},{4,0},{5,1},{6,2},{7,3},{8,12},{9,13},{10,... | collective-permute-start | bytes 3833864 | tf_op jit(solution)/shard_map/ppermute | solution.py:50
  101.1 50.3 %collective-permute-start.24 = (bf16[8,96,768]{2,1,0:T(8,128)(2,1)}, bf16[8,96,768]{2,1,0:T(8,128)(2,1)}, u32[]{:S(2)}, u32[]{:S(2)}) collective-permute-start(bf16[8,96,768]{2,1,0:T(8,128)(2,1)} %pad_maximum_fusion.1.refs_11_.refs_8_), channel_id=1, source_target_pairs={{0,4},{1,5},{2,6},{3,7},{4,0},{5,1},{6,2},{7,3},{8,12},{9,13},{10,... | collective-permute-start | bytes 3538952 | tf_op jit(solution)/shard_map/ppermute | solution.py:50
  101.7 51.8 %collective-permute-start.26 = (bf16[8,96,768]{2,1,0:T(8,128)(2,1)}, bf16[8,96,768]{2,1,0:T(8,128)(2,1)}, u32[]{:S(2)}, u32[]{:S(2)}) collective-permute-start(bf16[8,96,768]{2,1,0:T(8,128)(2,1)} %pad_maximum_fusion.2.refs_15_.refs_12_), channel_id=1, source_target_pairs={{0,4},{1,5},{2,6},{3,7},{4,0},{5,1},{6,2},{7,3},{8,12},{9,13},{10,... | collective-permute-start | bytes 3538952 | tf_op jit(solution)/shard_map/ppermute | solution.py:50
  109.6 16.7 %collective-permute-start.14 = (bf16[192,576]{1,0:T(8,128)(2,1)S(1)}, bf16[192,576]{1,0:T(8,128)(2,1)S(1)}, u32[]{:S(2)}, u32[]{:S(2)}) collective-permute-start(bf16[192,576]{1,0:T(8,128)(2,1)S(1)} %get-tuple-element.168), channel_id=1, source_target_pairs={{0,1},{1,0},{2,3},{3,2},{4,5},{5,4},{6,7},{7,6},{8,9},{9,8},{10,11... | collective-permute-start | bytes 663560 | tf_op jit(solution)/shard_map/ppermute | solution.py:62
  110.1 16.2 %collective-permute-start.15 = (bf16[192,576]{1,0:T(8,128)(2,1)S(1)}, bf16[192,576]{1,0:T(8,128)(2,1)S(1)}, u32[]{:S(2)}, u32[]{:S(2)}) collective-permute-start(bf16[192,576]{1,0:T(8,128)(2,1)S(1)} %get-tuple-element.169), channel_id=1, source_target_pairs={{0,8},{1,9},{2,10},{3,11},{4,12},{5,13},{6,14},{7,15},{8,0},{9,1},... | collective-permute-start | bytes 663560 | tf_op jit(solution)/shard_map/ppermute | solution.py:62
  111.4 44.3 %collective-permute-start.25 = (bf16[8,96,768]{2,1,0:T(8,128)(2,1)}, bf16[8,96,768]{2,1,0:T(8,128)(2,1)}, u32[]{:S(2)}, u32[]{:S(2)}) collective-permute-start(bf16[8,96,768]{2,1,0:T(8,128)(2,1)} %collective-permute-done.10.refs_12_.refs_9_), channel_id=1, source_target_pairs={{0,4},{1,5},{2,6},{3,7},{4,0},{5,1},{6,2},{7,3},{8,12},{9,13},{10,... | collective-permute-start | bytes 3538952 | tf_op jit(solution)/shard_map/ppermute | solution.py:50
  126.3 29.4 %collective-permute-start.27 = (bf16[8,96,768]{2,1,0:T(8,128)(2,1)}, bf16[8,96,768]{2,1,0:T(8,128)(2,1)}, u32[]{:S(2)}, u32[]{:S(2)}) collective-permute-start(bf16[8,96,768]{2,1,0:T(8,128)(2,1)} %collective-permute-done.11.refs_16_.refs_13_), channel_id=1, source_target_pairs={{0,4},{1,5},{2,6},{3,7},{4,0},{5,1},{6,2},{7,3},{8,12},{9,13},{10,... | collective-permute-start | bytes 3538952 | tf_op jit(solution)/shard_map/ppermute | solution.py:50
  266.2 96.0 %reduce-scatter.7.cloned.1.call-start = ((), (), s32[]{:S(2)}) async-start(), calls=%async_computation.5 | async-start | bytes 1474560 | tf_op jit(solution)/shard_map/reduce_scatter | solution.py:599
  285.1 17.7 %collective-permute-start.47 = (bf16[192,576]{1,0:T(8,128)(2,1)S(1)}, bf16[192,576]{1,0:T(8,128)(2,1)S(1)}, u32[]{:S(2)}, u32[]{:S(2)}) collective-permute-start(bf16[192,576]{1,0:T(8,128)(2,1)S(1)} %pad_maximum_fusion.16), channel_id=1, source_target_pairs={{0,8},{1,9},{2,10},{3,11},{4,12},{5,13},{6,14},{7,15},{8,0},{9,1},... | collective-permute-start | bytes 663560 | tf_op jit(solution)/shard_map/ppermute | solution.py:62
  285.9 16.9 %collective-permute-start.46 = (bf16[192,576]{1,0:T(8,128)(2,1)S(1)}, bf16[192,576]{1,0:T(8,128)(2,1)S(1)}, u32[]{:S(2)}, u32[]{:S(2)}) collective-permute-start(bf16[192,576]{1,0:T(8,128)(2,1)S(1)} %pad_maximum_fusion.15), channel_id=1, source_target_pairs={{0,1},{1,0},{2,3},{3,2},{4,5},{5,4},{6,7},{7,6},{8,9},{9,8},{10,11... | collective-permute-start | bytes 663560 | tf_op jit(solution)/shard_map/ppermute | solution.py:62
  329.1 110.3 %reduce-scatter.9.cloned.1.call-start = ((), (), s32[]{:S(2)}) async-start(), calls=%async_computation.6 | async-start | bytes 5898240 | tf_op jit(solution)/shard_map/reduce_scatter | solution.py:593
  352.9 150.0 %reduce-scatter.11.cloned.1.call-start = ((), (), s32[]{:S(2)}) async-start(), calls=%async_computation.7 | async-start | bytes 1474560 | tf_op jit(solution)/shard_map/reduce_scatter | solution.py:599
  355.0 14.9 %collective-permute-start.59 = (bf16[192,576]{1,0:T(8,128)(2,1)S(1)}, bf16[192,576]{1,0:T(8,128)(2,1)S(1)}, u32[]{:S(2)}, u32[]{:S(2)}) collective-permute-start(bf16[192,576]{1,0:T(8,128)(2,1)S(1)} %copy-done.95), channel_id=1, source_target_pairs={{0,9},{1,8},{2,11},{3,10},{4,13},{5,12},{6,15},{7,14},{8,1},{9,0},... | collective-permute-start | bytes 663560 | tf_op jit(solution)/shard_map/ppermute | solution.py:62
  356.5 23.6 %collective-permute-start.67 = (bf16[4,192,576]{2,1,0:T(8,128)(2,1)}, bf16[4,192,576]{2,1,0:T(8,128)(2,1)}, u32[]{:S(2)}, u32[]{:S(2)}) collective-permute-start(bf16[4,192,576]{2,1,0:T(8,128)(2,1)} %get-tuple-element.266.refs_13_), channel_id=1, source_target_pairs={{0,4},{1,5},{2,6},{3,7},{4,0},{5,1},{6,2},{7,3},{8,12},{9,13},{10,... | collective-permute-start | bytes 2654216 | tf_op jit(solution)/shard_map/ppermute | solution.py:50
  392.3 47.2 %collective-permute-start.69 = (bf16[8,96,896]{2,1,0:T(8,128)(2,1)}, bf16[8,96,896]{2,1,0:T(8,128)(2,1)}, u32[]{:S(2)}, u32[]{:S(2)}) collective-permute-start(bf16[8,96,896]{2,1,0:T(8,128)(2,1)} %get-tuple-element.273), channel_id=1, source_target_pairs={{0,16},{1,17},{2,18},{3,19},{4,20},{5,21},{6,22},{7,23},{8,24},{9,... | collective-permute-start | bytes 4128776 | tf_op jit(solution)/shard_map/ppermute | solution.py:50
  393.9 41.3 %collective-permute-start.70 = (bf16[8,96,768]{2,1,0:T(8,128)(2,1)}, bf16[8,96,768]{2,1,0:T(8,128)(2,1)}, u32[]{:S(2)}, u32[]{:S(2)}) collective-permute-start(bf16[8,96,768]{2,1,0:T(8,128)(2,1)} %get-tuple-element.274), channel_id=1, source_target_pairs={{0,8},{1,9},{2,10},{3,11},{4,12},{5,13},{6,14},{7,15},{8,0},{9,1},... | collective-permute-start | bytes 3538952 | tf_op jit(solution)/shard_map/ppermute | solution.py:50
  394.8 28.6 %collective-permute-start.71 = (bf16[2,192,768]{2,1,0:T(8,128)(2,1)S(1)}, bf16[2,192,768]{2,1,0:T(8,128)(2,1)S(1)}, u32[]{:S(2)}, u32[]{:S(2)}) collective-permute-start(bf16[2,192,768]{2,1,0:T(8,128)(2,1)S(1)} %pad_maximum_fusion.6.refs_0_), channel_id=1, source_target_pairs={{0,2},{1,3},{2,0},{3,1},{4,6},{5,7},{6,4},{7,5},{8,10},{9,11},{10,... | collective-permute-start | bytes 1769480 | tf_op jit(solution)/shard_map/ppermute | solution.py:50
  397.2 49.2 %collective-permute-start.74 = (bf16[2,192,768]{2,1,0:T(8,128)(2,1)S(1)}, bf16[2,192,768]{2,1,0:T(8,128)(2,1)S(1)}, u32[]{:S(2)}, u32[]{:S(2)}) collective-permute-start(bf16[2,192,768]{2,1,0:T(8,128)(2,1)S(1)} %pad_maximum_fusion.6.refs_0_), channel_id=1, source_target_pairs={{0,1},{1,0},{2,3},{3,2},{4,5},{5,4},{6,7},{7,6},{8,9},{9,8},{10,11... | collective-permute-start | bytes 1769480 | tf_op jit(solution)/shard_map/ppermute | solution.py:50
  441.6 36.8 %collective-permute-start.72 = (bf16[4,96,896]{2,1,0:T(8,128)(2,1)}, bf16[4,96,896]{2,1,0:T(8,128)(2,1)}, u32[]{:S(2)}, u32[]{:S(2)}) collective-permute-start(bf16[4,96,896]{2,1,0:T(8,128)(2,1)} %add_convert_fusion), channel_id=1, source_target_pairs={{0,8},{1,9},{2,10},{3,11},{4,12},{5,13},{6,14},{7,15},{8,0},{9,1},... | collective-permute-start | bytes 2064392 | tf_op jit(solution)/shard_map/ppermute | solution.py:50
  444.4 15.0 %collective-permute-start.73 = (bf16[4,96,768]{2,1,0:T(8,128)(2,1)S(1)}, bf16[4,96,768]{2,1,0:T(8,128)(2,1)S(1)}, u32[]{:S(2)}, u32[]{:S(2)}) collective-permute-start(bf16[4,96,768]{2,1,0:T(8,128)(2,1)S(1)} %add_convert_fusion.1), channel_id=1, source_target_pairs={{0,16},{1,17},{2,18},{3,19},{4,20},{5,21},{6,22},{7,23},{8,24},{9,... | collective-permute-start | bytes 1769480 | tf_op jit(solution)/shard_map/ppermute | solution.py:50
  445.0 33.4 %collective-permute-start.75 = (bf16[2,192,768]{2,1,0:T(8,128)(2,1)S(1)}, bf16[2,192,768]{2,1,0:T(8,128)(2,1)S(1)}, u32[]{:S(2)}, u32[]{:S(2)}) collective-permute-start(bf16[2,192,768]{2,1,0:T(8,128)(2,1)S(1)} %collective-permute-done.71.refs_1_), channel_id=1, source_target_pairs={{0,1},{1,0},{2,3},{3,2},{4,5},{5,4},{6,7},{7,6},{8,9},{9,8},{10,11... | collective-permute-start | bytes 1769480 | tf_op jit(solution)/shard_map/ppermute | solution.py:50
  (155 other events, 1290.1 us)
Sparse Core Ops, SparseCore 0:
  63.8 118.5 all-gather.2
  266.3 59.9 reduce-scatter.4
  329.3 32.8 reduce-scatter.6
  364.3 61.2 reduce-scatter.8
  443.2 38.4 reduce-scatter.10

commit v4 on v3

--- a/solution.py
+++ b/solution.py
@@ -13,7 +13,7 @@
 BF = jnp.bfloat16
 F32 = jnp.float32
 LIMIT = 48
-COST = 3.0e8
+COST = 1.0e9
 
 BITS = {"x": 16, "y": 8, "c": 4, "z2": 2, "z1": 1}
 
@@ -798,20 +798,17 @@
     frames = [jnp.stack([encoded, grad.astype(BF)])]
     last = Together(sums_a)
     (frames[0],) = last.wait(frames[0])
+    frames.append(swap(frames[0], "z2", shape))
+    frames += [swap(v, "z1", shape) for v in frames]
     for step in range(4):
-        got = []
         if step == 0:
-            got = [low_sum, swap(frames[0], "z2", shape)]
+            low_sum = sum_line(last.go(low_sum)[0])
         elif step == 1:
-            got = [swap(v, "z1", shape) for v in frames]
-        elif step == 3:
-            got = [low_sum]
-        got = list(last.go(*got))
-        if step == 0:
-            low_sum = sum_line(got.pop(0))
-        elif step == 3:
-            low_sum = got.pop()
-        frames += got
+            frames = last.go(*frames)
+        elif step == 2:
+            last.go()
+        else:
+            (low_sum,) = last.go(low_sum)
     small = total.reshape(LAYERS, 16, 768)
     encoded, grad_features = spread(frames)
     chunk, rest = (r.finish() for r in sums_a)

time: 533 us -> 523 us (0.981)
    reduce_scatter x2, waiting for transfers between devices: 5.66 us -> 0.01 us  [sum_line(): lax.psum_scatter(chunks, 'tensor', scatter_dimension=0, tiled=True)]
    unnamed x221 -> x203, local copies, waits for them, and re-layouts: 40.2 us -> 38.3 us
  transfers between devices with their start and end apart: 85 -> 85, of which waited for: 52 -> 50; matrix products, arithmetic and copies ran while one was open for 6% -> 5% of each run, Pallas kernels for 15% -> 15%
where the time goes in v4:
time: 523 us; the launch traced here: 512 us
  waiting for transfers between devices  249 us (48%)
  Pallas kernels  117 us (22%)
  starting transfers between devices  61.1 us (12%)
  local copies, waits for them, and re-layouts  42.7 us (8%)
  other arithmetic  26.7 us (5%)
  between operations  15.5 us (3%)
    ppermute x56, waiting for transfers between devices, swap(): return lax.ppermute(value, AXES, pairs)  163 us
    pallas_call x16, Pallas kernels, call(): pl.pallas_call(lambda *refs: kernel(*refs[len(ties):]), out_shape=[jax.Sh...  117 us
    ppermute x24, waiting for transfers between devices, swap_group(): return lax.ppermute(value, AXES, pairs)  84.7 us
    unnamed x203, local copies, waits for them, and re-layouts  38.3 us
    ppermute x56, starting transfers between devices, swap(): return lax.ppermute(value, AXES, pairs)  34.5 us
    ppermute x24, starting transfers between devices, swap_group(): return lax.ppermute(value, AXES, pairs)  26.4 us
  transfers between devices with their start and end apart: 85, of which 50 were waited for; matrix products, arithmetic and copies ran while one was open for 5% of the time, Pallas kernels for 15%

profile of v4, /device:TPU:0, one launch (start us, length us, event | category | flops | bytes accessed | tf_op | source)
XLA Modules:
  0.0 512.3 jit_solution(8123456696624797435)
XLA Ops:
  8.6 4.1 collective-permute-start.1
  16.4 10.7 %collective-permute-done.1 = bf16[1,96,768]{2,1,0:T(8,128)(2,1)S(1)} collective-permute-done((bf16[1,96,768]{2,1,0:T(8,128)(2,1)S(1)}, bf16[1,96,768]{2,1,0:T(8,128)(2,1)S(1)}, u32[]{:S(2)}, u32[]{:S(2)}) %collective-permute-start.1) | collective-permute-done | bytes 147488 | tf_op jit(solution)/shard_map/ppermute | solution.py:50
  36.7 4.5 collective-permute-done.5
  47.3 10.8 %collective-permute-done.8 = bf16[4,96,768]{2,1,0:T(8,128)(2,1)} collective-permute-done((bf16[4,96,768]{2,1,0:T(8,128)(2,1)S(1)}, bf16[4,96,768]{2,1,0:T(8,128)(2,1)}, u32[]{:S(2)}, u32[]{:S(2)}) %collective-permute-start.8) | collective-permute-done | bytes 589856 | tf_op jit(solution)/shard_map/ppermute | solution.py:50
  66.1 26.7 %collective-permute-done.10.refs_12_.refs_9_ = bf16[8,96,768]{2,1,0:T(8,128)(2,1)} collective-permute-done((bf16[8,96,768]{2,1,0:T(8,128)(2,1)}, bf16[8,96,768]{2,1,0:T(8,128)(2,1)}, u32[]{:S(2)}, u32[]{:S(2)}) %collective-permute-start.10) | collective-permute-done | bytes 1179680 | tf_op jit(solution)/shard_map/ppermute | solution.py:50
  93.1 7.9 %collective-permute-done.9.refs_4_.refs_8_.refs_5_.refs_12_ = bf16[8,104,768]{2,1,0:T(8,128)(2,1)} collective-permute-done((bf16[8,104,768]{2,1,0:T(8,128)(2,1)S(1)}, bf16[8,104,768]{2,1,0:T(8,128)(2,1)}, u32[]{:S(2)}, u32[]{:S(2)}) %collective-permute-start.9) | collective-permute-done | bytes 1277984 | tf_op jit(solution)/shard_map/ppermute | solution.py:50
  111.3 15.1 %collective-permute-done.14.refs_2_ = bf16[192,576]{1,0:T(8,128)(2,1)S(1)} collective-permute-done((bf16[192,576]{1,0:T(8,128)(2,1)S(1)}, bf16[192,576]{1,0:T(8,128)(2,1)S(1)}, u32[]{:S(2)}, u32[]{:S(2)}) %collective-permute-start.14) | collective-permute-done | bytes 221216 | tf_op jit(solution)/shard_map/ppermute | solution.py:62
  127.2 7.6 %collective-permute-done.16.refs_4_ = bf16[192,576]{1,0:T(8,128)(2,1)S(1)} collective-permute-done((bf16[192,576]{1,0:T(8,128)(2,1)S(1)}, bf16[192,576]{1,0:T(8,128)(2,1)S(1)}, u32[]{:S(2)}, u32[]{:S(2)}) %collective-permute-start.16) | collective-permute-done | bytes 221216 | tf_op jit(solution)/shard_map/ppermute | solution.py:62
  138.6 7.2 %attend.2 = (bf16[192,192]{1,0:T(8,128)(2,1)S(1)}, bf16[192,192]{1,0:T(8,128)(2,1)S(1)}, bf16[192,192]{1,0:T(8,128)(2,1)S(1)}, bf16[192,192]{1,0:T(8,128)(2,1)S(...) custom-call(s32[1]{0:T(128)} %bitcast.refs_0_.refs_1_, ...), custom_call_target="tpu_custom_call" | custom-call | flops 7000000000 | bytes 1000 | tf_op jit(solution)/shard_map/attend/pallas_call | solution.py:246
  153.3 6.6 %collective-permute-done.21.refs_1_ = bf16[192,192]{1,0:T(8,128)(2,1)S(1)} collective-permute-done((bf16[192,192]{1,0:T(8,128)(2,1)S(1)}, bf16[192,192]{1,0:T(8,128)(2,1)S(1)}, u32[]{:S(2)}, u32[]{:S(2)}) %collective-permute-start.21) | collective-permute-done | bytes 73760 | tf_op jit(solution)/shard_map/ppermute | solution.py:62
  159.9 5.3 %collective-permute-done.23.refs_3_ = bf16[192,192]{1,0:T(8,128)(2,1)S(1)} collective-permute-done((bf16[192,192]{1,0:T(8,128)(2,1)S(1)}, bf16[192,192]{1,0:T(8,128)(2,1)S(1)}, u32[]{:S(2)}, u32[]{:S(2)}) %collective-permute-start.23) | collective-permute-done | bytes 73760 | tf_op jit(solution)/shard_map/ppermute | solution.py:62
  167.7 10.2 %mlp.2 = (f32[192,768]{1,0:T(8,128)S(1)}, f32[192,768]{1,0:T(8,128)S(1)}, bf16[4,192,192]{2,1,0:T(8,128)(2,1)S(1)}, bf16[384,192]{1,0:T(8,128)(2,1)S(1)}, bf16[3...) custom-call(bf16[192,192]{1,0:T(8,128)(2,1)S(1)} %copy-done.78, ...), custom_call_target="tpu_custom_call" | custom-call | flops 12000000000 | bytes 1000 | tf_op jit(solution)/shard_map/mlp/pallas_call | solution.py:246
  190.3 5.2 %collective-permute-done.28.refs_2_ = bf16[192,576]{1,0:T(8,128)(2,1)S(1)} collective-permute-done((bf16[192,576]{1,0:T(8,128)(2,1)S(1)}, bf16[192,576]{1,0:T(8,128)(2,1)S(1)}, u32[]{:S(2)}, u32[]{:S(2)}) %collective-permute-start.28) | collective-permute-done | bytes 221216 | tf_op jit(solution)/shard_map/ppermute | solution.py:62
  196.2 4.1 collective-permute-done.30.refs_4_
  201.7 7.8 %attend.3 = (bf16[192,192]{1,0:T(8,128)(2,1)S(1)}, bf16[192,192]{1,0:T(8,128)(2,1)}, bf16[192,192]{1,0:T(8,128)(2,1)S(1)}, bf16[192,192]{1,0:T(8,128)(2,1)S(1)},...) custom-call(s32[1]{0:T(128)} %bitcast.refs_0_.refs_1_, ...), custom_call_target="tpu_custom_call" | custom-call | flops 7000000000 | bytes 1000 | tf_op jit(solution)/shard_map/attend/pallas_call | solution.py:246
  222.6 11.5 %mlp.3 = (f32[192,768]{1,0:T(8,128)S(1)}, f32[192,768]{1,0:T(8,128)S(1)}, bf16[4,192,192]{2,1,0:T(8,128)(2,1)S(1)}, bf16[384,192]{1,0:T(8,128)(2,1)S(1)}, bf16[3...) custom-call(bf16[192,192]{1,0:T(8,128)(2,1)S(1)} %copy-done.54, ...), custom_call_target="tpu_custom_call" | custom-call | flops 12000000000 | bytes 1000 | tf_op jit(solution)/shard_map/mlp/pallas_call | solution.py:246
  236.4 10.1 %mlp_back.2 = (bf16[192,192]{1,0:T(8,128)(2,1)S(1)}, bf16[192,192]{1,0:T(8,128)(2,1)S(1)}, bf16[192,192]{1,0:T(8,128)(2,1)S(1)}, bf16[192,192]{1,0:T(8,128)(2,1)...) custom-call(bf16[192,768]{1,0:T(8,128)(2,1)S(1)} %dynamic-slice_bitc, ...), custom_call_target="tpu_custom_call" | custom-call | flops 11000000512 | bytes 1000 | tf_op jit(solution)/shard_map/mlp_back/pallas_call | solution.py:246
  259.8 5.2 %weigh_both.2.refs_0_ = bf16[16,192,768]{2,1,0:T(8,128)(2,1)} custom-call(bf16[384,192]{1,0:T(8,128)(2,1)S(1)} %get-tuple-element.189.refs_0_, bf16[384,192]{1,0:T(8,128)(2,1)S(1)} %collective-permute-done.41.refs_1_, bf16[384,192]{1,0:T(8,128)(2,1)S(1)} %get-tuple-element.200.refs_2_, bf16[384,192]{1,0:T(8,128)(2,1)S(1)} %collective-permute-done.42.refs_3_, ...), custom_call_target="tpu_custom_call" | custom-call | flops 5000000000 | bytes 1000 | tf_op jit(solution)/shard_map/weigh_both/pallas_call | solution.py:246
  272.2 10.4 %attend_back.2 = (bf16[768,192]{1,0:T(8,128)(2,1)S(1)}, bf16[4,192,384]{2,1,0:T(8,128)(2,1)S(1)}, bf16[4,192,384]{2,1,0:T(8,128)(2,1)S(1)}) custom-call(bf16[16,192,768]{2,1,0:T(8,128)(2,1)} %weigh_both.2.refs_0_, s32[1]{0:T(128)} %bitcast.refs_0_.refs_1_, bf16[192,192]{1,0:T(8,128)(2,1)S(1)} %copy-done.38, bf16[192,192]{1,0:T(8,128)(2,1)S(1)} %copy-done.40, ...), custom_call_target="tpu_custom_call" | custom-call | flops 11000000512 | bytes 1000 | tf_op jit(solution)/shard_map/attend_back/pallas_call | solution.py:246
  288.7 6.0 %collective-permute-done.48.refs_4_ = bf16[192,576]{1,0:T(8,128)(2,1)S(1)} collective-permute-done((bf16[192,576]{1,0:T(8,128)(2,1)S(1)}, bf16[192,576]{1,0:T(8,128)(2,1)S(1)}, u32[]{:S(2)}, u32[]{:S(2)}) %collective-permute-start.48) | collective-permute-done | bytes 221216 | tf_op jit(solution)/shard_map/ppermute | solution.py:62
  294.8 9.9 %collective-permute-done.47.refs_3_ = bf16[192,576]{1,0:T(8,128)(2,1)S(1)} collective-permute-done((bf16[192,576]{1,0:T(8,128)(2,1)S(1)}, bf16[192,576]{1,0:T(8,128)(2,1)S(1)}, u32[]{:S(2)}, u32[]{:S(2)}) %collective-permute-start.47) | collective-permute-done | bytes 221216 | tf_op jit(solution)/shard_map/ppermute | solution.py:62
  304.7 4.5 project_back.2
  309.9 11.4 %mlp_back.3 = (bf16[192,192]{1,0:T(8,128)(2,1)S(1)}, bf16[192,192]{1,0:T(8,128)(2,1)S(1)}, bf16[192,192]{1,0:T(8,128)(2,1)S(1)}, bf16[192,192]{1,0:T(8,128)(2,1)...) custom-call(f32[192,768]{1,0:T(8,128)S(1)} %get-tuple-element.217.re, ...), custom_call_target="tpu_custom_call" | custom-call | flops 11000000512 | bytes 1000 | tf_op jit(solution)/shard_map/mlp_back/pallas_call | solution.py:246
  333.0 10.5 %attend_back.3 = (bf16[768,192]{1,0:T(8,128)(2,1)S(1)}, bf16[4,192,384]{2,1,0:T(8,128)(2,1)S(1)}, bf16[4,192,384]{2,1,0:T(8,128)(2,1)S(1)}) custom-call(s32[1]{0:T(128)} %bitcast.refs_0_.refs_1_, bf16[192,192]{1,0:T(8,128)(2,1)S(1)} %get-tuple-element.224.refs_1_, bf16[192,192]{1,0:T(8,128)(2,1)S(1)} %collective-permute-done.49.refs_2_, ...), custom_call_target="tpu_custom_call" | custom-call | flops 11000000512 | bytes 1000 | tf_op jit(solution)/shard_map/attend_back/pallas_call | solution.py:246
  349.6 6.2 %weigh_both.3.refs_0_ = bf16[16,192,768]{2,1,0:T(8,128)(2,1)} custom-call(bf16[384,192]{1,0:T(8,128)(2,1)S(1)} %copy-done.58, bf16[384,192]{1,0:T(8,128)(2,1)S(1)} %collective-permute-done.53.refs_1_, bf16[384,192]{1,0:T(8,128)(2,1)S(1)} %get-tuple-element.239.refs_2_, bf16[384,192]{1,0:T(8,128)(2,1)S(1)} %collective-permute-done.54.refs_3_, ...), custom_call_target="tpu_custom_call" | custom-call | flops 5000000000 | bytes 1000 | tf_op jit(solution)/shard_map/weigh_both/pallas_call | solution.py:246
  364.9 5.2 %collective-permute-done.58.refs_3_ = bf16[192,576]{1,0:T(8,128)(2,1)S(1)} collective-permute-done((bf16[192,576]{1,0:T(8,128)(2,1)}, bf16[192,576]{1,0:T(8,128)(2,1)S(1)}, u32[]{:S(2)}, u32[]{:S(2)}) %collective-permute-start.58) | collective-permute-done | bytes 221216 | tf_op jit(solution)/shard_map/ppermute | solution.py:62
  382.1 7.1 %weigh_attention.1 = (bf16[8,96,896]{2,1,0:T(8,128)(2,1)}, bf16[4,96,896]{2,1,0:T(8,128)(2,1)S(1)}, bf16[2,96,896]{2,1,0:T(8,128)(2,1)S(1)}, bf16[1,96,896]{2,1,...) custom-call(f32[32,768]{1,0:T(8,128)S(1)} %add.110.refs_0_, ...), custom_call_target="tpu_custom_call" | custom-call | flops 6000000000 | bytes 1000 | tf_op jit(solution)/shard_map/weigh_attention/pallas_call | solution.py:246
  395.1 25.8 %collective-permute-done.73.refs_1_ = bf16[2,192,768]{2,1,0:T(8,128)(2,1)} collective-permute-done((bf16[2,192,768]{2,1,0:T(8,128)(2,1)S(1)}, bf16[2,192,768]{2,1,0:T(8,128)(2,1)}, u32[]{:S(2)}, u32[]{:S(2)}) %collective-permute-start.73) | collective-permute-done | bytes 589856 | tf_op jit(solution)/shard_map/ppermute | solution.py:50
  420.9 12.4 %collective-permute-done.70 = bf16[8,96,768]{2,1,0:T(8,128)(2,1)} collective-permute-done((bf16[8,96,768]{2,1,0:T(8,128)(2,1)}, bf16[8,96,768]{2,1,0:T(8,128)(2,1)}, u32[]{:S(2)}, u32[]{:S(2)}) %collective-permute-start.70) | collective-permute-done | bytes 1179680 | tf_op jit(solution)/shard_map/ppermute | solution.py:50
  440.7 14.3 %collective-permute-done.72 = bf16[4,96,768]{2,1,0:T(8,128)(2,1)S(1)} collective-permute-done((bf16[4,96,768]{2,1,0:T(8,128)(2,1)S(1)}, bf16[4,96,768]{2,1,0:T(8,128)(2,1)S(1)}, u32[]{:S(2)}, u32[]{:S(2)}) %collective-permute-start.72) | collective-permute-done | bytes 589856 | tf_op jit(solution)/shard_map/ppermute | solution.py:50
  459.7 19.0 %collective-permute-done.77 = bf16[2,96,768]{2,1,0:T(8,128)(2,1)S(1)} collective-permute-done((bf16[2,96,768]{2,1,0:T(8,128)(2,1)S(1)}, bf16[2,96,768]{2,1,0:T(8,128)(2,1)S(1)}, u32[]{:S(2)}, u32[]{:S(2)}) %collective-permute-start.77) | collective-permute-done | bytes 294944 | tf_op jit(solution)/shard_map/ppermute | solution.py:50
  489.6 4.3 collective-permute-done.79
  (459 shorter events, 189.0 us)
Async XLA Ops:
  7.2 175.7 %all-gather.3.cloned.1.call-start = ((), (), s32[]{:S(2)}) async-start(), calls=%async_computation.8 | async-start | bytes 14598144 | tf_op jit(solution)/shard_map/all_gather | solution.py:724
  8.6 18.5 %collective-permute-start.1 = (bf16[1,96,768]{2,1,0:T(8,128)(2,1)S(1)}, bf16[1,96,768]{2,1,0:T(8,128)(2,1)S(1)}, u32[]{:S(2)}, u32[]{:S(2)}) collective-permute-start(bf16[1,96,768]{2,1,0:T(8,128)(2,1)S(1)} %get-tuple-element.373), channel_id=1, source_target_pairs={{0,2},{1,3},{2,0},{3,1},{4,6},{5,7},{6,4},{7,5},{8,10},{9,11},{10,... | collective-permute-start | bytes 442376 | tf_op jit(solution)/shard_map/ppermute | solution.py:50
  12.7 17.6 %collective-permute-start.2 = (bf16[1,96,768]{2,1,0:T(8,128)(2,1)S(1)}, bf16[1,96,768]{2,1,0:T(8,128)(2,1)S(1)}, u32[]{:S(2)}, u32[]{:S(2)}) collective-permute-start(bf16[1,96,768]{2,1,0:T(8,128)(2,1)S(1)} %get-tuple-element.361), channel_id=1, source_target_pairs={{0,2},{1,3},{2,0},{3,1},{4,6},{5,7},{6,4},{7,5},{8,10},{9,11},{10,... | collective-permute-start | bytes 442376 | tf_op jit(solution)/shard_map/ppermute | solution.py:50
  13.5 19.4 %collective-permute-start = (bf16[1,104,768]{2,1,0:T(8,128)(2,1)S(1)}, bf16[1,104,768]{2,1,0:T(8,128)(2,1)S(1)}, u32[]{:S(2)}, u32[]{:S(2)}) collective-permute-start(bf16[1,104,768]{2,1,0:T(8,128)(2,1)S(1)} %maximum_bitcast_fusion.3), channel_id=1, source_target_pairs={{0,2},{1,3},{2,0},{3,1},{4,6},{5,7},{6,4},{7,5},{8,10},{9,11},{10,... | collective-permute-start | bytes 479240 | tf_op jit(solution)/shard_map/ppermute | solution.py:50
  44.5 15.7 %collective-permute-start.7 = (bf16[4,96,768]{2,1,0:T(8,128)(2,1)S(1)}, bf16[4,96,768]{2,1,0:T(8,128)(2,1)}, u32[]{:S(2)}, u32[]{:S(2)}) collective-permute-start(bf16[4,96,768]{2,1,0:T(8,128)(2,1)S(1)} %pad_maximum_fusion.4), channel_id=1, source_target_pairs={{0,16},{1,17},{2,18},{3,19},{4,20},{5,21},{6,22},{7,23},{8,24},{9,... | collective-permute-start | bytes 1769480 | tf_op jit(solution)/shard_map/ppermute | solution.py:50
  46.0 16.4 %collective-permute-start.6 = (bf16[4,104,768]{2,1,0:T(8,128)(2,1)S(1)}, bf16[4,104,768]{2,1,0:T(8,128)(2,1)}, u32[]{:S(2)}, u32[]{:S(2)}) collective-permute-start(bf16[4,104,768]{2,1,0:T(8,128)(2,1)S(1)} %pad_maximum_fusion.3), channel_id=1, source_target_pairs={{0,8},{1,9},{2,10},{3,11},{4,12},{5,13},{6,14},{7,15},{8,0},{9,1},... | collective-permute-start | bytes 1916936 | tf_op jit(solution)/shard_map/ppermute | solution.py:50
  63.7 267.1 %reduce-scatter.5.cloned.1.call-start = ((), (), s32[]{:S(2)}) async-start(), calls=%async_computation.4 | async-start | bytes 5898240 | tf_op jit(solution)/shard_map/reduce_scatter | solution.py:593
  63.8 37.2 %collective-permute-start.9 = (bf16[8,104,768]{2,1,0:T(8,128)(2,1)S(1)}, bf16[8,104,768]{2,1,0:T(8,128)(2,1)}, u32[]{:S(2)}, u32[]{:S(2)}) collective-permute-start(bf16[8,104,768]{2,1,0:T(8,128)(2,1)S(1)} %pad_maximum_fusion.refs_3_.refs_7_.refs_4_.refs_11_), channel_id=1, source_target_pairs={{0,1},{1,0},{2,3},{3,2},{4,5},{5,4},{6,7},{7,6},{8,9},{9,8},{10,11... | collective-permute-start | bytes 3833864 | tf_op jit(solution)/shard_map/ppermute | solution.py:50
  64.1 28.8 %collective-permute-start.10 = (bf16[8,96,768]{2,1,0:T(8,128)(2,1)}, bf16[8,96,768]{2,1,0:T(8,128)(2,1)}, u32[]{:S(2)}, u32[]{:S(2)}) collective-permute-start(bf16[8,96,768]{2,1,0:T(8,128)(2,1)} %pad_maximum_fusion.1.refs_11_.refs_8_), channel_id=1, source_target_pairs={{0,8},{1,9},{2,10},{3,11},{4,12},{5,13},{6,14},{7,15},{8,0},{9,1},... | collective-permute-start | bytes 3538952 | tf_op jit(solution)/shard_map/ppermute | solution.py:50
  64.6 28.5 %collective-permute-start.11 = (bf16[8,96,768]{2,1,0:T(8,128)(2,1)}, bf16[8,96,768]{2,1,0:T(8,128)(2,1)}, u32[]{:S(2)}, u32[]{:S(2)}) collective-permute-start(bf16[8,96,768]{2,1,0:T(8,128)(2,1)} %pad_maximum_fusion.2.refs_15_.refs_12_), channel_id=1, source_target_pairs={{0,16},{1,17},{2,18},{3,19},{4,20},{5,21},{6,22},{7,23},{8,24},{9,... | collective-permute-start | bytes 3538952 | tf_op jit(solution)/shard_map/ppermute | solution.py:50
  66.1 36.0 %collective-permute-start.12 = (bf16[8,104,768]{2,1,0:T(8,128)(2,1)S(1)}, bf16[8,104,768]{2,1,0:T(8,128)(2,1)}, u32[]{:S(2)}, u32[]{:S(2)}) collective-permute-start(bf16[8,104,768]{2,1,0:T(8,128)(2,1)S(1)} %pad_maximum_fusion.refs_3_.refs_7_.refs_4_.refs_11_), channel_id=1, source_target_pairs={{0,4},{1,5},{2,6},{3,7},{4,0},{5,1},{6,2},{7,3},{8,12},{9,13},{10,... | collective-permute-start | bytes 3833864 | tf_op jit(solution)/shard_map/ppermute | solution.py:50
  109.7 16.6 %collective-permute-start.14 = (bf16[192,576]{1,0:T(8,128)(2,1)S(1)}, bf16[192,576]{1,0:T(8,128)(2,1)S(1)}, u32[]{:S(2)}, u32[]{:S(2)}) collective-permute-start(bf16[192,576]{1,0:T(8,128)(2,1)S(1)} %get-tuple-element.169), channel_id=1, source_target_pairs={{0,1},{1,0},{2,3},{3,2},{4,5},{5,4},{6,7},{7,6},{8,9},{9,8},{10,11... | collective-permute-start | bytes 663560 | tf_op jit(solution)/shard_map/ppermute | solution.py:62
  110.1 16.5 %collective-permute-start.17 = (bf16[192,384]{1,0:T(8,128)(2,1)S(1)}, bf16[192,384]{1,0:T(8,128)(2,1)S(1)}, u32[]{:S(2)}, u32[]{:S(2)}) collective-permute-start(bf16[192,384]{1,0:T(8,128)(2,1)S(1)} %slice.284), channel_id=1, source_target_pairs={{0,4},{1,5},{2,6},{3,7},{4,0},{5,1},{6,2},{7,3},{8,12},{9,13},{10,... | collective-permute-start | bytes 442376 | tf_op jit(solution)/shard_map/ppermute | solution.py:50
  110.2 39.5 %collective-permute-start.24 = (bf16[8,96,768]{2,1,0:T(8,128)(2,1)S(1)}, bf16[8,96,768]{2,1,0:T(8,128)(2,1)S(1)}, u32[]{:S(2)}, u32[]{:S(2)}) collective-permute-start(bf16[8,96,768]{2,1,0:T(8,128)(2,1)S(1)} %copy-done.4), channel_id=1, source_target_pairs={{0,4},{1,5},{2,6},{3,7},{4,0},{5,1},{6,2},{7,3},{8,12},{9,13},{10,... | collective-permute-start | bytes 3538952 | tf_op jit(solution)/shard_map/ppermute | solution.py:50
  110.7 41.0 %collective-permute-start.26 = (bf16[8,96,768]{2,1,0:T(8,128)(2,1)S(1)}, bf16[8,96,768]{2,1,0:T(8,128)(2,1)S(1)}, u32[]{:S(2)}, u32[]{:S(2)}) collective-permute-start(bf16[8,96,768]{2,1,0:T(8,128)(2,1)S(1)} %copy-done.80), channel_id=1, source_target_pairs={{0,4},{1,5},{2,6},{3,7},{4,0},{5,1},{6,2},{7,3},{8,12},{9,13},{10,... | collective-permute-start | bytes 3538952 | tf_op jit(solution)/shard_map/ppermute | solution.py:50
  110.8 16.0 %collective-permute-start.15 = (bf16[192,576]{1,0:T(8,128)(2,1)S(1)}, bf16[192,576]{1,0:T(8,128)(2,1)S(1)}, u32[]{:S(2)}, u32[]{:S(2)}) collective-permute-start(bf16[192,576]{1,0:T(8,128)(2,1)S(1)} %get-tuple-element.170), channel_id=1, source_target_pairs={{0,8},{1,9},{2,10},{3,11},{4,12},{5,13},{6,14},{7,15},{8,0},{9,1},... | collective-permute-start | bytes 663560 | tf_op jit(solution)/shard_map/ppermute | solution.py:62
  126.7 26.5 %collective-permute-start.25 = (bf16[8,96,768]{2,1,0:T(8,128)(2,1)}, bf16[8,96,768]{2,1,0:T(8,128)(2,1)}, u32[]{:S(2)}, u32[]{:S(2)}) collective-permute-start(bf16[8,96,768]{2,1,0:T(8,128)(2,1)} %collective-permute-done.10.refs_12_.refs_9_), channel_id=1, source_target_pairs={{0,4},{1,5},{2,6},{3,7},{4,0},{5,1},{6,2},{7,3},{8,12},{9,13},{10,... | collective-permute-start | bytes 3538952 | tf_op jit(solution)/shard_map/ppermute | solution.py:50
  134.8 18.5 %collective-permute-start.27 = (bf16[8,96,768]{2,1,0:T(8,128)(2,1)}, bf16[8,96,768]{2,1,0:T(8,128)(2,1)}, u32[]{:S(2)}, u32[]{:S(2)}) collective-permute-start(bf16[8,96,768]{2,1,0:T(8,128)(2,1)} %collective-permute-done.11.refs_16_.refs_13_), channel_id=1, source_target_pairs={{0,4},{1,5},{2,6},{3,7},{4,0},{5,1},{6,2},{7,3},{8,12},{9,13},{10,... | collective-permute-start | bytes 3538952 | tf_op jit(solution)/shard_map/ppermute | solution.py:50
  265.0 94.4 %reduce-scatter.7.cloned.1.call-start = ((), (), s32[]{:S(2)}) async-start(), calls=%async_computation.5 | async-start | bytes 1474560 | tf_op jit(solution)/shard_map/reduce_scatter | solution.py:599
  286.5 18.2 %collective-permute-start.47 = (bf16[192,576]{1,0:T(8,128)(2,1)S(1)}, bf16[192,576]{1,0:T(8,128)(2,1)S(1)}, u32[]{:S(2)}, u32[]{:S(2)}) collective-permute-start(bf16[192,576]{1,0:T(8,128)(2,1)S(1)} %pad_maximum_fusion.16), channel_id=1, source_target_pairs={{0,8},{1,9},{2,10},{3,11},{4,12},{5,13},{6,14},{7,15},{8,0},{9,1},... | collective-permute-start | bytes 663560 | tf_op jit(solution)/shard_map/ppermute | solution.py:62
  287.9 16.8 %collective-permute-start.46 = (bf16[192,576]{1,0:T(8,128)(2,1)S(1)}, bf16[192,576]{1,0:T(8,128)(2,1)S(1)}, u32[]{:S(2)}, u32[]{:S(2)}) collective-permute-start(bf16[192,576]{1,0:T(8,128)(2,1)S(1)} %pad_maximum_fusion.15), channel_id=1, source_target_pairs={{0,1},{1,0},{2,3},{3,2},{4,5},{5,4},{6,7},{7,6},{8,9},{9,8},{10,11... | collective-permute-start | bytes 663560 | tf_op jit(solution)/shard_map/ppermute | solution.py:62
  330.8 104.4 %reduce-scatter.9.cloned.1.call-start = ((), (), s32[]{:S(2)}) async-start(), calls=%async_computation.6 | async-start | bytes 5898240 | tf_op jit(solution)/shard_map/reduce_scatter | solution.py:593
  355.8 132.8 %reduce-scatter.11.cloned.1.call-start = ((), (), s32[]{:S(2)}) async-start(), calls=%async_computation.7 | async-start | bytes 1474560 | tf_op jit(solution)/shard_map/reduce_scatter | solution.py:599
  359.4 21.7 %collective-permute-start.67 = (bf16[4,192,576]{2,1,0:T(8,128)(2,1)}, bf16[4,192,576]{2,1,0:T(8,128)(2,1)}, u32[]{:S(2)}, u32[]{:S(2)}) collective-permute-start(bf16[4,192,576]{2,1,0:T(8,128)(2,1)} %get-tuple-element.267.refs_13_), channel_id=1, source_target_pairs={{0,4},{1,5},{2,6},{3,7},{4,0},{5,1},{6,2},{7,3},{8,12},{9,13},{10,... | collective-permute-start | bytes 2654216 | tf_op jit(solution)/shard_map/ppermute | solution.py:50
  389.8 45.5 %collective-permute-start.69 = (bf16[8,96,896]{2,1,0:T(8,128)(2,1)}, bf16[8,96,896]{2,1,0:T(8,128)(2,1)}, u32[]{:S(2)}, u32[]{:S(2)}) collective-permute-start(bf16[8,96,896]{2,1,0:T(8,128)(2,1)} %get-tuple-element.274), channel_id=1, source_target_pairs={{0,16},{1,17},{2,18},{3,19},{4,20},{5,21},{6,22},{7,23},{8,24},{9,... | collective-permute-start | bytes 4128776 | tf_op jit(solution)/shard_map/ppermute | solution.py:50
  391.0 42.3 %collective-permute-start.70 = (bf16[8,96,768]{2,1,0:T(8,128)(2,1)}, bf16[8,96,768]{2,1,0:T(8,128)(2,1)}, u32[]{:S(2)}, u32[]{:S(2)}) collective-permute-start(bf16[8,96,768]{2,1,0:T(8,128)(2,1)} %get-tuple-element.275), channel_id=1, source_target_pairs={{0,8},{1,9},{2,10},{3,11},{4,12},{5,13},{6,14},{7,15},{8,0},{9,1},... | collective-permute-start | bytes 3538952 | tf_op jit(solution)/shard_map/ppermute | solution.py:50
  392.4 28.5 %collective-permute-start.73 = (bf16[2,192,768]{2,1,0:T(8,128)(2,1)S(1)}, bf16[2,192,768]{2,1,0:T(8,128)(2,1)}, u32[]{:S(2)}, u32[]{:S(2)}) collective-permute-start(bf16[2,192,768]{2,1,0:T(8,128)(2,1)S(1)} %pad_maximum_fusion.6.refs_0_), channel_id=1, source_target_pairs={{0,2},{1,3},{2,0},{3,1},{4,6},{5,7},{6,4},{7,5},{8,10},{9,11},{10,... | collective-permute-start | bytes 1769480 | tf_op jit(solution)/shard_map/ppermute | solution.py:50
  393.6 47.1 %collective-permute-start.74 = (bf16[2,192,768]{2,1,0:T(8,128)(2,1)S(1)}, bf16[2,192,768]{2,1,0:T(8,128)(2,1)}, u32[]{:S(2)}, u32[]{:S(2)}) collective-permute-start(bf16[2,192,768]{2,1,0:T(8,128)(2,1)S(1)} %pad_maximum_fusion.6.refs_0_), channel_id=1, source_target_pairs={{0,1},{1,0},{2,3},{3,2},{4,5},{5,4},{6,7},{7,6},{8,9},{9,8},{10,11... | collective-permute-start | bytes 1769480 | tf_op jit(solution)/shard_map/ppermute | solution.py:50
  420.9 19.8 %collective-permute-start.75 = (bf16[2,192,768]{2,1,0:T(8,128)(2,1)}, bf16[2,192,768]{2,1,0:T(8,128)(2,1)}, u32[]{:S(2)}, u32[]{:S(2)}) collective-permute-start(bf16[2,192,768]{2,1,0:T(8,128)(2,1)} %collective-permute-done.73.refs_1_), channel_id=1, source_target_pairs={{0,1},{1,0},{2,3},{3,2},{4,5},{5,4},{6,7},{7,6},{8,9},{9,8},{10,11... | collective-permute-start | bytes 1769480 | tf_op jit(solution)/shard_map/ppermute | solution.py:50
  437.4 17.7 %collective-permute-start.71 = (bf16[4,96,896]{2,1,0:T(8,128)(2,1)}, bf16[4,96,896]{2,1,0:T(8,128)(2,1)S(1)}, u32[]{:S(2)}, u32[]{:S(2)}) collective-permute-start(bf16[4,96,896]{2,1,0:T(8,128)(2,1)} %add_convert_fusion), channel_id=1, source_target_pairs={{0,8},{1,9},{2,10},{3,11},{4,12},{5,13},{6,14},{7,15},{8,0},{9,1},... | collective-permute-start | bytes 2064392 | tf_op jit(solution)/shard_map/ppermute | solution.py:50
  456.4 22.3 %collective-permute-start.76 = (bf16[2,96,896]{2,1,0:T(8,128)(2,1)S(1)}, bf16[2,96,896]{2,1,0:T(8,128)(2,1)S(1)}, u32[]{:S(2)}, u32[]{:S(2)}) collective-permute-start(bf16[2,96,896]{2,1,0:T(8,128)(2,1)S(1)} %add_convert_fusion.4), channel_id=1, source_target_pairs={{0,1},{1,0},{2,3},{3,2},{4,5},{5,4},{6,7},{7,6},{8,9},{9,8},{10,11... | collective-permute-start | bytes 1032200 | tf_op jit(solution)/shard_map/ppermute | solution.py:50
  459.1 19.6 %collective-permute-start.77 = (bf16[2,96,768]{2,1,0:T(8,128)(2,1)S(1)}, bf16[2,96,768]{2,1,0:T(8,128)(2,1)S(1)}, u32[]{:S(2)}, u32[]{:S(2)}) collective-permute-start(bf16[2,96,768]{2,1,0:T(8,128)(2,1)S(1)} %add_convert_fusion.5), channel_id=1, source_target_pairs={{0,1},{1,0},{2,3},{3,2},{4,5},{5,4},{6,7},{7,6},{8,9},{9,8},{10,11... | collective-permute-start | bytes 884744 | tf_op jit(solution)/shard_map/ppermute | solution.py:50
  (146 other events, 1297.0 us)
Sparse Core Ops, SparseCore 0:
  63.8 119.0 all-gather.2
  265.1 57.2 reduce-scatter.4
  331.0 27.8 reduce-scatter.6
  361.0 61.9 reduce-scatter.8
  439.0 33.8 reduce-scatter.10

commit v5 on v4

--- a/solution.py
+++ b/solution.py
@@ -808,12 +808,12 @@
         elif step == 2:
             last.go()
         else:
-            (low_sum,) = last.go(low_sum)
+            ge, gs = (jnp.stack([low_sum[at : at + 96], high_sum[at : at + 96]]) for at in (0, 96))
+            ge, gs = last.go(ge, gs.transpose(0, 2, 1))
     small = total.reshape(LAYERS, 16, 768)
     encoded, grad_features = spread(frames)
     chunk, rest = (r.finish() for r in sums_a)
     g_a = [jnp.concatenate([chunk[at : at + 48, :768], rest[at : at + 48]], axis=0) for at in (0, 48)]
-    g_e, g_s = ([low_sum[:96], high_sum[:96]], [low_sum[96:], high_sum[96:]])
 
     if dp_size != 2:
         start = (lax.rem(dp, 2) * 4 + seq) * 96
@@ -822,8 +822,10 @@
             whole = lax.dynamic_update_slice_in_dim(jnp.zeros((768, 768), F32), block, start, axis=0)
             return lax.psum_scatter(whole, ("dp", "seq"), scatter_dimension=0, tiled=True)
 
-        g_a, g_e, g_s = ([down(g) for g in gs] for gs in (g_a, g_e, g_s))
-    ga, ge, gs = jnp.stack(g_a), jnp.stack(g_e), jnp.stack(g_s)
+        g_a = [down(g) for g in g_a]
+        ge = jnp.stack([down(g) for g in ge])
+        gs = jnp.stack([down(g) for g in gs.transpose(0, 2, 1)]).transpose(0, 2, 1)
+    ga = jnp.stack(g_a)
     if dp_size == 2:
         turned = chunk[:, 768:864].T.reshape(3, LAYERS, 16, 96)
         grad_vectors = turned[0, :, :6]
@@ -855,7 +857,7 @@
         ga[:, :, 576:].transpose(0, 2, 1),
         ge,
         grad_eb,
-        gs.transpose(0, 2, 1),
+        gs,
     )
 
 

time: 523 us -> 518 us (level)
    unnamed x203 -> x211, local copies, waits for them, and re-layouts: 38.3 us -> 38.3 us
where the time goes in v5:
time: 518 us; the launch traced here: 508 us
  waiting for transfers between devices  245 us (47%)
  Pallas kernels  117 us (23%)
  starting transfers between devices  61.3 us (12%)
  local copies, waits for them, and re-layouts  42.7 us (8%)
  other arithmetic  26.1 us (5%)
  between operations  15.6 us (3%)
    ppermute x56, waiting for transfers between devices, swap(): return lax.ppermute(value, AXES, pairs)  159 us
    pallas_call x16, Pallas kernels, call(): pl.pallas_call(lambda *refs: kernel(*refs[len(ties):]), out_shape=[jax.Sh...  117 us
    ppermute x24, waiting for transfers between devices, swap_group(): return lax.ppermute(value, AXES, pairs)  84.5 us
    unnamed x211, local copies, waits for them, and re-layouts  38.3 us
    ppermute x56, starting transfers between devices, swap(): return lax.ppermute(value, AXES, pairs)  34.7 us
    ppermute x24, starting transfers between devices, swap_group(): return lax.ppermute(value, AXES, pairs)  26.4 us
  transfers between devices with their start and end apart: 85, of which 50 were waited for; matrix products, arithmetic and copies ran while one was open for 5% of the time, Pallas kernels for 15%

profile of v5, /device:TPU:0, one launch (start us, length us, event | category | flops | bytes accessed | tf_op | source)
XLA Modules:
  0.0 507.8 jit_solution(7752519807684324514)
XLA Ops:
  8.6 4.1 collective-permute-start.1
  16.4 10.7 %collective-permute-done.1 = bf16[1,96,768]{2,1,0:T(8,128)(2,1)S(1)} collective-permute-done((bf16[1,96,768]{2,1,0:T(8,128)(2,1)S(1)}, bf16[1,96,768]{2,1,0:T(8,128)(2,1)S(1)}, u32[]{:S(2)}, u32[]{:S(2)}) %collective-permute-start.1) | collective-permute-done | bytes 147488 | tf_op jit(solution)/shard_map/ppermute | solution.py:50
  36.7 4.5 collective-permute-done.5
  47.3 10.8 %collective-permute-done.8 = bf16[4,96,768]{2,1,0:T(8,128)(2,1)} collective-permute-done((bf16[4,96,768]{2,1,0:T(8,128)(2,1)S(1)}, bf16[4,96,768]{2,1,0:T(8,128)(2,1)}, u32[]{:S(2)}, u32[]{:S(2)}) %collective-permute-start.8) | collective-permute-done | bytes 589856 | tf_op jit(solution)/shard_map/ppermute | solution.py:50
  66.1 26.7 %collective-permute-done.10.refs_12_.refs_9_ = bf16[8,96,768]{2,1,0:T(8,128)(2,1)} collective-permute-done((bf16[8,96,768]{2,1,0:T(8,128)(2,1)}, bf16[8,96,768]{2,1,0:T(8,128)(2,1)}, u32[]{:S(2)}, u32[]{:S(2)}) %collective-permute-start.10) | collective-permute-done | bytes 1179680 | tf_op jit(solution)/shard_map/ppermute | solution.py:50
  93.1 7.9 %collective-permute-done.9.refs_4_.refs_8_.refs_5_.refs_12_ = bf16[8,104,768]{2,1,0:T(8,128)(2,1)} collective-permute-done((bf16[8,104,768]{2,1,0:T(8,128)(2,1)S(1)}, bf16[8,104,768]{2,1,0:T(8,128)(2,1)}, u32[]{:S(2)}, u32[]{:S(2)}) %collective-permute-start.9) | collective-permute-done | bytes 1277984 | tf_op jit(solution)/shard_map/ppermute | solution.py:50
  111.3 15.1 %collective-permute-done.14.refs_2_ = bf16[192,576]{1,0:T(8,128)(2,1)S(1)} collective-permute-done((bf16[192,576]{1,0:T(8,128)(2,1)S(1)}, bf16[192,576]{1,0:T(8,128)(2,1)S(1)}, u32[]{:S(2)}, u32[]{:S(2)}) %collective-permute-start.14) | collective-permute-done | bytes 221216 | tf_op jit(solution)/shard_map/ppermute | solution.py:62
  127.2 7.6 %collective-permute-done.16.refs_4_ = bf16[192,576]{1,0:T(8,128)(2,1)S(1)} collective-permute-done((bf16[192,576]{1,0:T(8,128)(2,1)S(1)}, bf16[192,576]{1,0:T(8,128)(2,1)S(1)}, u32[]{:S(2)}, u32[]{:S(2)}) %collective-permute-start.16) | collective-permute-done | bytes 221216 | tf_op jit(solution)/shard_map/ppermute | solution.py:62
  138.6 7.2 %attend.2 = (bf16[192,192]{1,0:T(8,128)(2,1)S(1)}, bf16[192,192]{1,0:T(8,128)(2,1)S(1)}, bf16[192,192]{1,0:T(8,128)(2,1)S(1)}, bf16[192,192]{1,0:T(8,128)(2,1)S(...) custom-call(s32[1]{0:T(128)} %bitcast.refs_0_.refs_1_, ...), custom_call_target="tpu_custom_call" | custom-call | flops 7000000000 | bytes 1000 | tf_op jit(solution)/shard_map/attend/pallas_call | solution.py:246
  153.3 6.6 %collective-permute-done.21.refs_1_ = bf16[192,192]{1,0:T(8,128)(2,1)S(1)} collective-permute-done((bf16[192,192]{1,0:T(8,128)(2,1)S(1)}, bf16[192,192]{1,0:T(8,128)(2,1)S(1)}, u32[]{:S(2)}, u32[]{:S(2)}) %collective-permute-start.21) | collective-permute-done | bytes 73760 | tf_op jit(solution)/shard_map/ppermute | solution.py:62
  159.9 5.3 %collective-permute-done.23.refs_3_ = bf16[192,192]{1,0:T(8,128)(2,1)S(1)} collective-permute-done((bf16[192,192]{1,0:T(8,128)(2,1)S(1)}, bf16[192,192]{1,0:T(8,128)(2,1)S(1)}, u32[]{:S(2)}, u32[]{:S(2)}) %collective-permute-start.23) | collective-permute-done | bytes 73760 | tf_op jit(solution)/shard_map/ppermute | solution.py:62
  167.7 10.2 %mlp.2 = (f32[192,768]{1,0:T(8,128)S(1)}, f32[192,768]{1,0:T(8,128)S(1)}, bf16[4,192,192]{2,1,0:T(8,128)(2,1)S(1)}, bf16[384,192]{1,0:T(8,128)(2,1)S(1)}, bf16[3...) custom-call(bf16[192,192]{1,0:T(8,128)(2,1)S(1)} %copy-done.78, ...), custom_call_target="tpu_custom_call" | custom-call | flops 12000000000 | bytes 1000 | tf_op jit(solution)/shard_map/mlp/pallas_call | solution.py:246
  190.4 5.2 %collective-permute-done.28.refs_2_ = bf16[192,576]{1,0:T(8,128)(2,1)S(1)} collective-permute-done((bf16[192,576]{1,0:T(8,128)(2,1)S(1)}, bf16[192,576]{1,0:T(8,128)(2,1)S(1)}, u32[]{:S(2)}, u32[]{:S(2)}) %collective-permute-start.28) | collective-permute-done | bytes 221216 | tf_op jit(solution)/shard_map/ppermute | solution.py:62
  196.3 4.1 collective-permute-done.30.refs_4_
  201.8 7.8 %attend.3 = (bf16[192,192]{1,0:T(8,128)(2,1)S(1)}, bf16[192,192]{1,0:T(8,128)(2,1)}, bf16[192,192]{1,0:T(8,128)(2,1)S(1)}, bf16[192,192]{1,0:T(8,128)(2,1)S(1)},...) custom-call(s32[1]{0:T(128)} %bitcast.refs_0_.refs_1_, ...), custom_call_target="tpu_custom_call" | custom-call | flops 7000000000 | bytes 1000 | tf_op jit(solution)/shard_map/attend/pallas_call | solution.py:246
  222.6 11.5 %mlp.3 = (f32[192,768]{1,0:T(8,128)S(1)}, f32[192,768]{1,0:T(8,128)S(1)}, bf16[4,192,192]{2,1,0:T(8,128)(2,1)S(1)}, bf16[384,192]{1,0:T(8,128)(2,1)S(1)}, bf16[3...) custom-call(bf16[192,192]{1,0:T(8,128)(2,1)S(1)} %copy-done.54, ...), custom_call_target="tpu_custom_call" | custom-call | flops 12000000000 | bytes 1000 | tf_op jit(solution)/shard_map/mlp/pallas_call | solution.py:246
  236.5 10.1 %mlp_back.2 = (bf16[192,192]{1,0:T(8,128)(2,1)S(1)}, bf16[192,192]{1,0:T(8,128)(2,1)S(1)}, bf16[192,192]{1,0:T(8,128)(2,1)S(1)}, bf16[192,192]{1,0:T(8,128)(2,1)...) custom-call(bf16[192,768]{1,0:T(8,128)(2,1)S(1)} %dynamic-slice_bitc, ...), custom_call_target="tpu_custom_call" | custom-call | flops 11000000512 | bytes 1000 | tf_op jit(solution)/shard_map/mlp_back/pallas_call | solution.py:246
  259.9 5.2 %weigh_both.2.refs_0_ = bf16[16,192,768]{2,1,0:T(8,128)(2,1)} custom-call(bf16[384,192]{1,0:T(8,128)(2,1)S(1)} %get-tuple-element.190.refs_0_, bf16[384,192]{1,0:T(8,128)(2,1)S(1)} %collective-permute-done.41.refs_1_, bf16[384,192]{1,0:T(8,128)(2,1)S(1)} %get-tuple-element.201.refs_2_, bf16[384,192]{1,0:T(8,128)(2,1)S(1)} %collective-permute-done.42.refs_3_, ...), custom_call_target="tpu_custom_call" | custom-call | flops 5000000000 | bytes 1000 | tf_op jit(solution)/shard_map/weigh_both/pallas_call | solution.py:246
  272.3 10.4 %attend_back.2 = (bf16[768,192]{1,0:T(8,128)(2,1)S(1)}, bf16[4,192,384]{2,1,0:T(8,128)(2,1)S(1)}, bf16[4,192,384]{2,1,0:T(8,128)(2,1)S(1)}) custom-call(bf16[16,192,768]{2,1,0:T(8,128)(2,1)} %weigh_both.2.refs_0_, s32[1]{0:T(128)} %bitcast.refs_0_.refs_1_, bf16[192,192]{1,0:T(8,128)(2,1)S(1)} %copy-done.38, bf16[192,192]{1,0:T(8,128)(2,1)S(1)} %copy-done.40, ...), custom_call_target="tpu_custom_call" | custom-call | flops 11000000512 | bytes 1000 | tf_op jit(solution)/shard_map/attend_back/pallas_call | solution.py:246
  288.8 6.0 %collective-permute-done.48.refs_4_ = bf16[192,576]{1,0:T(8,128)(2,1)S(1)} collective-permute-done((bf16[192,576]{1,0:T(8,128)(2,1)S(1)}, bf16[192,576]{1,0:T(8,128)(2,1)S(1)}, u32[]{:S(2)}, u32[]{:S(2)}) %collective-permute-start.48) | collective-permute-done | bytes 221216 | tf_op jit(solution)/shard_map/ppermute | solution.py:62
  294.9 9.9 %collective-permute-done.47.refs_3_ = bf16[192,576]{1,0:T(8,128)(2,1)S(1)} collective-permute-done((bf16[192,576]{1,0:T(8,128)(2,1)S(1)}, bf16[192,576]{1,0:T(8,128)(2,1)S(1)}, u32[]{:S(2)}, u32[]{:S(2)}) %collective-permute-start.47) | collective-permute-done | bytes 221216 | tf_op jit(solution)/shard_map/ppermute | solution.py:62
  304.8 4.5 project_back.2
  310.0 11.4 %mlp_back.3 = (bf16[192,192]{1,0:T(8,128)(2,1)S(1)}, bf16[192,192]{1,0:T(8,128)(2,1)S(1)}, bf16[192,192]{1,0:T(8,128)(2,1)S(1)}, bf16[192,192]{1,0:T(8,128)(2,1)...) custom-call(f32[192,768]{1,0:T(8,128)S(1)} %get-tuple-element.218.re, ...), custom_call_target="tpu_custom_call" | custom-call | flops 11000000512 | bytes 1000 | tf_op jit(solution)/shard_map/mlp_back/pallas_call | solution.py:246
  333.2 10.5 %attend_back.3 = (bf16[768,192]{1,0:T(8,128)(2,1)S(1)}, bf16[4,192,384]{2,1,0:T(8,128)(2,1)S(1)}, bf16[4,192,384]{2,1,0:T(8,128)(2,1)S(1)}) custom-call(s32[1]{0:T(128)} %bitcast.refs_0_.refs_1_, bf16[192,192]{1,0:T(8,128)(2,1)S(1)} %get-tuple-element.225.refs_1_, bf16[192,192]{1,0:T(8,128)(2,1)S(1)} %collective-permute-done.49.refs_2_, ...), custom_call_target="tpu_custom_call" | custom-call | flops 11000000512 | bytes 1000 | tf_op jit(solution)/shard_map/attend_back/pallas_call | solution.py:246
  349.7 6.2 %weigh_both.3.refs_0_ = bf16[16,192,768]{2,1,0:T(8,128)(2,1)} custom-call(bf16[384,192]{1,0:T(8,128)(2,1)S(1)} %copy-done.58, bf16[384,192]{1,0:T(8,128)(2,1)S(1)} %collective-permute-done.53.refs_1_, bf16[384,192]{1,0:T(8,128)(2,1)S(1)} %get-tuple-element.240.refs_2_, bf16[384,192]{1,0:T(8,128)(2,1)S(1)} %collective-permute-done.54.refs_3_, ...), custom_call_target="tpu_custom_call" | custom-call | flops 5000000000 | bytes 1000 | tf_op jit(solution)/shard_map/weigh_both/pallas_call | solution.py:246
  365.1 5.0 collective-permute-done.58.refs_3_
  381.9 7.1 %weigh_attention.1 = (bf16[8,96,896]{2,1,0:T(8,128)(2,1)}, bf16[4,96,896]{2,1,0:T(8,128)(2,1)S(1)}, bf16[2,96,896]{2,1,0:T(8,128)(2,1)S(1)}, bf16[1,96,896]{2,1,...) custom-call(f32[32,768]{1,0:T(8,128)S(1)} %add.110.refs_0_, ...), custom_call_target="tpu_custom_call" | custom-call | flops 6000000000 | bytes 1000 | tf_op jit(solution)/shard_map/weigh_attention/pallas_call | solution.py:246
  395.1 25.8 %collective-permute-done.73.refs_1_ = bf16[2,192,768]{2,1,0:T(8,128)(2,1)} collective-permute-done((bf16[2,192,768]{2,1,0:T(8,128)(2,1)S(1)}, bf16[2,192,768]{2,1,0:T(8,128)(2,1)}, u32[]{:S(2)}, u32[]{:S(2)}) %collective-permute-start.73) | collective-permute-done | bytes 589856 | tf_op jit(solution)/shard_map/ppermute | solution.py:50
  420.9 12.4 %collective-permute-done.70 = bf16[8,96,768]{2,1,0:T(8,128)(2,1)} collective-permute-done((bf16[8,96,768]{2,1,0:T(8,128)(2,1)}, bf16[8,96,768]{2,1,0:T(8,128)(2,1)}, u32[]{:S(2)}, u32[]{:S(2)}) %collective-permute-start.70) | collective-permute-done | bytes 1179680 | tf_op jit(solution)/shard_map/ppermute | solution.py:50
  440.8 14.3 %collective-permute-done.72 = bf16[4,96,768]{2,1,0:T(8,128)(2,1)S(1)} collective-permute-done((bf16[4,96,768]{2,1,0:T(8,128)(2,1)S(1)}, bf16[4,96,768]{2,1,0:T(8,128)(2,1)S(1)}, u32[]{:S(2)}, u32[]{:S(2)}) %collective-permute-start.72) | collective-permute-done | bytes 589856 | tf_op jit(solution)/shard_map/ppermute | solution.py:50
  463.3 12.8 %collective-permute-done.77 = bf16[2,96,768]{2,1,0:T(8,128)(2,1)S(1)} collective-permute-done((bf16[2,96,768]{2,1,0:T(8,128)(2,1)S(1)}, bf16[2,96,768]{2,1,0:T(8,128)(2,1)S(1)}, u32[]{:S(2)}, u32[]{:S(2)}) %collective-permute-start.77) | collective-permute-done | bytes 294944 | tf_op jit(solution)/shard_map/ppermute | solution.py:50
  484.9 6.4 %collective-permute-done.79 = bf16[1,96,768]{2,1,0:T(8,128)(2,1)} collective-permute-done((bf16[1,96,768]{2,1,0:T(8,128)(2,1)}, bf16[1,96,768]{2,1,0:T(8,128)(2,1)}, u32[]{:S(2)}, u32[]{:S(2)}) %collective-permute-start.79) | collective-permute-done | bytes 147488 | tf_op jit(solution)/shard_map/ppermute | solution.py:50
  (467 shorter events, 188.9 us)
Async XLA Ops:
  7.2 175.8 %all-gather.3.cloned.1.call-start = ((), (), s32[]{:S(2)}) async-start(), calls=%async_computation.8 | async-start | bytes 14598144 | tf_op jit(solution)/shard_map/all_gather | solution.py:724
  8.6 18.5 %collective-permute-start.1 = (bf16[1,96,768]{2,1,0:T(8,128)(2,1)S(1)}, bf16[1,96,768]{2,1,0:T(8,128)(2,1)S(1)}, u32[]{:S(2)}, u32[]{:S(2)}) collective-permute-start(bf16[1,96,768]{2,1,0:T(8,128)(2,1)S(1)} %get-tuple-element.375), channel_id=1, source_target_pairs={{0,2},{1,3},{2,0},{3,1},{4,6},{5,7},{6,4},{7,5},{8,10},{9,11},{10,... | collective-permute-start | bytes 442376 | tf_op jit(solution)/shard_map/ppermute | solution.py:50
  12.7 17.6 %collective-permute-start.2 = (bf16[1,96,768]{2,1,0:T(8,128)(2,1)S(1)}, bf16[1,96,768]{2,1,0:T(8,128)(2,1)S(1)}, u32[]{:S(2)}, u32[]{:S(2)}) collective-permute-start(bf16[1,96,768]{2,1,0:T(8,128)(2,1)S(1)} %get-tuple-element.363), channel_id=1, source_target_pairs={{0,2},{1,3},{2,0},{3,1},{4,6},{5,7},{6,4},{7,5},{8,10},{9,11},{10,... | collective-permute-start | bytes 442376 | tf_op jit(solution)/shard_map/ppermute | solution.py:50
  13.5 19.4 %collective-permute-start = (bf16[1,104,768]{2,1,0:T(8,128)(2,1)S(1)}, bf16[1,104,768]{2,1,0:T(8,128)(2,1)S(1)}, u32[]{:S(2)}, u32[]{:S(2)}) collective-permute-start(bf16[1,104,768]{2,1,0:T(8,128)(2,1)S(1)} %maximum_bitcast_fusion.3), channel_id=1, source_target_pairs={{0,2},{1,3},{2,0},{3,1},{4,6},{5,7},{6,4},{7,5},{8,10},{9,11},{10,... | collective-permute-start | bytes 479240 | tf_op jit(solution)/shard_map/ppermute | solution.py:50
  44.5 15.8 %collective-permute-start.7 = (bf16[4,96,768]{2,1,0:T(8,128)(2,1)S(1)}, bf16[4,96,768]{2,1,0:T(8,128)(2,1)}, u32[]{:S(2)}, u32[]{:S(2)}) collective-permute-start(bf16[4,96,768]{2,1,0:T(8,128)(2,1)S(1)} %pad_maximum_fusion.4), channel_id=1, source_target_pairs={{0,16},{1,17},{2,18},{3,19},{4,20},{5,21},{6,22},{7,23},{8,24},{9,... | collective-permute-start | bytes 1769480 | tf_op jit(solution)/shard_map/ppermute | solution.py:50
  46.0 16.5 %collective-permute-start.6 = (bf16[4,104,768]{2,1,0:T(8,128)(2,1)S(1)}, bf16[4,104,768]{2,1,0:T(8,128)(2,1)}, u32[]{:S(2)}, u32[]{:S(2)}) collective-permute-start(bf16[4,104,768]{2,1,0:T(8,128)(2,1)S(1)} %pad_maximum_fusion.3), channel_id=1, source_target_pairs={{0,8},{1,9},{2,10},{3,11},{4,12},{5,13},{6,14},{7,15},{8,0},{9,1},... | collective-permute-start | bytes 1916936 | tf_op jit(solution)/shard_map/ppermute | solution.py:50
  63.7 267.3 %reduce-scatter.5.cloned.1.call-start = ((), (), s32[]{:S(2)}) async-start(), calls=%async_computation.4 | async-start | bytes 5898240 | tf_op jit(solution)/shard_map/reduce_scatter | solution.py:593
  63.8 37.2 %collective-permute-start.9 = (bf16[8,104,768]{2,1,0:T(8,128)(2,1)S(1)}, bf16[8,104,768]{2,1,0:T(8,128)(2,1)}, u32[]{:S(2)}, u32[]{:S(2)}) collective-permute-start(bf16[8,104,768]{2,1,0:T(8,128)(2,1)S(1)} %pad_maximum_fusion.refs_3_.refs_7_.refs_4_.refs_11_), channel_id=1, source_target_pairs={{0,1},{1,0},{2,3},{3,2},{4,5},{5,4},{6,7},{7,6},{8,9},{9,8},{10,11... | collective-permute-start | bytes 3833864 | tf_op jit(solution)/shard_map/ppermute | solution.py:50
  64.1 28.8 %collective-permute-start.10 = (bf16[8,96,768]{2,1,0:T(8,128)(2,1)}, bf16[8,96,768]{2,1,0:T(8,128)(2,1)}, u32[]{:S(2)}, u32[]{:S(2)}) collective-permute-start(bf16[8,96,768]{2,1,0:T(8,128)(2,1)} %pad_maximum_fusion.1.refs_11_.refs_8_), channel_id=1, source_target_pairs={{0,8},{1,9},{2,10},{3,11},{4,12},{5,13},{6,14},{7,15},{8,0},{9,1},... | collective-permute-start | bytes 3538952 | tf_op jit(solution)/shard_map/ppermute | solution.py:50
  64.6 28.5 %collective-permute-start.11 = (bf16[8,96,768]{2,1,0:T(8,128)(2,1)}, bf16[8,96,768]{2,1,0:T(8,128)(2,1)}, u32[]{:S(2)}, u32[]{:S(2)}) collective-permute-start(bf16[8,96,768]{2,1,0:T(8,128)(2,1)} %pad_maximum_fusion.2.refs_15_.refs_12_), channel_id=1, source_target_pairs={{0,16},{1,17},{2,18},{3,19},{4,20},{5,21},{6,22},{7,23},{8,24},{9,... | collective-permute-start | bytes 3538952 | tf_op jit(solution)/shard_map/ppermute | solution.py:50
  66.1 36.0 %collective-permute-start.12 = (bf16[8,104,768]{2,1,0:T(8,128)(2,1)S(1)}, bf16[8,104,768]{2,1,0:T(8,128)(2,1)}, u32[]{:S(2)}, u32[]{:S(2)}) collective-permute-start(bf16[8,104,768]{2,1,0:T(8,128)(2,1)S(1)} %pad_maximum_fusion.refs_3_.refs_7_.refs_4_.refs_11_), channel_id=1, source_target_pairs={{0,4},{1,5},{2,6},{3,7},{4,0},{5,1},{6,2},{7,3},{8,12},{9,13},{10,... | collective-permute-start | bytes 3833864 | tf_op jit(solution)/shard_map/ppermute | solution.py:50
  109.8 16.6 %collective-permute-start.14 = (bf16[192,576]{1,0:T(8,128)(2,1)S(1)}, bf16[192,576]{1,0:T(8,128)(2,1)S(1)}, u32[]{:S(2)}, u32[]{:S(2)}) collective-permute-start(bf16[192,576]{1,0:T(8,128)(2,1)S(1)} %get-tuple-element.170), channel_id=1, source_target_pairs={{0,1},{1,0},{2,3},{3,2},{4,5},{5,4},{6,7},{7,6},{8,9},{9,8},{10,11... | collective-permute-start | bytes 663560 | tf_op jit(solution)/shard_map/ppermute | solution.py:62
  110.1 16.5 %collective-permute-start.17 = (bf16[192,384]{1,0:T(8,128)(2,1)S(1)}, bf16[192,384]{1,0:T(8,128)(2,1)S(1)}, u32[]{:S(2)}, u32[]{:S(2)}) collective-permute-start(bf16[192,384]{1,0:T(8,128)(2,1)S(1)} %slice.284), channel_id=1, source_target_pairs={{0,4},{1,5},{2,6},{3,7},{4,0},{5,1},{6,2},{7,3},{8,12},{9,13},{10,... | collective-permute-start | bytes 442376 | tf_op jit(solution)/shard_map/ppermute | solution.py:50
  110.2 39.6 %collective-permute-start.24 = (bf16[8,96,768]{2,1,0:T(8,128)(2,1)S(1)}, bf16[8,96,768]{2,1,0:T(8,128)(2,1)S(1)}, u32[]{:S(2)}, u32[]{:S(2)}) collective-permute-start(bf16[8,96,768]{2,1,0:T(8,128)(2,1)S(1)} %copy-done.4), channel_id=1, source_target_pairs={{0,4},{1,5},{2,6},{3,7},{4,0},{5,1},{6,2},{7,3},{8,12},{9,13},{10,... | collective-permute-start | bytes 3538952 | tf_op jit(solution)/shard_map/ppermute | solution.py:50
  110.7 41.0 %collective-permute-start.26 = (bf16[8,96,768]{2,1,0:T(8,128)(2,1)S(1)}, bf16[8,96,768]{2,1,0:T(8,128)(2,1)S(1)}, u32[]{:S(2)}, u32[]{:S(2)}) collective-permute-start(bf16[8,96,768]{2,1,0:T(8,128)(2,1)S(1)} %copy-done.80), channel_id=1, source_target_pairs={{0,4},{1,5},{2,6},{3,7},{4,0},{5,1},{6,2},{7,3},{8,12},{9,13},{10,... | collective-permute-start | bytes 3538952 | tf_op jit(solution)/shard_map/ppermute | solution.py:50
  110.8 16.0 %collective-permute-start.15 = (bf16[192,576]{1,0:T(8,128)(2,1)S(1)}, bf16[192,576]{1,0:T(8,128)(2,1)S(1)}, u32[]{:S(2)}, u32[]{:S(2)}) collective-permute-start(bf16[192,576]{1,0:T(8,128)(2,1)S(1)} %get-tuple-element.171), channel_id=1, source_target_pairs={{0,8},{1,9},{2,10},{3,11},{4,12},{5,13},{6,14},{7,15},{8,0},{9,1},... | collective-permute-start | bytes 663560 | tf_op jit(solution)/shard_map/ppermute | solution.py:62
  126.8 26.5 %collective-permute-start.25 = (bf16[8,96,768]{2,1,0:T(8,128)(2,1)}, bf16[8,96,768]{2,1,0:T(8,128)(2,1)}, u32[]{:S(2)}, u32[]{:S(2)}) collective-permute-start(bf16[8,96,768]{2,1,0:T(8,128)(2,1)} %collective-permute-done.10.refs_12_.refs_9_), channel_id=1, source_target_pairs={{0,4},{1,5},{2,6},{3,7},{4,0},{5,1},{6,2},{7,3},{8,12},{9,13},{10,... | collective-permute-start | bytes 3538952 | tf_op jit(solution)/shard_map/ppermute | solution.py:50
  134.8 18.5 %collective-permute-start.27 = (bf16[8,96,768]{2,1,0:T(8,128)(2,1)}, bf16[8,96,768]{2,1,0:T(8,128)(2,1)}, u32[]{:S(2)}, u32[]{:S(2)}) collective-permute-start(bf16[8,96,768]{2,1,0:T(8,128)(2,1)} %collective-permute-done.11.refs_16_.refs_13_), channel_id=1, source_target_pairs={{0,4},{1,5},{2,6},{3,7},{4,0},{5,1},{6,2},{7,3},{8,12},{9,13},{10,... | collective-permute-start | bytes 3538952 | tf_op jit(solution)/shard_map/ppermute | solution.py:50
  265.1 94.5 %reduce-scatter.7.cloned.1.call-start = ((), (), s32[]{:S(2)}) async-start(), calls=%async_computation.5 | async-start | bytes 1474560 | tf_op jit(solution)/shard_map/reduce_scatter | solution.py:599
  286.5 18.3 %collective-permute-start.47 = (bf16[192,576]{1,0:T(8,128)(2,1)S(1)}, bf16[192,576]{1,0:T(8,128)(2,1)S(1)}, u32[]{:S(2)}, u32[]{:S(2)}) collective-permute-start(bf16[192,576]{1,0:T(8,128)(2,1)S(1)} %pad_maximum_fusion.16), channel_id=1, source_target_pairs={{0,8},{1,9},{2,10},{3,11},{4,12},{5,13},{6,14},{7,15},{8,0},{9,1},... | collective-permute-start | bytes 663560 | tf_op jit(solution)/shard_map/ppermute | solution.py:62
  288.1 16.8 %collective-permute-start.46 = (bf16[192,576]{1,0:T(8,128)(2,1)S(1)}, bf16[192,576]{1,0:T(8,128)(2,1)S(1)}, u32[]{:S(2)}, u32[]{:S(2)}) collective-permute-start(bf16[192,576]{1,0:T(8,128)(2,1)S(1)} %pad_maximum_fusion.15), channel_id=1, source_target_pairs={{0,1},{1,0},{2,3},{3,2},{4,5},{5,4},{6,7},{7,6},{8,9},{9,8},{10,11... | collective-permute-start | bytes 663560 | tf_op jit(solution)/shard_map/ppermute | solution.py:62
  331.0 104.3 %reduce-scatter.9.cloned.1.call-start = ((), (), s32[]{:S(2)}) async-start(), calls=%async_computation.6 | async-start | bytes 5898240 | tf_op jit(solution)/shard_map/reduce_scatter | solution.py:593
  356.0 126.1 %reduce-scatter.11.cloned.1.call-start = ((), (), s32[]{:S(2)}) async-start(), calls=%async_computation.7 | async-start | bytes 1474560 | tf_op jit(solution)/shard_map/reduce_scatter | solution.py:599
  359.6 21.4 %collective-permute-start.67 = (bf16[4,192,576]{2,1,0:T(8,128)(2,1)}, bf16[4,192,576]{2,1,0:T(8,128)(2,1)}, u32[]{:S(2)}, u32[]{:S(2)}) collective-permute-start(bf16[4,192,576]{2,1,0:T(8,128)(2,1)} %get-tuple-element.268.refs_13_), channel_id=1, source_target_pairs={{0,4},{1,5},{2,6},{3,7},{4,0},{5,1},{6,2},{7,3},{8,12},{9,13},{10,... | collective-permute-start | bytes 2654216 | tf_op jit(solution)/shard_map/ppermute | solution.py:50
  389.7 45.6 %collective-permute-start.69 = (bf16[8,96,896]{2,1,0:T(8,128)(2,1)}, bf16[8,96,896]{2,1,0:T(8,128)(2,1)}, u32[]{:S(2)}, u32[]{:S(2)}) collective-permute-start(bf16[8,96,896]{2,1,0:T(8,128)(2,1)} %get-tuple-element.275), channel_id=1, source_target_pairs={{0,16},{1,17},{2,18},{3,19},{4,20},{5,21},{6,22},{7,23},{8,24},{9,... | collective-permute-start | bytes 4128776 | tf_op jit(solution)/shard_map/ppermute | solution.py:50
  391.1 42.3 %collective-permute-start.70 = (bf16[8,96,768]{2,1,0:T(8,128)(2,1)}, bf16[8,96,768]{2,1,0:T(8,128)(2,1)}, u32[]{:S(2)}, u32[]{:S(2)}) collective-permute-start(bf16[8,96,768]{2,1,0:T(8,128)(2,1)} %get-tuple-element.276), channel_id=1, source_target_pairs={{0,8},{1,9},{2,10},{3,11},{4,12},{5,13},{6,14},{7,15},{8,0},{9,1},... | collective-permute-start | bytes 3538952 | tf_op jit(solution)/shard_map/ppermute | solution.py:50
  392.4 28.6 %collective-permute-start.73 = (bf16[2,192,768]{2,1,0:T(8,128)(2,1)S(1)}, bf16[2,192,768]{2,1,0:T(8,128)(2,1)}, u32[]{:S(2)}, u32[]{:S(2)}) collective-permute-start(bf16[2,192,768]{2,1,0:T(8,128)(2,1)S(1)} %pad_maximum_fusion.6.refs_0_), channel_id=1, source_target_pairs={{0,2},{1,3},{2,0},{3,1},{4,6},{5,7},{6,4},{7,5},{8,10},{9,11},{10,... | collective-permute-start | bytes 1769480 | tf_op jit(solution)/shard_map/ppermute | solution.py:50
  393.6 47.1 %collective-permute-start.74 = (bf16[2,192,768]{2,1,0:T(8,128)(2,1)S(1)}, bf16[2,192,768]{2,1,0:T(8,128)(2,1)}, u32[]{:S(2)}, u32[]{:S(2)}) collective-permute-start(bf16[2,192,768]{2,1,0:T(8,128)(2,1)S(1)} %pad_maximum_fusion.6.refs_0_), channel_id=1, source_target_pairs={{0,1},{1,0},{2,3},{3,2},{4,5},{5,4},{6,7},{7,6},{8,9},{9,8},{10,11... | collective-permute-start | bytes 1769480 | tf_op jit(solution)/shard_map/ppermute | solution.py:50
  420.9 19.8 %collective-permute-start.75 = (bf16[2,192,768]{2,1,0:T(8,128)(2,1)}, bf16[2,192,768]{2,1,0:T(8,128)(2,1)}, u32[]{:S(2)}, u32[]{:S(2)}) collective-permute-start(bf16[2,192,768]{2,1,0:T(8,128)(2,1)} %collective-permute-done.73.refs_1_), channel_id=1, source_target_pairs={{0,1},{1,0},{2,3},{3,2},{4,5},{5,4},{6,7},{7,6},{8,9},{9,8},{10,11... | collective-permute-start | bytes 1769480 | tf_op jit(solution)/shard_map/ppermute | solution.py:50
  437.4 17.6 %collective-permute-start.71 = (bf16[4,96,896]{2,1,0:T(8,128)(2,1)}, bf16[4,96,896]{2,1,0:T(8,128)(2,1)}, u32[]{:S(2)}, u32[]{:S(2)}) collective-permute-start(bf16[4,96,896]{2,1,0:T(8,128)(2,1)} %add_convert_fusion), channel_id=1, source_target_pairs={{0,8},{1,9},{2,10},{3,11},{4,12},{5,13},{6,14},{7,15},{8,0},{9,1},... | collective-permute-start | bytes 2064392 | tf_op jit(solution)/shard_map/ppermute | solution.py:50
  456.5 19.6 %collective-permute-start.76 = (bf16[2,96,896]{2,1,0:T(8,128)(2,1)S(1)}, bf16[2,96,896]{2,1,0:T(8,128)(2,1)S(1)}, u32[]{:S(2)}, u32[]{:S(2)}) collective-permute-start(bf16[2,96,896]{2,1,0:T(8,128)(2,1)S(1)} %add_convert_fusion.4), channel_id=1, source_target_pairs={{0,1},{1,0},{2,3},{3,2},{4,5},{5,4},{6,7},{7,6},{8,9},{9,8},{10,11... | collective-permute-start | bytes 1032200 | tf_op jit(solution)/shard_map/ppermute | solution.py:50
  459.2 17.0 %collective-permute-start.77 = (bf16[2,96,768]{2,1,0:T(8,128)(2,1)S(1)}, bf16[2,96,768]{2,1,0:T(8,128)(2,1)S(1)}, u32[]{:S(2)}, u32[]{:S(2)}) collective-permute-start(bf16[2,96,768]{2,1,0:T(8,128)(2,1)S(1)} %add_convert_fusion.5), channel_id=1, source_target_pairs={{0,1},{1,0},{2,3},{3,2},{4,5},{5,4},{6,7},{7,6},{8,9},{9,8},{10,11... | collective-permute-start | bytes 884744 | tf_op jit(solution)/shard_map/ppermute | solution.py:50
  (150 other events, 1315.0 us)
Sparse Core Ops, SparseCore 0:
  63.8 119.0 all-gather.2
  265.2 57.1 reduce-scatter.4
  331.1 27.7 reduce-scatter.6
  361.1 61.9 reduce-scatter.8
  435.5 32.1 reduce-scatter.10
